TPU v7x, 32 devices: a whole 2x2x4 slice. The times are simulated.
32 devices in a mesh: tile: 8 (over z, y), freq: 4 (over x, core).
Axes of the slice: x: 2, y: 2, z: 4, core: 2. Of those that a mesh axis runs over, the one named last changes fastest.
Arguments:
- source_field: float32 [2, 8, 192, 1024], P(None, 'freq', 'tile'), may hold values from -6 to 6
- receiver_field: float32 [2, 8, 192, 1024], P(None, 'freq', 'tile'), may hold values from -6 to 6
- slowness: float32 [2, 192, 1024], P(None, 'tile', 'freq'), may hold values from 0.5 to 1
- frequency: float32 [8], P('freq'), may hold values from 0.5 to 2
- order_table: int32 [2, 8], P(None, 'freq'), may hold values from 2 to 4, as said below
- filter_coeffs: float32 [2, 5, 3], replicated, may hold values from -2 to 2
- aperture: int32 [8], replicated, may hold values from 8 to 24, as said below
Outputs:
- image_out: float32 [2, 192, 1024], P(None, 'tile', 'freq')
- receiver_out: float32 [2, 8, 192, 1024], P(None, 'freq', 'tile')
Inputs may be any that keep to these rules, and one draw needn't show every extreme that they name: Tile t holds aperture[t] grid rows; the entries sum to 128, and some tile holds exactly 24. `order_table`: the order 4 occurs in every draw.
All inputs are finite; a program needn't handle non-finite values.
Results may differ from a plain program's by a relative error of at most 0.0003.
Values sent between devices are 32-bit elements; how exact they have to be, the bound alone decides.
No kernel may reach another device: no remote copies, remote signals or barrier semaphores. Data moves between devices by JAX's collectives and lax.ppermute only.
A program may use at most 64 MiB of HBM per device.

v0:
```python
import jax
import jax.numpy as jnp
from jax import lax
from jax.sharding import PartitionSpec as P

ORDER = 4
NDEPTH = 2


def passed_along(value, axis, steps):
    count = lax.axis_size(axis)
    initial, last = (max(0, -steps), min(count, count - steps))
    return lax.ppermute(value, axis, [(source, source + steps) for source in range(initial, last)])


def mcclellan(values):
    lead = [(0, 0)] * (values.ndim - 2)
    padded_x = jnp.pad(values, lead + [(1, 1), (0, 0)])
    blur_rows = 0.25 * (padded_x[..., :-2, :] + padded_x[..., 2:, :]) + 0.5 * values
    padded_cols = jnp.pad(blur_rows, lead + [(0, 0), (1, 1)])
    blur_cols = 0.25 * (padded_cols[..., :-2] + padded_cols[..., 2:]) + 0.5 * blur_rows
    return 2.0 * blur_cols - values


def weighted(term_index, cheb_term, wavenumber, coeffs, active):
    powers = coeffs.shape[2]
    coef_re = coeffs[0, term_index, powers - 1] + 0.0 * wavenumber
    coef_im = coeffs[1, term_index, powers - 1] + 0.0 * wavenumber
    for power_index in range(powers - 2, -1, -1):
        coef_re = coef_re * wavenumber + coeffs[0, term_index, power_index]
        coef_im = coef_im * wavenumber + coeffs[1, term_index, power_index]
    coef_re = coef_re * active
    coef_im = coef_im * active
    src_re = coef_re * cheb_term[0, 0] + coef_im * cheb_term[0, 1]
    src_im = coef_re * cheb_term[0, 1] - coef_im * cheb_term[0, 0]
    rec_re = coef_re * cheb_term[1, 0] - coef_im * cheb_term[1, 1]
    rec_im = coef_re * cheb_term[1, 1] + coef_im * cheb_term[1, 0]
    return jnp.stack([jnp.stack([src_re, src_im]), jnp.stack([rec_re, rec_im])])


def extended(fields, tile_width, halo_rows):
    row_axis = fields.ndim - 2
    upper_rows = lax.dynamic_slice_in_dim(fields, tile_width - halo_rows, halo_rows, row_axis)
    lower_rows = fields[..., :halo_rows, :]
    from_below = passed_along(upper_rows, "tile", 1)
    from_above = passed_along(lower_rows, "tile", -1)
    spare_rows = jnp.zeros(fields.shape[:-2] + (halo_rows, fields.shape[-1]), fields.dtype)
    joined = jnp.concatenate([from_below, fields, spare_rows], axis=row_axis)
    return lax.dynamic_update_slice_in_dim(joined, from_above, halo_rows + tile_width, row_axis)


def shards(source_field, receiver_field, slowness, frequency, order_table, filter_coeffs, aperture):
    tile_index = lax.axis_index("tile")
    row_count = source_field.shape[2]
    tile_width = aperture[tile_index]
    live_rows = (jnp.arange(row_count, dtype=jnp.int32) < tile_width).astype(jnp.float32)[:, None]
    fields = jnp.stack([source_field, receiver_field]) * live_rows
    planes = lax.all_gather(slowness, "freq", axis=2, tiled=True)
    images = []
    for depth_index in range(NDEPTH):
        wavenumber = frequency[:, None, None] * planes[depth_index][None]
        active = (
            jnp.arange(ORDER + 1, dtype=jnp.int32)[:, None] <= order_table[depth_index][None, :]
        ).astype(jnp.float32)
        result = weighted(0, fields, wavenumber, filter_coeffs, active[0][:, None, None])
        previous = fields
        current = live_rows * mcclellan(extended(fields, tile_width, 1))[..., 1 : 1 + row_count, :]
        result = result + weighted(1, current, wavenumber, filter_coeffs, active[1][:, None, None])
        for term_index in range(2, ORDER + 1):
            spread = mcclellan(extended(current, tile_width, 1))[..., 1 : 1 + row_count, :]
            following = live_rows * (2.0 * spread - previous)
            result = result + weighted(
                term_index, following, wavenumber, filter_coeffs, active[term_index][:, None, None]
            )
            previous, current = (current, following)
        fields = result
        images.append(jnp.sum(fields[0, 0] * fields[1, 0] + fields[0, 1] * fields[1, 1], axis=0))
    stacked = jnp.stack(images)
    summed = lax.psum(stacked, "freq")
    column_count = stacked.shape[2] // lax.axis_size("freq")
    image_out = lax.dynamic_slice_in_dim(
        summed, lax.axis_index("freq") * column_count, column_count, 2
    )
    return (image_out, fields[1])


def solution(mesh):
    placed = (
        P(None, "freq", "tile", None),
        P(None, "freq", "tile", None),
        P(None, "tile", "freq"),
        P("freq"),
        P(None, "freq"),
        P(),
        P(),
    )
    return jax.shard_map(
        shards,
        mesh=mesh,
        in_specs=placed,
        out_specs=(P(None, "tile", "freq"), P(None, "freq", "tile", None)),
        check_vma=False,
    )
```

profile of v0, /device:TPU:0, one launch (start us, length us, event | category | flops | bytes accessed | tf_op | source)
XLA Modules:
  0.0 190.8 jit_solution(7751911031121321575)
XLA Ops:
  11.8 4.9 %collective-permute-start = (f32[2,2,2,1,1024]{4,3,2,1,0:T(1,128)S(1)}, f32[2,2,2,1,1024]{4,3,2,1,0:T(1,128)S(1)}, u32[]{:S(2)}, u32[]{:S(2)}) collective-permute-start(f32[2,2,2,1,1024]{4,3,2,1,0:T(1,128)S(1)} %get-tuple-element.73), channel_id=1, source_target_pairs={{0,4},{4,8},{8,12},{12,16},{16,20},{20,24},{24,28},{1,5},{5,9},{9,... | collective-permute-start | bytes 98312 | tf_op jit(solution)/shard_map/ppermute | solution.py:13
  19.3 5.6 %all_gather.3 = f32[2,24,1024]{2,1,0:T(8,128)S(1)} all-gather(f32[2,24,256]{2,1,0:T(8,128)S(1)} %copy-done.34), channel_id=1, replica_groups=mesh['tile'=8,'freq'=4] {'freq'}, dimensions={2}, use_global_device_ids=true | all-gather | bytes 245760 | tf_op jit(solution)/shard_map/all_gather | solution.py:58
  25.5 3.9 %multiply_add_fusion.25 = (f32[1,2,24,1024]{3,2,1,0:T(8,128)S(1)}, f32[1,2,24,1024]{3,2,1,0:T(8,128)S(1)}, f32[1,2,24,1024]{3,2,1,0:T(8,128)S(1)}, f32[1,2,24,1024]{3,2,1,0:T(8,128)S(1)}) fusion(f32[2,2,2,24,1024]{4,3,2,1,0:T(8,128)S(1)} %maximum_multiply_fusion, f32[]{:T(128)} %bitcast.12, f32[]{:T(128)} %bitcast.11, f32[]{:T(128)} %bitcast.10, ...), kind=kLoop, calls=%fused_computation.341 | loop fusion | flops 1277952 | bytes 1671208 | tf_op jit(solution)/shard_map/add | solution.py:34
  33.5 4.5 %collective-permute-start.2 = (f32[2,2,2,1,1024]{4,3,2,1,0:T(1,128)S(1)}, f32[2,2,2,1,1024]{4,3,2,1,0:T(1,128)S(1)}, u32[]{:S(2)}, u32[]{:S(2)}) collective-permute-start(f32[2,2,2,1,1024]{4,3,2,1,0:T(1,128)S(1)} %get-tuple-element.71), channel_id=1, source_target_pairs={{0,4},{4,8},{8,12},{12,16},{16,20},{20,24},{24,28},{1,5},{5,9},{9,... | collective-permute-start | bytes 98312 | tf_op jit(solution)/shard_map/ppermute | solution.py:13
  38.0 1.3 collective-permute-start.3
  39.3 4.1 %multiply_add_fusion.23 = (f32[1,2,24,1024]{3,2,1,0:T(8,128)S(1)}, f32[1,2,24,1024]{3,2,1,0:T(8,128)S(1)}, f32[1,2,24,1024]{3,2,1,0:T(8,128)S(1)}, f32[1,2,24,1024]{3,2,1,0:T(8,128)S(1)}) fusion(f32[2,2,2,24,1024]{4,3,2,1,0:T(8,128)S(1)} %fusion.60, f32[]{:T(128)} %bitcast.25, f32[]{:T(128)} %bitcast.24, f32[]{:T(128)} %bitcast.23, ...), kind=kLoop, calls=%fused_computation.337 | loop fusion | flops 1277952 | bytes 1671208 | tf_op jit(solution)/shard_map/add | solution.py:34
  47.4 5.0 %collective-permute-start.4 = (f32[2,2,2,1,1024]{4,3,2,1,0:T(1,128)S(1)}, f32[2,2,2,1,1024]{4,3,2,1,0:T(1,128)S(1)}, u32[]{:S(2)}, u32[]{:S(2)}) collective-permute-start(f32[2,2,2,1,1024]{4,3,2,1,0:T(1,128)S(1)} %get-tuple-element.69), channel_id=1, source_target_pairs={{0,4},{4,8},{8,12},{12,16},{16,20},{20,24},{24,28},{1,5},{5,9},{9,... | collective-permute-start | bytes 98312 | tf_op jit(solution)/shard_map/ppermute | solution.py:13
  52.4 1.3 collective-permute-start.5
  53.7 4.0 %multiply_add_fusion.21 = (f32[1,2,24,1024]{3,2,1,0:T(8,128)S(1)}, f32[1,2,24,1024]{3,2,1,0:T(8,128)S(1)}, f32[1,2,24,1024]{3,2,1,0:T(8,128)S(1)}, f32[1,2,24,1024]{3,2,1,0:T(8,128)S(1)}) fusion(f32[2,2,2,24,1024]{4,3,2,1,0:T(8,128)S(1)} %fusion.56, f32[]{:T(128)} %bitcast.38, f32[]{:T(128)} %bitcast.37, f32[]{:T(128)} %bitcast.36, ...), kind=kLoop, calls=%fused_computation.333 | loop fusion | flops 1277952 | bytes 1671208 | tf_op jit(solution)/shard_map/add | solution.py:34
  61.3 5.4 %collective-permute-start.6 = (f32[2,2,2,1,1024]{4,3,2,1,0:T(1,128)S(1)}, f32[2,2,2,1,1024]{4,3,2,1,0:T(1,128)S(1)}, u32[]{:S(2)}, u32[]{:S(2)}) collective-permute-start(f32[2,2,2,1,1024]{4,3,2,1,0:T(1,128)S(1)} %get-tuple-element.67), channel_id=1, source_target_pairs={{0,4},{4,8},{8,12},{12,16},{16,20},{20,24},{24,28},{1,5},{5,9},{9,... | collective-permute-start | bytes 98312 | tf_op jit(solution)/shard_map/ppermute | solution.py:13
  66.7 1.3 collective-permute-start.7
  68.0 4.0 %multiply_add_fusion.19 = (f32[1,2,24,1024]{3,2,1,0:T(8,128)S(1)}, f32[1,2,24,1024]{3,2,1,0:T(8,128)S(1)}, f32[1,2,24,1024]{3,2,1,0:T(8,128)S(1)}, f32[1,2,24,1024]{3,2,1,0:T(8,128)S(1)}) fusion(f32[2,2,2,24,1024]{4,3,2,1,0:T(8,128)S(1)} %fusion.50, f32[]{:T(128)} %bitcast.51, f32[]{:T(128)} %bitcast.50, f32[]{:T(128)} %bitcast.49, f32[2]{0:T(128)S(1)} %copy-done.40, ...), kind=kLoop, calls=%fused_computation.329 | loop fusion | flops 1277952 | bytes 1671208 | tf_op jit(solution)/shard_map/add | solution.py:34
  75.4 3.9 %multiply_add_fusion.17 = (f32[1,2,24,1024]{3,2,1,0:T(8,128)S(1)}, f32[1,2,24,1024]{3,2,1,0:T(8,128)S(1)}, f32[1,2,24,1024]{3,2,1,0:T(8,128)S(1)}, f32[1,2,24,1024]{3,2,1,0:T(8,128)S(1)}) fusion(f32[2,2,2,24,1024]{4,3,2,1,0:T(8,128)S(1)} %fusion.44, f32[]{:T(128)} %bitcast.64, f32[]{:T(128)} %bitcast.63, f32[]{:T(128)} %bitcast.62, f32[2]{0:T(128)S(1)} %copy-done.39, ...), kind=kLoop, calls=%fused_computation.325 | loop fusion | flops 1277952 | bytes 1671208 | tf_op jit(solution)/shard_map/add | solution.py:34
  82.3 4.8 %collective-permute-start.8 = (f32[2,2,2,1,1024]{4,3,2,1,0:T(1,128)S(1)}, f32[2,2,2,1,1024]{4,3,2,1,0:T(1,128)S(1)}, u32[]{:S(2)}, u32[]{:S(2)}) collective-permute-start(f32[2,2,2,1,1024]{4,3,2,1,0:T(1,128)S(1)} %get-tuple-element.65), channel_id=1, source_target_pairs={{0,4},{4,8},{8,12},{12,16},{16,20},{20,24},{24,28},{1,5},{5,9},{9,... | collective-permute-start | bytes 98312 | tf_op jit(solution)/shard_map/ppermute | solution.py:13
  88.4 3.9 %fusion.134 = (f32[1,2,24,1024]{3,2,1,0:T(8,128)S(1)}, f32[1,2,24,1024]{3,2,1,0:T(8,128)S(1)}, f32[1,2,24,1024]{3,2,1,0:T(8,128)S(1)}, f32[1,2,24,1024]{3,2,1,0:T(8,128)S(1)}) fusion(f32[2,2,2,24,1024]{4,3,2,1,0:T(8,128)S(1)} %fusion.66, f32[2]{0:T(128)S(1)} %copy-done.38, f32[24,1024]{1,0:T(8,128)S(1)} %get-tuple-element.74, f32[]{:T(128)} %bitcast.12, ...), kind=kLoop, calls=%fused_computation.301 | loop fusion | flops 1277952 | bytes 1671208 | tf_op jit(solution)/shard_map/add | solution.py:34
  95.9 5.0 %collective-permute-start.10 = (f32[2,2,2,1,1024]{4,3,2,1,0:T(1,128)S(1)}, f32[2,2,2,1,1024]{4,3,2,1,0:T(1,128)S(1)}, u32[]{:S(2)}, u32[]{:S(2)}) collective-permute-start(f32[2,2,2,1,1024]{4,3,2,1,0:T(1,128)S(1)} %get-tuple-element.63), channel_id=1, source_target_pairs={{0,4},{4,8},{8,12},{12,16},{16,20},{20,24},{24,28},{1,5},{5,9},{9,... | collective-permute-start | bytes 98312 | tf_op jit(solution)/shard_map/ppermute | solution.py:13
  102.2 4.1 %multiply_add_fusion.15 = (f32[1,2,24,1024]{3,2,1,0:T(8,128)S(1)}, f32[1,2,24,1024]{3,2,1,0:T(8,128)S(1)}, f32[1,2,24,1024]{3,2,1,0:T(8,128)S(1)}, f32[1,2,24,1024]{3,2,1,0:T(8,128)S(1)}) fusion(f32[2,2,2,24,1024]{4,3,2,1,0:T(8,128)S(1)} %fusion.38, f32[2]{0:T(128)S(1)} %copy-done.37, f32[24,1024]{1,0:T(8,128)S(1)} %get-tuple-element.74, f32[]{:T(128)} %bitcast.25, ...), kind=kLoop, calls=%fused_computation.320 | loop fusion | flops 1277952 | bytes 1671208 | tf_op jit(solution)/shard_map/add | solution.py:34
  111.4 5.4 %collective-permute-start.12 = (f32[2,2,2,1,1024]{4,3,2,1,0:T(1,128)S(1)}, f32[2,2,2,1,1024]{4,3,2,1,0:T(1,128)S(1)}, u32[]{:S(2)}, u32[]{:S(2)}) collective-permute-start(f32[2,2,2,1,1024]{4,3,2,1,0:T(1,128)S(1)} %get-tuple-element.61), channel_id=1, source_target_pairs={{0,4},{4,8},{8,12},{12,16},{16,20},{20,24},{24,28},{1,5},{5,9},{9,... | collective-permute-start | bytes 98312 | tf_op jit(solution)/shard_map/ppermute | solution.py:13
  118.2 4.0 %multiply_add_fusion.13 = (f32[1,2,24,1024]{3,2,1,0:T(8,128)S(1)}, f32[1,2,24,1024]{3,2,1,0:T(8,128)S(1)}, f32[1,2,24,1024]{3,2,1,0:T(8,128)S(1)}, f32[1,2,24,1024]{3,2,1,0:T(8,128)S(1)}) fusion(f32[2,2,2,24,1024]{4,3,2,1,0:T(8,128)S(1)} %fusion.34, f32[2]{0:T(128)S(1)} %copy-done.36, f32[24,1024]{1,0:T(8,128)S(1)} %get-tuple-element.74, f32[]{:T(128)} %bitcast.38, ...), kind=kLoop, calls=%fused_computation.316 | loop fusion | flops 1277952 | bytes 1671208 | tf_op jit(solution)/shard_map/add | solution.py:34
  125.7 5.4 %collective-permute-start.14 = (f32[2,2,2,1,1024]{4,3,2,1,0:T(1,128)S(1)}, f32[2,2,2,1,1024]{4,3,2,1,0:T(1,128)S(1)}, u32[]{:S(2)}, u32[]{:S(2)}) collective-permute-start(f32[2,2,2,1,1024]{4,3,2,1,0:T(1,128)S(1)} %get-tuple-element.59), channel_id=1, source_target_pairs={{0,4},{4,8},{8,12},{12,16},{16,20},{20,24},{24,28},{1,5},{5,9},{9,... | collective-permute-start | bytes 98312 | tf_op jit(solution)/shard_map/ppermute | solution.py:13
  132.5 4.0 %multiply_add_fusion.11 = (f32[1,2,24,1024]{3,2,1,0:T(8,128)S(1)}, f32[1,2,24,1024]{3,2,1,0:T(8,128)S(1)}, f32[1,2,24,1024]{3,2,1,0:T(8,128)S(1)}, f32[1,2,24,1024]{3,2,1,0:T(8,128)S(1)}) fusion(f32[2,2,2,24,1024]{4,3,2,1,0:T(8,128)S(1)} %fusion.28, f32[2]{0:T(128)S(1)} %copy-done.35, f32[24,1024]{1,0:T(8,128)S(1)} %get-tuple-element.74, f32[]{:T(128)} %bitcast.51, ...), kind=kLoop, calls=%fused_computation.312 | loop fusion | flops 1277952 | bytes 1671208 | tf_op jit(solution)/shard_map/add | solution.py:34
  140.0 4.0 %multiply_add_fusion.9 = (f32[1,2,24,1024]{3,2,1,0:T(8,128)S(1)}, f32[1,2,24,1024]{3,2,1,0:T(8,128)S(1)}, f32[1,2,24,1024]{3,2,1,0:T(8,128)S(1)}, f32[1,2,24,1024]{3,2,1,0:T(8,128)S(1)}) fusion(f32[2,2,2,24,1024]{4,3,2,1,0:T(8,128)S(1)} %fusion.22, f32[2]{0:T(128)S(1)} %get-tuple-element.76, f32[24,1024]{1,0:T(8,128)S(1)} %get-tuple-element.74, ...), kind=kLoop, calls=%fused_computation.308 | loop fusion | flops 1277952 | bytes 1671208 | tf_op jit(solution)/shard_map/add | solution.py:34
  147.8 34.8 %all-reduce.18.cloned.1.call-done = f32[2,24,1024]{2,1,0:T(8,128)} async-done(((f32[2,24,1024]{2,1,0:T(8,128)}), f32[2,24,1024]{2,1,0:T(8,128)}) %all-reduce.18.cloned.1.call-update) | async-done | bytes 196624 | tf_op jit(solution)/shard_map/psum | solution.py:79
  182.6 1.4 constant_dynamic-slice_fusion
  (192 shorter events, 47.1 us)
Async XLA Ops:
  7.2 10.8 %copy-start.32 = (f32[2,5,3]{1,0,2:T(2,128)S(1)}, f32[2,5,3]{1,0,2:T(2,128)}, u32[]{:S(2)}) copy-start(f32[2,5,3]{1,0,2:T(2,128)} %param.12) | copy-start | bytes 364
  7.2 11.5 %copy-start.41 = (s32[2,2]{1,0:T(2,128)S(1)}, s32[2,2]{1,0:T(2,128)}, u32[]{:S(2)}) copy-start(s32[2,2]{1,0:T(2,128)} %param.11) | copy-start | bytes 52
  7.2 12.1 %copy-start.34 = (f32[2,24,256]{2,1,0:T(8,128)S(1)}, f32[2,24,256]{2,1,0:T(8,128)}, u32[]{:S(2)}) copy-start(f32[2,24,256]{2,1,0:T(8,128)} %param.9) | copy-start | bytes 147460
  7.2 175.4 %all-reduce.18.cloned.1.call-start = ((), (), s32[]{:S(2)}) async-start(), calls=%async_computation | async-start | bytes 393216 | tf_op jit(solution)/shard_map/psum | solution.py:79
  10.4 15.1 %copy-start.33 = (f32[2]{0:T(128)S(1)}, f32[2]{0:T(128)}, u32[]{:S(2)}) copy-start(f32[2]{0:T(128)} %param.10) | copy-start | bytes 28
  11.8 19.8 %collective-permute-start = (f32[2,2,2,1,1024]{4,3,2,1,0:T(1,128)S(1)}, f32[2,2,2,1,1024]{4,3,2,1,0:T(1,128)S(1)}, u32[]{:S(2)}, u32[]{:S(2)}) collective-permute-start(f32[2,2,2,1,1024]{4,3,2,1,0:T(1,128)S(1)} %get-tuple-element.73), channel_id=1, source_target_pairs={{0,4},{4,8},{8,12},{12,16},{16,20},{20,24},{24,28},{1,5},{5,9},{9,... | collective-permute-start | bytes 98312 | tf_op jit(solution)/shard_map/ppermute | solution.py:13
  16.7 15.1 %collective-permute-start.1 = (f32[2,2,2,1,1024]{4,3,2,1,0:T(1,128)S(1)}, f32[2,2,2,1,1024]{4,3,2,1,0:T(1,128)S(1)}, u32[]{:S(2)}, u32[]{:S(2)}) collective-permute-start(f32[2,2,2,1,1024]{4,3,2,1,0:T(1,128)S(1)} %get-tuple-element.72), channel_id=1, source_target_pairs={{4,0},{8,4},{12,8},{16,12},{20,16},{24,20},{28,24},{5,1},{9,5},{13... | collective-permute-start | bytes 98312 | tf_op jit(solution)/shard_map/ppermute | solution.py:13
  33.5 11.5 %collective-permute-start.2 = (f32[2,2,2,1,1024]{4,3,2,1,0:T(1,128)S(1)}, f32[2,2,2,1,1024]{4,3,2,1,0:T(1,128)S(1)}, u32[]{:S(2)}, u32[]{:S(2)}) collective-permute-start(f32[2,2,2,1,1024]{4,3,2,1,0:T(1,128)S(1)} %get-tuple-element.71), channel_id=1, source_target_pairs={{0,4},{4,8},{8,12},{12,16},{16,20},{20,24},{24,28},{1,5},{5,9},{9,... | collective-permute-start | bytes 98312 | tf_op jit(solution)/shard_map/ppermute | solution.py:13
  38.0 7.2 %collective-permute-start.3 = (f32[2,2,2,1,1024]{4,3,2,1,0:T(1,128)S(1)}, f32[2,2,2,1,1024]{4,3,2,1,0:T(1,128)S(1)}, u32[]{:S(2)}, u32[]{:S(2)}) collective-permute-start(f32[2,2,2,1,1024]{4,3,2,1,0:T(1,128)S(1)} %get-tuple-element.70), channel_id=1, source_target_pairs={{4,0},{8,4},{12,8},{16,12},{20,16},{24,20},{28,24},{5,1},{9,5},{13... | collective-permute-start | bytes 98312 | tf_op jit(solution)/shard_map/ppermute | solution.py:13
  47.4 11.9 %collective-permute-start.4 = (f32[2,2,2,1,1024]{4,3,2,1,0:T(1,128)S(1)}, f32[2,2,2,1,1024]{4,3,2,1,0:T(1,128)S(1)}, u32[]{:S(2)}, u32[]{:S(2)}) collective-permute-start(f32[2,2,2,1,1024]{4,3,2,1,0:T(1,128)S(1)} %get-tuple-element.69), channel_id=1, source_target_pairs={{0,4},{4,8},{8,12},{12,16},{16,20},{20,24},{24,28},{1,5},{5,9},{9,... | collective-permute-start | bytes 98312 | tf_op jit(solution)/shard_map/ppermute | solution.py:13
  52.4 7.1 %collective-permute-start.5 = (f32[2,2,2,1,1024]{4,3,2,1,0:T(1,128)S(1)}, f32[2,2,2,1,1024]{4,3,2,1,0:T(1,128)S(1)}, u32[]{:S(2)}, u32[]{:S(2)}) collective-permute-start(f32[2,2,2,1,1024]{4,3,2,1,0:T(1,128)S(1)} %get-tuple-element.68), channel_id=1, source_target_pairs={{4,0},{8,4},{12,8},{16,12},{20,16},{24,20},{28,24},{5,1},{9,5},{13... | collective-permute-start | bytes 98312 | tf_op jit(solution)/shard_map/ppermute | solution.py:13
  60.6 7.5 %copy-start.40 = (f32[2]{0:T(128)S(1)}, f32[2]{0:T(128)}, u32[]{:S(2)}) copy-start(f32[2]{0:T(128)} %get-tuple-element.82) | copy-start | bytes 28
  61.3 10.9 %collective-permute-start.6 = (f32[2,2,2,1,1024]{4,3,2,1,0:T(1,128)S(1)}, f32[2,2,2,1,1024]{4,3,2,1,0:T(1,128)S(1)}, u32[]{:S(2)}, u32[]{:S(2)}) collective-permute-start(f32[2,2,2,1,1024]{4,3,2,1,0:T(1,128)S(1)} %get-tuple-element.67), channel_id=1, source_target_pairs={{0,4},{4,8},{8,12},{12,16},{16,20},{20,24},{24,28},{1,5},{5,9},{9,... | collective-permute-start | bytes 98312 | tf_op jit(solution)/shard_map/ppermute | solution.py:13
  66.7 6.7 %collective-permute-start.7 = (f32[2,2,2,1,1024]{4,3,2,1,0:T(1,128)S(1)}, f32[2,2,2,1,1024]{4,3,2,1,0:T(1,128)S(1)}, u32[]{:S(2)}, u32[]{:S(2)}) collective-permute-start(f32[2,2,2,1,1024]{4,3,2,1,0:T(1,128)S(1)} %get-tuple-element.66), channel_id=1, source_target_pairs={{4,0},{8,4},{12,8},{16,12},{20,16},{24,20},{28,24},{5,1},{9,5},{13... | collective-permute-start | bytes 98312 | tf_op jit(solution)/shard_map/ppermute | solution.py:13
  80.8 7.6 %copy-start.38 = (f32[2]{0:T(128)S(1)}, f32[2]{0:T(128)}, u32[]{:S(2)}) copy-start(f32[2]{0:T(128)} %get-tuple-element.80) | copy-start | bytes 28
  82.3 11.6 %collective-permute-start.8 = (f32[2,2,2,1,1024]{4,3,2,1,0:T(1,128)S(1)}, f32[2,2,2,1,1024]{4,3,2,1,0:T(1,128)S(1)}, u32[]{:S(2)}, u32[]{:S(2)}) collective-permute-start(f32[2,2,2,1,1024]{4,3,2,1,0:T(1,128)S(1)} %get-tuple-element.65), channel_id=1, source_target_pairs={{0,4},{4,8},{8,12},{12,16},{16,20},{20,24},{24,28},{1,5},{5,9},{9,... | collective-permute-start | bytes 98312 | tf_op jit(solution)/shard_map/ppermute | solution.py:13
  87.1 7.0 %collective-permute-start.9 = (f32[2,2,2,1,1024]{4,3,2,1,0:T(1,128)S(1)}, f32[2,2,2,1,1024]{4,3,2,1,0:T(1,128)S(1)}, u32[]{:S(2)}, u32[]{:S(2)}) collective-permute-start(f32[2,2,2,1,1024]{4,3,2,1,0:T(1,128)S(1)} %get-tuple-element.64), channel_id=1, source_target_pairs={{4,0},{8,4},{12,8},{16,12},{20,16},{24,20},{28,24},{5,1},{9,5},{13... | collective-permute-start | bytes 98312 | tf_op jit(solution)/shard_map/ppermute | solution.py:13
  95.9 12.0 %collective-permute-start.10 = (f32[2,2,2,1,1024]{4,3,2,1,0:T(1,128)S(1)}, f32[2,2,2,1,1024]{4,3,2,1,0:T(1,128)S(1)}, u32[]{:S(2)}, u32[]{:S(2)}) collective-permute-start(f32[2,2,2,1,1024]{4,3,2,1,0:T(1,128)S(1)} %get-tuple-element.63), channel_id=1, source_target_pairs={{0,4},{4,8},{8,12},{12,16},{16,20},{20,24},{24,28},{1,5},{5,9},{9,... | collective-permute-start | bytes 98312 | tf_op jit(solution)/shard_map/ppermute | solution.py:13
  100.9 7.2 %collective-permute-start.11 = (f32[2,2,2,1,1024]{4,3,2,1,0:T(1,128)S(1)}, f32[2,2,2,1,1024]{4,3,2,1,0:T(1,128)S(1)}, u32[]{:S(2)}, u32[]{:S(2)}) collective-permute-start(f32[2,2,2,1,1024]{4,3,2,1,0:T(1,128)S(1)} %get-tuple-element.62), channel_id=1, source_target_pairs={{4,0},{8,4},{12,8},{16,12},{20,16},{24,20},{28,24},{5,1},{9,5},{13... | collective-permute-start | bytes 98312 | tf_op jit(solution)/shard_map/ppermute | solution.py:13
  110.4 7.8 %copy-start.36 = (f32[2]{0:T(128)S(1)}, f32[2]{0:T(128)}, u32[]{:S(2)}) copy-start(f32[2]{0:T(128)} %get-tuple-element.78) | copy-start | bytes 28
  111.4 12.4 %collective-permute-start.12 = (f32[2,2,2,1,1024]{4,3,2,1,0:T(1,128)S(1)}, f32[2,2,2,1,1024]{4,3,2,1,0:T(1,128)S(1)}, u32[]{:S(2)}, u32[]{:S(2)}) collective-permute-start(f32[2,2,2,1,1024]{4,3,2,1,0:T(1,128)S(1)} %get-tuple-element.61), channel_id=1, source_target_pairs={{0,4},{4,8},{8,12},{12,16},{16,20},{20,24},{24,28},{1,5},{5,9},{9,... | collective-permute-start | bytes 98312 | tf_op jit(solution)/shard_map/ppermute | solution.py:13
  116.9 7.1 %collective-permute-start.13 = (f32[2,2,2,1,1024]{4,3,2,1,0:T(1,128)S(1)}, f32[2,2,2,1,1024]{4,3,2,1,0:T(1,128)S(1)}, u32[]{:S(2)}, u32[]{:S(2)}) collective-permute-start(f32[2,2,2,1,1024]{4,3,2,1,0:T(1,128)S(1)} %get-tuple-element.60), channel_id=1, source_target_pairs={{4,0},{8,4},{12,8},{16,12},{20,16},{24,20},{28,24},{5,1},{9,5},{13... | collective-permute-start | bytes 98312 | tf_op jit(solution)/shard_map/ppermute | solution.py:13
  125.7 12.3 %collective-permute-start.14 = (f32[2,2,2,1,1024]{4,3,2,1,0:T(1,128)S(1)}, f32[2,2,2,1,1024]{4,3,2,1,0:T(1,128)S(1)}, u32[]{:S(2)}, u32[]{:S(2)}) collective-permute-start(f32[2,2,2,1,1024]{4,3,2,1,0:T(1,128)S(1)} %get-tuple-element.59), channel_id=1, source_target_pairs={{0,4},{4,8},{8,12},{12,16},{16,20},{20,24},{24,28},{1,5},{5,9},{9,... | collective-permute-start | bytes 98312 | tf_op jit(solution)/shard_map/ppermute | solution.py:13
  131.2 7.1 %collective-permute-start.15 = (f32[2,2,2,1,1024]{4,3,2,1,0:T(1,128)S(1)}, f32[2,2,2,1,1024]{4,3,2,1,0:T(1,128)S(1)}, u32[]{:S(2)}, u32[]{:S(2)}) collective-permute-start(f32[2,2,2,1,1024]{4,3,2,1,0:T(1,128)S(1)} %get-tuple-element.58), channel_id=1, source_target_pairs={{4,0},{8,4},{12,8},{16,12},{20,16},{24,20},{28,24},{5,1},{9,5},{13... | collective-permute-start | bytes 98312 | tf_op jit(solution)/shard_map/ppermute | solution.py:13
  (35 other events, 99.4 us)
Sparse Core Ops, SparseCore 0:
  147.1 35.3 all-reduce.17
where the time goes:
time: 192 us; the launch traced here: 191 us
  other arithmetic  62.5 us (33%)
  starting transfers between devices  50.9 us (27%)
  waiting for transfers between devices  35.9 us (19%)
  local copies, waits for them, and re-layouts  18.2 us (9%)
  between operations  17.7 us (9%)
  blocking collectives  5.59 us (3%)
    ppermute x16, starting transfers between devices, passed_along(): lax.ppermute(value, axis, [(source, source + steps) for source in range(i...  50.9 us
    add x10, other arithmetic, weighted(): src_re = coef_re * cheb_term[0, 0] + coef_im * cheb_term[0, 1]  39.8 us
    psum x1, waiting for transfers between devices, shards(): summed = lax.psum(stacked, 'freq')  34.8 us
    another operation x20, other arithmetic, weighted(): return jnp.stack([jnp.stack([src_re, src_im]), jnp.stack([rec_re, rec_im])])  9.64 us
    all_gather x1, blocking collectives, shards(): planes = lax.all_gather(slowness, 'freq', axis=2, tiled=True)  5.59 us
    unnamed x84, local copies, waits for them, and re-layouts  5.41 us
    slice x8, local copies, waits for them, and re-layouts, mcclellan(): padded_cols[..., :-2] + padded_cols[..., 2:]  4.84 us
    mul x6, other arithmetic, shards(): following = live_rows * (2.0 * spread - previous)  4.05 us
  transfers between devices with their start and end apart: 17, of which 2 were waited for; matrix products, arithmetic and copies ran while one was open for 24% of the time, Pallas kernels for 0%

commit v1 on v0

v1 whole, which is shorter than its diff:
```python
import jax
import jax.numpy as jnp
from jax import lax
from jax.experimental import pallas as pl
from jax.experimental.pallas import tpu as pltpu
from jax.sharding import PartitionSpec as P

ORDER = 4
NDEPTH = 2
HALO = ORDER * NDEPTH
PAD = 10
F32 = jnp.float32
VMEM = pl.BlockSpec(memory_space=pltpu.VMEM)
SMEM = pl.BlockSpec(memory_space=pltpu.SMEM)


def to_rows(flat, load_tile, row_tiles):
    for i in range(row_tiles):
        for j in range(8):
            flat[pl.ds((i * 8 + j) * 8, 8), :] = load_tile(i, j)


def row_of(flat, row):
    start = (row // 8) * 64 + row % 8
    return flat[pl.ds(start, 8, stride=8), :]


def pack_kernel(aperture, source, receiver, planes, ahead, behind, *flats):
    width = aperture[lax.axis_index("tile")]
    row_tiles = source.shape[2] // 8
    plane = 0
    for field in (source, receiver):
        for part in range(2):
            for freq in range(source.shape[1]):
                flat = flats[plane]
                to_rows(
                    flat,
                    lambda i, j: field[part, freq, pl.ds(8 * i, 8), pl.ds(128 * j, 128)],
                    row_tiles,
                )
                for k in range(HALO):
                    ahead[plane * HALO + k] = row_of(flat, width - HALO + k)
                    behind[plane * HALO + k] = row_of(flat, k)
                plane += 1
    flat = flats[plane]
    to_rows(
        flat,
        lambda i, j: planes[j // 2, 0, pl.ds(8 * i, 8), pl.ds(128 * (j % 2), 128)],
        row_tiles,
    )
    for k in range(ORDER):
        ahead[plane * HALO + k] = row_of(flat, width - ORDER + k)
        behind[plane * HALO + k] = row_of(flat, k)


def spread(above, here, below, before, masks):
    first_lane, last_lane, first_cell, last_cell = masks
    rows = (above + below) + (here + here)
    from_left = pltpu.roll(rows, 1, 1)
    from_right = pltpu.roll(rows, 127, 1)
    wrap_left = pltpu.roll(from_left, 1, 0)
    wrap_right = pltpu.roll(from_right, 7, 0)
    left = jnp.where(first_lane, jnp.where(first_cell, 0.0, wrap_left), from_left)
    right = jnp.where(last_lane, jnp.where(last_cell, 0.0, wrap_right), from_right)
    blurred = (left + right) + (rows + rows)
    if before is None:
        return 0.125 * blurred - here
    return (0.25 * blurred - (here + here)) - before


def main_kernel(
    aperture, frequency, order_table, filter_coeffs,
    source, receiver, planes, from_before, from_after,
    image_out, receiver_out,
    flat, slow, weights, images, *buffers,
):
    tile = lax.axis_index("tile")
    last_tile = lax.axis_size("tile") - 1
    width = aperture[tile]
    freqs = source.shape[1]
    stored = source.shape[2]
    row_tiles = stored // 8
    count = 4 * freqs
    start, middle = buffers[:count], buffers[count : 2 * count]
    terms = [buffers[(2 + n) * count : (3 + n) * count] for n in range(ORDER)]

    lane = lax.broadcasted_iota(jnp.int32, (8, 128), 1)
    sub = lax.broadcasted_iota(jnp.int32, (8, 128), 0)
    first_lane, last_lane = lane == 0, lane == 127
    masks = (first_lane, last_lane, sub == 0, sub == 7)

    base = PAD + HALO
    plane = 0
    for field in (source, receiver):
        for part in range(2):
            for freq in range(freqs):
                to_rows(
                    flat.at[plane % 2],
                    lambda i, j: field[part, freq, pl.ds(8 * i, 8), pl.ds(128 * j, 128)],
                    row_tiles,
                )
                for r in range(stored):
                    start[plane][base + r] = row_of(flat.at[plane % 2], r)
                for k in range(HALO):
                    start[plane][PAD + k] = from_before[plane * HALO + k]
                    start[plane][base + width + k] = from_after[plane * HALO + k]
                plane += 1
    for depth in range(NDEPTH):
        to_rows(
            flat.at[depth],
            lambda i, j: planes[j // 2, depth, pl.ds(8 * i, 8), pl.ds(128 * (j % 2), 128)],
            row_tiles,
        )
        for r in range(stored):
            slow[depth, base + r] = row_of(flat.at[depth], r)
    for k in range(ORDER):
        slow[0, base - ORDER + k] = from_before[count * HALO + k]
        slow[0, base + width + k] = from_after[count * HALO + k]

    @pl.when(tile == 0)
    def _():
        for p in range(count):
            start[p][base - 1] = jnp.zeros((8, 128), F32)
            for k in range(1, HALO):
                start[p][base - 1 - k] = -start[p][base + k - 1]
        slow[0, base - 1] = slow[0, base]
        for k in range(1, ORDER):
            slow[0, base - 1 - k] = slow[0, base + k - 1]

    @pl.when(tile == last_tile)
    def _():
        for p in range(count):
            start[p][base + width] = jnp.zeros((8, 128), F32)
            for k in range(1, HALO):
                start[p][base + width + k] = -start[p][base + width - k]
        slow[0, base + width] = slow[0, base + width - 1]
        for k in range(1, ORDER):
            slow[0, base + width + k] = slow[0, base + width - k]

    powers = filter_coeffs.shape[2]
    for depth in range(NDEPTH):
        for freq in range(freqs):
            for n in range(ORDER + 1):
                active = jnp.where(order_table[depth, freq] >= n, 1.0, 0.0)
                for c in range(2):
                    for m in range(powers):
                        weights[depth, freq, (n * 2 + c) * powers + m] = jnp.full(
                            (8, 128), filter_coeffs[c, n, m] * active, F32
                        )

    def weigh(depth, freq, row, slow_row, fields):
        wavenumber = frequency[freq] * slow[depth, slow_row]
        out = [None] * 4
        for n in range(ORDER + 1):
            def poly(c):
                at = (n * 2 + c) * powers
                value = weights[depth, freq, at + powers - 1]
                for m in range(powers - 2, -1, -1):
                    value = value * wavenumber + weights[depth, freq, at + m]
                return value

            re, im = poly(0), poly(1)
            level = fields if n == 0 else terms[n - 1]
            src_re, src_im, rec_re, rec_im = (level[q * freqs + freq][row] for q in range(4))
            part = (
                re * src_re + im * src_im,
                re * src_im - im * src_re,
                re * rec_re - im * rec_im,
                re * rec_im + im * rec_re,
            )
            out = part if n == 0 else tuple(a + b for a, b in zip(out, part))
        return out

    def sweep(depth, fields, results, rows, slow_shift):
        def step(i, carry):
            row = i - (2 * ORDER - 1)
            total = None
            for freq in range(freqs):
                out = weigh(depth, freq, row, row + slow_shift, fields)
                for q in range(4):
                    results[q * freqs + freq][row - ORDER] = out[q]
                term = out[0] * out[2] + out[1] * out[3]
                total = term if total is None else total + term
            images[depth, row - ORDER] = total
            for n in range(ORDER, 0, -1):
                row = i - 2 * (n - 1)
                level = fields if n == 1 else terms[n - 2]
                older = None if n == 1 else (fields if n == 2 else terms[n - 3])
                for p in range(count):
                    terms[n - 1][p][row] = spread(
                        level[p][row - 1], level[p][row], level[p][row + 1],
                        None if n == 1 else older[p][row], masks,
                    )
            return carry

        lax.fori_loop(PAD + 1, PAD + rows + ORDER - 1, step, 0)

    total_rows = stored + 2 * HALO
    sweep(0, start, middle, total_rows, 0)
    sweep(1, middle, start, total_rows - 2 * ORDER, ORDER)

    for depth in range(NDEPTH):
        shift = PAD + HALO - ORDER * (depth + 1)
        for r in range(stored):
            value = jnp.where(r < width, images[depth, shift + r], 0.0)
            image_out[pl.ds(depth * stored + r, 8, stride=NDEPTH * stored), :] = value
    for part in range(2):
        for freq in range(freqs):
            p = (2 + part) * freqs + freq
            for r in range(stored):
                at = (r // 8) * 64 + r % 8
                flat[p % 2, pl.ds(at, 8, stride=8), :] = jnp.where(
                    r < width, start[p][PAD + r], 0.0
                )
            for i in range(row_tiles):
                for j in range(8):
                    receiver_out[part, freq, pl.ds(8 * i, 8), pl.ds(128 * j, 128)] = flat[
                        p % 2, pl.ds((i * 8 + j) * 8, 8), :
                    ]


def image_kernel(parts, out):
    senders = 4
    depths, stored = out.shape[0], out.shape[1]
    size = parts.shape[0] // senders
    for j in range(size // (depths * stored)):
        for depth in range(depths):
            total = None
            for s in range(senders):
                at = s * size + (j * depths + depth) * stored
                term = parts[pl.ds(at, stored), :]
                total = term if total is None else total + term
            out[depth, :, pl.ds(128 * j, 128)] = total


def passed_along(value, axis, steps):
    count = lax.axis_size(axis)
    initial, last = (max(0, -steps), min(count, count - steps))
    return lax.ppermute(value, axis, [(source, source + steps) for source in range(initial, last)])


def shards(source_field, receiver_field, slowness, frequency, order_table, filter_coeffs, aperture):
    freqs, stored = source_field.shape[1:3]
    count = 4 * freqs
    planes = lax.all_gather(slowness, "freq", axis=0)
    halo = jax.ShapeDtypeStruct((count * HALO + ORDER, 8, 128), F32)
    ahead, behind = pl.pallas_call(
        pack_kernel,
        out_shape=(halo, halo),
        in_specs=[SMEM] + [VMEM] * 3,
        out_specs=(VMEM, VMEM),
        scratch_shapes=[pltpu.VMEM((stored * 8, 128), F32)] * (count + 1),
        compiler_params=pltpu.CompilerParams(vmem_limit_bytes=32 << 20),
        name="pack",
    )(aperture, source_field, receiver_field, planes)
    from_before = passed_along(ahead, "tile", 1)
    from_after = passed_along(behind, "tile", -1)
    rows = PAD + stored + 2 * HALO + PAD
    image_parts, receiver_out = pl.pallas_call(
        main_kernel,
        out_shape=(
            jax.ShapeDtypeStruct((8 * NDEPTH * stored, 128), F32),
            jax.ShapeDtypeStruct(receiver_field.shape, F32),
        ),
        in_specs=[SMEM] * 4 + [VMEM] * 5,
        out_specs=(VMEM, VMEM),
        scratch_shapes=[
            pltpu.VMEM((2, stored * 8, 128), F32),
            pltpu.VMEM((NDEPTH, rows, 8, 128), F32),
            pltpu.VMEM((NDEPTH, freqs, 2 * (ORDER + 1) * filter_coeffs.shape[2], 8, 128), F32),
            pltpu.VMEM((NDEPTH, rows, 8, 128), F32),
        ]
        + [pltpu.VMEM((rows, 8, 128), F32)] * (count * (2 + ORDER)),
        compiler_params=pltpu.CompilerParams(vmem_limit_bytes=48 << 20),
        name="migrate",
    )(
        aperture, frequency, order_table, filter_coeffs,
        source_field, receiver_field, planes, from_before, from_after,
    )
    exchanged = lax.all_to_all(image_parts, "freq", 0, 0, tiled=True)
    image_out = pl.pallas_call(
        image_kernel,
        out_shape=jax.ShapeDtypeStruct(slowness.shape, F32),
        in_specs=[VMEM],
        out_specs=VMEM,
        name="image",
    )(exchanged)
    return image_out, receiver_out


def solution(mesh):
    placed = (
        P(None, "freq", "tile", None),
        P(None, "freq", "tile", None),
        P(None, "tile", "freq"),
        P("freq"),
        P(None, "freq"),
        P(),
        P(),
    )
    return jax.shard_map(
        shards,
        mesh=mesh,
        in_specs=placed,
        out_specs=(P(None, "tile", "freq"), P(None, "freq", "tile", None)),
        check_vma=False,
    )
```

time: 192 us -> 52 us (0.27)
  other arithmetic: 62.5 us -> 0 us
  starting transfers between devices: 50.9 us -> 4.95 us
  waiting for transfers between devices: 35.9 us -> 10.9 us
  between operations: 17.7 us -> 0.7 us
  Pallas kernels: 0 us -> 16.5 us
  local copies, waits for them, and re-layouts: 18.2 us -> 2.77 us
  blocking collectives: 5.59 us -> 15.4 us
    ppermute x16 -> x2, starting transfers between devices: 50.9 us -> 4.95 us  [passed_along(): lax.ppermute(value, axis, [(source, source + steps) for source in range(i...]
    add x20 -> x0, other arithmetic: 42.9 us -> none  [the longest x10 39.8 us: weighted(): src_re = coef_re * cheb_term[0, 0] + coef_im * cheb_term[0, 1]]
    psum x1 -> x0, waiting for transfers between devices: 34.8 us -> none  [shards(): summed = lax.psum(stacked, 'freq')]
    pallas_call x0 -> x3, Pallas kernels: none -> 16.5 us  [the longest x1 14.2 us: shards(): pl.pallas_call(main_kernel, out_shape=(jax.ShapeDtypeStruct((8 * NDEPTH *...]
    another operation x21 -> x0, other arithmetic: 10.3 us -> none  [the longest x20 9.64 us: weighted(): return jnp.stack([jnp.stack([src_re, src_im]), jnp.stack([rec_re, rec_im])])]
    ppermute x16 -> x2, waiting for transfers between devices: 1.13 us -> 10.9 us  [passed_along(): lax.ppermute(value, axis, [(source, source + steps) for source in range(i...]
    all_to_all x0 -> x1, blocking collectives: none -> 8.38 us  [shards(): exchanged = lax.all_to_all(image_parts, 'freq', 0, 0, tiled=True)]
    slice x18 -> x0, local copies, waits for them, and re-layouts: 6.63 us -> none  [the longest x8 4.84 us: mcclellan(): padded_cols[..., :-2] + padded_cols[..., 2:]]
  transfers between devices with their start and end apart: 17 -> 2, of which waited for: 2 -> 1; matrix products, arithmetic and copies ran while one was open for 24% -> 0% of each run, Pallas kernels for 0% -> 0%
where the time goes in v1:
time: 52 us; the launch traced here: 51.3 us
  Pallas kernels  16.5 us (32%)
  blocking collectives  15.4 us (30%)
  waiting for transfers between devices  10.9 us (21%)
  starting transfers between devices  4.95 us (10%)
  local copies, waits for them, and re-layouts  2.77 us (5%)
  between operations  0.7 us (1%)
    pallas_call x1, Pallas kernels, shards(): pl.pallas_call(main_kernel, out_shape=(jax.ShapeDtypeStruct((8 * NDEPTH *...  14.2 us
    ppermute x2, waiting for transfers between devices, passed_along(): lax.ppermute(value, axis, [(source, source + steps) for source in range(i...  10.9 us
    all_to_all x1, blocking collectives, shards(): exchanged = lax.all_to_all(image_parts, 'freq', 0, 0, tiled=True)  8.38 us
    all_gather x1, blocking collectives, shards(): planes = lax.all_gather(slowness, 'freq', axis=0)  7.05 us
    ppermute x2, starting transfers between devices, passed_along(): lax.ppermute(value, axis, [(source, source + steps) for source in range(i...  4.95 us
    unnamed x17, local copies, waits for them, and re-layouts  2.77 us
    pallas_call x1, Pallas kernels, shards(): pl.pallas_call(image_kernel, out_shape=jax.ShapeDtypeStruct(slowness.shap...  1.56 us
  transfers between devices with their start and end apart: 2, of which 1 were waited for; matrix products, arithmetic and copies ran while one was open for 0% of the time, Pallas kernels for 0%

profile of v1, /device:TPU:0, one launch (start us, length us, event | category | flops | bytes accessed | tf_op | source)
XLA Modules:
  0.0 51.3 jit_solution(16692389509278193123)
XLA Ops:
  0.6 7.0 %all-gather = f32[8,24,256]{2,1,0:T(8,128)S(1)} all-gather(f32[2,24,256]{2,1,0:T(8,128)} %param.9), channel_id=2, replica_groups=mesh['tile'=8,'freq'=4] {'freq'}, dimensions={0}, use_global_device_ids=true | all-gather | bytes 245760 | tf_op jit(solution)/shard_map/all_gather | solution.py:245
  7.7 0.0 copy-start.4
  7.7 0.7 %copy-done.4 = s32[8]{0:T(128)S(1)} copy-done((s32[8]{0:T(128)S(1)}, s32[8]{0:T(128)}, u32[]{:S(2)}) %copy-start.4) | copy-done | bytes 56
  8.3 0.0 copy-start
  8.3 1.0 %copy-done = f32[2,2,24,1024]{3,2,1,0:T(8,128)S(1)} copy-done((f32[2,2,24,1024]{3,2,1,0:T(8,128)S(1)}, f32[2,2,24,1024]{3,2,1,0:T(8,128)}, u32[]{:S(2)}) %copy-start) | copy-done | bytes 393240
  9.3 0.0 copy-start.2
  9.3 1.0 %copy-done.2 = f32[2,2,24,1024]{3,2,1,0:T(8,128)S(1)} copy-done((f32[2,2,24,1024]{3,2,1,0:T(8,128)S(1)}, f32[2,2,24,1024]{3,2,1,0:T(8,128)}, u32[]{:S(2)}) %copy-start.2) | copy-done | bytes 393240
  10.3 0.7 %pack.1 = (f32[68,8,128]{2,1,0:T(8,128)S(1)}, f32[68,8,128]{2,1,0:T(8,128)S(1)}) custom-call(s32[8]{0:T(128)S(1)} %copy-done.4, f32[2,2,24,1024]{3,2,1,0:T(8,128)S(1)} %copy-done, f32[2,2,24,1024]{3,2,1,0:T(8,128)S(1)} %copy-done.2, f32[4,2,24,256]{3,2,1,0:T(8,128)S(1)} %bitcast.3), custom_call_target="tpu_custom_call" | custom-call | tf_op jit(solution)/shard_map/pack/pallas_call | solution.py:247
  11.0 0.0 copy-start.7
  11.1 3.7 %collective-permute-start = (f32[68,8,128]{2,1,0:T(8,128)S(1)}, f32[68,8,128]{2,1,0:T(8,128)S(1)}, u32[]{:S(2)}, u32[]{:S(2)}) collective-permute-start(f32[68,8,128]{2,1,0:T(8,128)S(1)} %get-tuple-element.6), channel_id=1, source_target_pairs={{0,4},{4,8},{8,12},{12,16},{16,20},{20,24},{24,28},{1,5},{5,9},{9,... | collective-permute-start | bytes 835592 | tf_op jit(solution)/shard_map/ppermute | solution.py:239
  14.7 0.0 copy-start.5
  14.7 0.0 copy-start.6
  14.7 1.3 %collective-permute-start.1 = (f32[68,8,128]{2,1,0:T(8,128)S(1)}, f32[68,8,128]{2,1,0:T(8,128)S(1)}, u32[]{:S(2)}, u32[]{:S(2)}) collective-permute-start(f32[68,8,128]{2,1,0:T(8,128)S(1)} %get-tuple-element.7), channel_id=1, source_target_pairs={{4,0},{8,4},{12,8},{16,12},{20,16},{24,20},{28,24},{5,1},{9,5},{13... | collective-permute-start | bytes 835592 | tf_op jit(solution)/shard_map/ppermute | solution.py:239
  16.0 0.0 copy-done.7
  16.1 0.1 copy.10.filter_coeffs
  16.2 10.9 %collective-permute-done.from_before = f32[68,8,128]{2,1,0:T(8,128)S(1)} collective-permute-done((f32[68,8,128]{2,1,0:T(8,128)S(1)}, f32[68,8,128]{2,1,0:T(8,128)S(1)}, u32[]{:S(2)}, u32[]{:S(2)}) %collective-permute-start) | collective-permute-done | bytes 278560 | tf_op jit(solution)/shard_map/ppermute | solution.py:239
  27.1 0.0 collective-permute-done.1.from_after
  27.1 0.0 copy-done.1
  27.1 0.0 copy-done.3
  27.1 0.0 copy-done.5
  27.1 0.0 copy-done.6
  27.1 14.2 %migrate.1 = (f32[384,128]{1,0:T(8,128)S(1)}, f32[2,2,24,1024]{3,2,1,0:T(8,128)}) custom-call(s32[8]{0:T(128)S(1)} %copy-done.4, f32[2]{0:T(128)S(1)} %copy-done.6, s32[2,2]{1,0:T(2,128)S(1)} %copy-done.5, f32[2,5,3]{2,1,0:T(8,128)S(1)} %copy.10.filter_coeffs, f32[2,2,24,1024]{3,2,1,0:T(8,128)S(1)} %copy-done.1, f32[2,2,24,1024]{3,2,1,0:T(8,128)S(1)} %copy-done.3, ...), custom_call_target="tpu_custom_call" | custom-call | tf_op jit(solution)/shard_map/migrate/pallas_call | solution.py:259
  41.3 8.4 %all_to_all.11 = f32[4,96,128]{2,1,0:T(8,128)} all-to-all(f32[4,96,128]{2,1,0:T(8,128)S(1)} %bitcast.5), channel_id=1, replica_groups=mesh['tile'=8,'freq'=4] {'freq'}, dimensions={0} | all-to-all | bytes 393216 | tf_op jit(solution)/shard_map/all_to_all | solution.py:280
  49.7 1.6 %image.1 = f32[2,24,256]{2,1,0:T(8,128)} custom-call(f32[384,128]{1,0:T(8,128)} %bitcast.6), custom_call_target="tpu_custom_call" | custom-call | tf_op jit(solution)/shard_map/image/pallas_call | solution.py:281
  (2 shorter events, 0.0 us)
Async XLA Ops:
  7.7 0.7 %copy-start.4 = (s32[8]{0:T(128)S(1)}, s32[8]{0:T(128)}, u32[]{:S(2)}) copy-start(s32[8]{0:T(128)} %aperture.3) | copy-start | bytes 100
  8.3 1.0 %copy-start = (f32[2,2,24,1024]{3,2,1,0:T(8,128)S(1)}, f32[2,2,24,1024]{3,2,1,0:T(8,128)}, u32[]{:S(2)}) copy-start(f32[2,2,24,1024]{3,2,1,0:T(8,128)} %source.3) | copy-start | bytes 1179652
  9.3 1.0 %copy-start.2 = (f32[2,2,24,1024]{3,2,1,0:T(8,128)S(1)}, f32[2,2,24,1024]{3,2,1,0:T(8,128)}, u32[]{:S(2)}) copy-start(f32[2,2,24,1024]{3,2,1,0:T(8,128)} %receiver.3) | copy-start | bytes 1179652
  10.3 16.8 %copy-start.1 = (f32[2,2,24,1024]{3,2,1,0:T(8,128)S(1)}, f32[2,2,24,1024]{3,2,1,0:T(8,128)}, u32[]{:S(2)}) copy-start(f32[2,2,24,1024]{3,2,1,0:T(8,128)} %source.3) | copy-start | bytes 1179652
  10.3 16.8 %copy-start.3 = (f32[2,2,24,1024]{3,2,1,0:T(8,128)S(1)}, f32[2,2,24,1024]{3,2,1,0:T(8,128)}, u32[]{:S(2)}) copy-start(f32[2,2,24,1024]{3,2,1,0:T(8,128)} %receiver.3) | copy-start | bytes 1179652
  11.0 5.0 %copy-start.7 = (f32[2,5,3]{1,0,2:T(2,128)S(1)}, f32[2,5,3]{1,0,2:T(2,128)}, u32[]{:S(2)}) copy-start(f32[2,5,3]{1,0,2:T(2,128)} %param.12) | copy-start | bytes 364
  11.1 16.0 %collective-permute-start = (f32[68,8,128]{2,1,0:T(8,128)S(1)}, f32[68,8,128]{2,1,0:T(8,128)S(1)}, u32[]{:S(2)}, u32[]{:S(2)}) collective-permute-start(f32[68,8,128]{2,1,0:T(8,128)S(1)} %get-tuple-element.6), channel_id=1, source_target_pairs={{0,4},{4,8},{8,12},{12,16},{16,20},{20,24},{24,28},{1,5},{5,9},{9,... | collective-permute-start | bytes 835592 | tf_op jit(solution)/shard_map/ppermute | solution.py:239
  14.7 12.4 %copy-start.5 = (s32[2,2]{1,0:T(2,128)S(1)}, s32[2,2]{1,0:T(2,128)}, u32[]{:S(2)}) copy-start(s32[2,2]{1,0:T(2,128)} %order_table.1) | copy-start | bytes 52
  14.7 12.4 %copy-start.6 = (f32[2]{0:T(128)S(1)}, f32[2]{0:T(128)}, u32[]{:S(2)}) copy-start(f32[2]{0:T(128)} %frequency.1) | copy-start | bytes 28
  14.7 12.3 %collective-permute-start.1 = (f32[68,8,128]{2,1,0:T(8,128)S(1)}, f32[68,8,128]{2,1,0:T(8,128)S(1)}, u32[]{:S(2)}, u32[]{:S(2)}) collective-permute-start(f32[68,8,128]{2,1,0:T(8,128)S(1)} %get-tuple-element.7), channel_id=1, source_target_pairs={{4,0},{8,4},{12,8},{16,12},{20,16},{24,20},{28,24},{5,1},{9,5},{13... | collective-permute-start | bytes 835592 | tf_op jit(solution)/shard_map/ppermute | solution.py:239

commit v2 on v1

--- a/solution.py
+++ b/solution.py
@@ -199,11 +199,20 @@
     sweep(0, start, middle, total_rows, 0)
     sweep(1, middle, start, total_rows - 2 * ORDER, ORDER)
 
+    columns = image_out.shape[3]
     for depth in range(NDEPTH):
         shift = PAD + HALO - ORDER * (depth + 1)
         for r in range(stored):
-            value = jnp.where(r < width, images[depth, shift + r], 0.0)
-            image_out[pl.ds(depth * stored + r, 8, stride=NDEPTH * stored), :] = value
+            at = (r // 8) * 64 + r % 8
+            flat[depth, pl.ds(at, 8, stride=8), :] = jnp.where(
+                r < width, images[depth, shift + r], 0.0
+            )
+        for i in range(row_tiles):
+            for j in range(8):
+                owner, column = (128 * j) // columns, (128 * j) % columns
+                image_out[owner, depth, pl.ds(8 * i, 8), pl.ds(column, 128)] = flat[
+                    depth, pl.ds((i * 8 + j) * 8, 8), :
+                ]
     for part in range(2):
         for freq in range(freqs):
             p = (2 + part) * freqs + freq
@@ -217,20 +226,6 @@
                     receiver_out[part, freq, pl.ds(8 * i, 8), pl.ds(128 * j, 128)] = flat[
                         p % 2, pl.ds((i * 8 + j) * 8, 8), :
                     ]
-
-
-def image_kernel(parts, out):
-    senders = 4
-    depths, stored = out.shape[0], out.shape[1]
-    size = parts.shape[0] // senders
-    for j in range(size // (depths * stored)):
-        for depth in range(depths):
-            total = None
-            for s in range(senders):
-                at = s * size + (j * depths + depth) * stored
-                term = parts[pl.ds(at, stored), :]
-                total = term if total is None else total + term
-            out[depth, :, pl.ds(128 * j, 128)] = total
 
 
 def passed_along(value, axis, steps):
@@ -259,7 +254,7 @@
     image_parts, receiver_out = pl.pallas_call(
         main_kernel,
         out_shape=(
-            jax.ShapeDtypeStruct((8 * NDEPTH * stored, 128), F32),
+            jax.ShapeDtypeStruct((lax.axis_size("freq"),) + slowness.shape, F32),
             jax.ShapeDtypeStruct(receiver_field.shape, F32),
         ),
         in_specs=[SMEM] * 4 + [VMEM] * 5,
@@ -277,14 +272,7 @@
         aperture, frequency, order_table, filter_coeffs,
         source_field, receiver_field, planes, from_before, from_after,
     )
-    exchanged = lax.all_to_all(image_parts, "freq", 0, 0, tiled=True)
-    image_out = pl.pallas_call(
-        image_kernel,
-        out_shape=jax.ShapeDtypeStruct(slowness.shape, F32),
-        in_specs=[VMEM],
-        out_specs=VMEM,
-        name="image",
-    )(exchanged)
+    image_out = lax.psum_scatter(image_parts, "freq", scatter_dimension=0)
     return image_out, receiver_out
 
 

time: 52 us -> 77.1 us (1.48)
  waiting for transfers between devices: 10.9 us -> 33 us
  between operations: 0.7 us -> 14.1 us
  blocking collectives: 15.4 us -> 7.05 us
  Pallas kernels: 16.5 us -> 14.9 us
    reduce_scatter x0 -> x1, waiting for transfers between devices: none -> 22 us  [shards(): image_out = lax.psum_scatter(image_parts, 'freq', scatter_dimension=0)]
    all_to_all x1 -> x0, blocking collectives: 8.38 us -> none  [shards(): exchanged = lax.all_to_all(image_parts, 'freq', 0, 0, tiled=True)]
    pallas_call x2 -> x1, Pallas kernels: 15.8 us -> 14.2 us  [shards(): pl.pallas_call(main_kernel, out_shape=(jax.ShapeDtypeStruct((lax.axis_siz...]
  transfers between devices with their start and end apart: 2 -> 3, of which waited for: 1 -> 2; matrix products, arithmetic and copies ran while one was open for 0% -> 0% of each run, Pallas kernels for 0% -> 0%
where the time goes in v2:
time: 77.1 us; the launch traced here: 76.8 us
  waiting for transfers between devices  33 us (43%)
  Pallas kernels  14.9 us (19%)
  between operations  14.1 us (18%)
  blocking collectives  7.05 us (9%)
  starting transfers between devices  4.99 us (6%)
  local copies, waits for them, and re-layouts  2.77 us (4%)
    reduce_scatter x1, waiting for transfers between devices, shards(): image_out = lax.psum_scatter(image_parts, 'freq', scatter_dimension=0)  22 us
    pallas_call x1, Pallas kernels, shards(): pl.pallas_call(main_kernel, out_shape=(jax.ShapeDtypeStruct((lax.axis_siz...  14.2 us
    ppermute x2, waiting for transfers between devices, passed_along(): lax.ppermute(value, axis, [(source, source + steps) for source in range(i...  10.9 us
    all_gather x1, blocking collectives, shards(): planes = lax.all_gather(slowness, 'freq', axis=0)  7.05 us
    ppermute x2, starting transfers between devices, passed_along(): lax.ppermute(value, axis, [(source, source + steps) for source in range(i...  4.95 us
    unnamed x17, local copies, waits for them, and re-layouts  2.77 us
  transfers between devices with their start and end apart: 3, of which 2 were waited for; matrix products, arithmetic and copies ran while one was open for 0% of the time, Pallas kernels for 0%

profile of v2, /device:TPU:0, one launch (start us, length us, event | category | flops | bytes accessed | tf_op | source)
XLA Modules:
  0.0 76.8 jit_solution(474300554286889265)
XLA Ops:
  7.2 0.0 reduce-scatter.2.cloned.1.call-start
  7.2 7.0 %all-gather = f32[8,24,256]{2,1,0:T(8,128)S(1)} all-gather(f32[2,24,256]{2,1,0:T(8,128)} %param.9), channel_id=2, replica_groups=mesh['tile'=8,'freq'=4] {'freq'}, dimensions={0}, use_global_device_ids=true | all-gather | bytes 245760 | tf_op jit(solution)/shard_map/all_gather | solution.py:240
  14.3 0.0 copy-start.4
  14.3 0.7 copy-done.4
  14.9 0.0 copy-start
  14.9 1.0 %copy-done = f32[2,2,24,1024]{3,2,1,0:T(8,128)S(1)} copy-done((f32[2,2,24,1024]{3,2,1,0:T(8,128)S(1)}, f32[2,2,24,1024]{3,2,1,0:T(8,128)}, u32[]{:S(2)}) %copy-start) | copy-done | bytes 393240
  15.9 1.0 %copy-done.2 = f32[2,2,24,1024]{3,2,1,0:T(8,128)S(1)} copy-done((f32[2,2,24,1024]{3,2,1,0:T(8,128)S(1)}, f32[2,2,24,1024]{3,2,1,0:T(8,128)}, u32[]{:S(2)}) %copy-start.2) | copy-done | bytes 393240
  16.9 0.7 pack.1
  17.6 0.0 copy-start.7
  17.6 3.7 %collective-permute-start = (f32[68,8,128]{2,1,0:T(8,128)S(1)}, f32[68,8,128]{2,1,0:T(8,128)S(1)}, u32[]{:S(2)}, u32[]{:S(2)}) collective-permute-start(f32[68,8,128]{2,1,0:T(8,128)S(1)} %get-tuple-element.6), channel_id=1, source_target_pairs={{0,4},{4,8},{8,12},{12,16},{16,20},{20,24},{24,28},{1,5},{5,9},{9,... | collective-permute-start | bytes 835592 | tf_op jit(solution)/shard_map/ppermute | solution.py:234
  21.3 0.0 copy-start.5
  21.3 0.0 copy-start.6
  21.3 1.3 %collective-permute-start.1 = (f32[68,8,128]{2,1,0:T(8,128)S(1)}, f32[68,8,128]{2,1,0:T(8,128)S(1)}, u32[]{:S(2)}, u32[]{:S(2)}) collective-permute-start(f32[68,8,128]{2,1,0:T(8,128)S(1)} %get-tuple-element.7), channel_id=1, source_target_pairs={{4,0},{8,4},{12,8},{16,12},{20,16},{24,20},{28,24},{5,1},{9,5},{13... | collective-permute-start | bytes 835592 | tf_op jit(solution)/shard_map/ppermute | solution.py:234
  22.6 0.0 copy-done.7
  22.6 0.1 copy.10.filter_coeffs
  22.7 10.9 %collective-permute-done.from_before = f32[68,8,128]{2,1,0:T(8,128)S(1)} collective-permute-done((f32[68,8,128]{2,1,0:T(8,128)S(1)}, f32[68,8,128]{2,1,0:T(8,128)S(1)}, u32[]{:S(2)}, u32[]{:S(2)}) %collective-permute-start) | collective-permute-done | bytes 278560 | tf_op jit(solution)/shard_map/ppermute | solution.py:234
  33.7 0.0 collective-permute-done.1.from_after
  33.7 0.0 copy-done.1
  33.7 0.0 copy-done.3
  33.7 0.0 copy-done.5
  33.7 0.0 copy-done.6
  33.7 14.2 %migrate.1 = (f32[4,2,24,256]{3,2,1,0:T(8,128)}, f32[2,2,24,1024]{3,2,1,0:T(8,128)}) custom-call(s32[8]{0:T(128)S(1)} %copy-done.4, f32[2]{0:T(128)S(1)} %copy-done.6, s32[2,2]{1,0:T(2,128)S(1)} %copy-done.5, f32[2,5,3]{2,1,0:T(8,128)S(1)} %copy.10.filter_coeffs, f32[2,2,24,1024]{3,2,1,0:T(8,128)S(1)} %copy-done.1, f32[2,2,24,1024]{3,2,1,0:T(8,128)S(1)} %copy-done.3, ...), custom_call_target="tpu_custom_call" | custom-call | tf_op jit(solution)/shard_map/migrate/pallas_call | solution.py:254
  47.9 0.0 reduce-scatter.2.cloned.1.call-update
  47.9 22.0 %reduce-scatter.2.cloned.1.call-done = f32[1,2,24,256]{3,2,1,0:T(8,128)} async-done(((f32[4,2,24,256]{3,2,1,0:T(8,128)}), f32[1,2,24,256]{3,2,1,0:T(8,128)}) %reduce-scatter.2.cloned.1.call-update) | async-done | bytes 49168 | tf_op jit(solution)/shard_map/reduce_scatter | solution.py:275
  (3 shorter events, 0.0 us)
Async XLA Ops:
  7.2 62.8 %reduce-scatter.2.cloned.1.call-start = ((), (), s32[]{:S(2)}) async-start(), calls=%async_computation.1 | async-start | bytes 245760 | tf_op jit(solution)/shard_map/reduce_scatter | solution.py:275
  14.3 0.7 copy-start.4
  14.9 1.0 %copy-start = (f32[2,2,24,1024]{3,2,1,0:T(8,128)S(1)}, f32[2,2,24,1024]{3,2,1,0:T(8,128)}, u32[]{:S(2)}) copy-start(f32[2,2,24,1024]{3,2,1,0:T(8,128)} %source.3) | copy-start | bytes 1179652
  15.9 1.0 %copy-start.2 = (f32[2,2,24,1024]{3,2,1,0:T(8,128)S(1)}, f32[2,2,24,1024]{3,2,1,0:T(8,128)}, u32[]{:S(2)}) copy-start(f32[2,2,24,1024]{3,2,1,0:T(8,128)} %receiver.3) | copy-start | bytes 1179652
  16.9 16.8 %copy-start.1 = (f32[2,2,24,1024]{3,2,1,0:T(8,128)S(1)}, f32[2,2,24,1024]{3,2,1,0:T(8,128)}, u32[]{:S(2)}) copy-start(f32[2,2,24,1024]{3,2,1,0:T(8,128)} %source.3) | copy-start | bytes 1179652
  16.9 16.8 %copy-start.3 = (f32[2,2,24,1024]{3,2,1,0:T(8,128)S(1)}, f32[2,2,24,1024]{3,2,1,0:T(8,128)}, u32[]{:S(2)}) copy-start(f32[2,2,24,1024]{3,2,1,0:T(8,128)} %receiver.3) | copy-start | bytes 1179652
  17.6 5.0 %copy-start.7 = (f32[2,5,3]{1,0,2:T(2,128)S(1)}, f32[2,5,3]{1,0,2:T(2,128)}, u32[]{:S(2)}) copy-start(f32[2,5,3]{1,0,2:T(2,128)} %param.12) | copy-start | bytes 364
  17.6 16.0 %collective-permute-start = (f32[68,8,128]{2,1,0:T(8,128)S(1)}, f32[68,8,128]{2,1,0:T(8,128)S(1)}, u32[]{:S(2)}, u32[]{:S(2)}) collective-permute-start(f32[68,8,128]{2,1,0:T(8,128)S(1)} %get-tuple-element.6), channel_id=1, source_target_pairs={{0,4},{4,8},{8,12},{12,16},{16,20},{20,24},{24,28},{1,5},{5,9},{9,... | collective-permute-start | bytes 835592 | tf_op jit(solution)/shard_map/ppermute | solution.py:234
  21.3 12.4 %copy-start.5 = (s32[2,2]{1,0:T(2,128)S(1)}, s32[2,2]{1,0:T(2,128)}, u32[]{:S(2)}) copy-start(s32[2,2]{1,0:T(2,128)} %order_table.1) | copy-start | bytes 52
  21.3 12.4 %copy-start.6 = (f32[2]{0:T(128)S(1)}, f32[2]{0:T(128)}, u32[]{:S(2)}) copy-start(f32[2]{0:T(128)} %frequency.1) | copy-start | bytes 28
  21.3 12.3 %collective-permute-start.1 = (f32[68,8,128]{2,1,0:T(8,128)S(1)}, f32[68,8,128]{2,1,0:T(8,128)S(1)}, u32[]{:S(2)}, u32[]{:S(2)}) collective-permute-start(f32[68,8,128]{2,1,0:T(8,128)S(1)} %get-tuple-element.7), channel_id=1, source_target_pairs={{4,0},{8,4},{12,8},{16,12},{20,16},{24,20},{28,24},{5,1},{9,5},{13... | collective-permute-start | bytes 835592 | tf_op jit(solution)/shard_map/ppermute | solution.py:234
Sparse Core Ops, SparseCore 0:
  48.0 21.8 reduce-scatter.1

commit v3 on v0

v3 whole, which is shorter than its diff:
```python
from math import comb

import jax
import jax.numpy as jnp
import numpy as np
from jax import lax
from jax.experimental import pallas as pl
from jax.experimental.pallas import tpu as pltpu
from jax.sharding import PartitionSpec as P

ORDER = 4
NDEPTH = 2
HALO = ORDER * NDEPTH
F32 = jnp.float32
BF16 = jnp.bfloat16
VMEM = pl.BlockSpec(memory_space=pltpu.VMEM)
SMEM = pl.BlockSpec(memory_space=pltpu.SMEM)

SHIFTED = ((1,), (-1, 2), (1, -8, 8), (-1, 18, -48, 32), (1, -32, 160, -256, 128))


def y_weights():
    out = np.zeros((256, ORDER * 128), np.float32)

    def add(k, column, sign):
        for m in range(1, ORDER + 1):
            for lane in range(max(0, column - m), min(128, column + m + 1)):
                out[k, (m - 1) * 128 + lane] += sign * comb(2 * m, m + lane - column) / 16.0**m

    for lane in range(128):
        add(lane, lane, 1)
    for lane in range(4):
        add(128 + lane, 128 + lane, 1)
        add(128 + 124 + lane, lane - 4, 1)
    for k in range(3):
        add(128 + 8 + k, -2 - k, -1)
        add(128 + 5 + k, 131 - k, -1)
    return out


def seam(values):
    lane = lax.broadcasted_iota(jnp.int32, (1, 8, 128), 2)
    sub = lax.broadcasted_iota(jnp.int32, (1, 8, 128), 1)
    inner = ((lane < 4) & (sub < 7)) | ((lane >= 124) & (sub > 0))
    edge = ((sub == 0) & (lane >= 8) & (lane <= 10)) | ((sub == 7) & (lane >= 5) & (lane <= 7))
    beside = jnp.where(lane < 64, pltpu.roll(values, 7, 1), pltpu.roll(values, 1, 1))
    return jnp.where(inner, beside, jnp.where(edge, pltpu.roll(values, 8, 2), 0.0))


def y_powers(values, weights):
    rows = values.shape[0]

    def halves(x):
        x = x.reshape(rows * 8, 128)
        high = x.astype(BF16)
        return high, (x - high.astype(F32)).astype(BF16)

    high, low = halves(values)
    seam_high, seam_low = halves(seam(values))
    left = jnp.concatenate([high, seam_high, low, seam_low], axis=1)
    right = jnp.concatenate([weights, weights], axis=0)
    out = jnp.dot(left, right, preferred_element_type=F32)
    return [out[:, m * 128 : (m + 1) * 128].reshape(rows, 8, 128) for m in range(ORDER)]


def to_rows(flat, load_tile, row_tiles):
    for i in range(row_tiles):
        for j in range(8):
            flat[pl.ds((i * 8 + j) * 8, 8), :] = load_tile(i, j)


def row_of(flat, row):
    start = (row // 8) * 64 + row % 8
    return flat[pl.ds(start, 8, stride=8), :]


def planes_of(source, receiver):
    for field in (source, receiver):
        for part in range(2):
            for freq in range(source.shape[1]):
                yield lambda i, j: field[part, freq, pl.ds(8 * i, 8), pl.ds(128 * j, 128)]


def ahead_kernel(aperture, source, receiver, slowness, ahead, slowness_out, *flats):
    width = aperture[lax.axis_index("tile")]
    row_tiles = source.shape[2] // 8
    for plane, load in enumerate(planes_of(source, receiver)):
        to_rows(flats[plane], load, row_tiles)
        for k in range(HALO):
            ahead[plane * HALO + k] = row_of(flats[plane], width - HALO + k)
    slowness_out[...] = slowness[...]


def slow_tile(planes, depth):
    columns = planes.shape[3]
    return lambda i, j: planes[
        128 * j // columns, depth, pl.ds(8 * i, 8), pl.ds(128 * j % columns, 128)
    ]


def behind_kernel(aperture, source, receiver, planes, behind, slow_ahead, *flats):
    width = aperture[lax.axis_index("tile")]
    row_tiles = source.shape[2] // 8
    count = 4 * source.shape[1]
    for plane, load in enumerate(planes_of(source, receiver)):
        to_rows(flats[plane], load, HALO // 8)
        for k in range(HALO):
            behind[plane * HALO + k] = row_of(flats[plane], k)
    to_rows(flats[count], slow_tile(planes, 0), row_tiles)
    for k in range(ORDER):
        slow_ahead[k] = row_of(flats[count], width - ORDER + k)
        behind[count * HALO + k] = row_of(flats[count], k)


def coefficients(weights, freq, slow_row, store):
    powers = weights.shape[1] // (2 * (ORDER + 1))
    for part in range(2 * (ORDER + 1)):
        value = weights[freq, part * powers + powers - 1]
        for power in range(powers - 2, -1, -1):
            value = value * slow_row + weights[freq, part * powers + power]
        store(part, value)


def own_kernel(
    frequency, order_table, filter_coeffs, source, receiver, planes, y_matrix,
    rows_out, powers_out, slow_out, weights_out, later_out, flat, later_weights,
):
    freqs, stored = source.shape[1:3]
    row_tiles = stored // 8
    powers = filter_coeffs.shape[2]
    for plane, load in enumerate(planes_of(source, receiver)):
        to_rows(flat.at[plane % 2], load, row_tiles)
        for r in range(stored):
            rows_out[plane, r] = row_of(flat.at[plane % 2], r)
    for depth in range(NDEPTH):
        to_rows(flat.at[depth], slow_tile(planes, depth), row_tiles)
        for r in range(stored):
            slow_out[depth, r] = row_of(flat.at[depth], r)

    for depth, weights in enumerate((weights_out, later_weights)):
        for freq in range(freqs):
            omega = frequency[freq]
            active = [jnp.where(order_table[depth, freq] >= n, 1.0, 0.0) for n in range(ORDER + 1)]
            for c in range(2):
                scale = None
                for j in range(powers):
                    scaled = [filter_coeffs[c, n, j] * active[n] for n in range(ORDER + 1)]
                    for m in range(ORDER + 1):
                        total = None
                        for n in range(m, ORDER + 1):
                            term = scaled[n] * float(SHIFTED[n][m])
                            total = term if total is None else total + term
                        if scale is not None:
                            total = total * scale
                        weights[freq, (m * 2 + c) * powers + j] = jnp.full((8, 128), total, F32)
                    scale = omega if scale is None else scale * omega

    def later(r, carry):
        for freq in range(freqs):
            def store(part, value):
                later_out[freq, part, r] = value

            coefficients(later_weights, freq, slow_out[1, r], store)
        return carry

    lax.fori_loop(0, stored, later, 0)

    matrix = y_matrix[...]

    def spread(plane, carry):
        for m, value in enumerate(y_powers(rows_out[plane], matrix)):
            powers_out[plane, m] = value
        return carry

    lax.fori_loop(0, 4 * freqs, spread, 0)


def main_kernel(
    aperture, rows_in, powers_in, slow_in, weights, later, y_matrix,
    from_before, slow_before, from_after,
    image_out, receiver_out,
    flat, edges, start, middle, powers, slow, first, images,
):
    tile = lax.axis_index("tile")
    width = aperture[tile]
    count, stored = rows_in.shape[:2]
    freqs = count // 4
    row_tiles = stored // 8
    rows_one = stored + 2 * ORDER
    matrix = y_matrix[...]

    for p in range(count):
        start[p, pl.ds(HALO, stored)] = rows_in[p]
        for m in range(ORDER):
            powers[p, m, pl.ds(HALO, stored)] = powers_in[p, m]
    slow[pl.ds(ORDER, stored)] = slow_in[0]

    @pl.when(tile == 0)
    def _():
        for p in range(count):
            edges[p, HALO - 1] = jnp.zeros((8, 128), F32)
            for k in range(1, HALO):
                edges[p, HALO - 1 - k] = -rows_in[p, k - 1]
        slow[ORDER - 1] = slow_in[0, 0]
        for k in range(1, ORDER):
            slow[ORDER - 1 - k] = slow_in[0, k - 1]

    @pl.when(tile > 0)
    def _():
        for p in range(count):
            edges[p, pl.ds(0, HALO)] = from_before[pl.ds(p * HALO, HALO)]
        slow[pl.ds(0, ORDER)] = slow_before[...]

    @pl.when(tile == lax.axis_size("tile") - 1)
    def _():
        for p in range(count):
            edges[p, HALO] = jnp.zeros((8, 128), F32)
            for k in range(1, HALO):
                edges[p, HALO + k] = -rows_in[p, width - k]
        slow[ORDER + width] = slow_in[0, width - 1]
        for k in range(1, ORDER):
            slow[ORDER + width + k] = slow_in[0, width - k]

    @pl.when(tile < lax.axis_size("tile") - 1)
    def _():
        for p in range(count):
            edges[p, pl.ds(HALO, HALO)] = from_after[pl.ds(p * HALO, HALO)]
        slow[pl.ds(ORDER + width, ORDER)] = from_after[pl.ds(count * HALO, ORDER)]

    def spread_edges(p, carry):
        values = edges[p]
        start[p, pl.ds(0, HALO)] = values[:HALO]
        start[p, pl.ds(HALO + width, HALO)] = values[HALO:]
        for m, value in enumerate(y_powers(values, matrix)):
            powers[p, m, pl.ds(0, HALO)] = value[:HALO]
            powers[p, m, pl.ds(HALO + width, HALO)] = value[HALO:]
        return carry

    lax.fori_loop(0, count, spread_edges, 0)

    def first_row(r, carry):
        for freq in range(freqs):
            def store(part, value):
                first[freq, part, r] = value

            coefficients(weights, freq, slow[r], store)
        return carry

    lax.fori_loop(0, rows_one, first_row, 0)

    def sweep(depth, fields, results, coefs, rows):
        def feed(held, value):
            kept = []
            for last in held:
                kept.append(value)
                value = value + last
            return kept, value

        for freq in range(freqs):
            for field in range(2):
                pair = [(2 * field + part) * freqs + freq for part in range(2)]
                held = []
                for p in pair:
                    for m in range(1, ORDER + 1):
                        chain = []
                        for k in range(2 * m):
                            value = powers[p, m - 1, ORDER - m + k]
                            chain, value = feed(chain, value)
                            chain.append(value)
                        held.append(chain)

                def step(o, held, freq=freq, field=field, pair=pair):
                    totals, kept = [], []
                    for at, p in enumerate(pair):
                        sums = [fields[p, o + ORDER]]
                        for m in range(1, ORDER + 1):
                            chain, value = feed(
                                held[at * ORDER + m - 1], powers[p, m - 1, o + ORDER + m]
                            )
                            kept.append(chain)
                            sums.append(value)
                        totals.append(sums)
                    re = im = None
                    for m in range(ORDER + 1):
                        g_re, g_im = coefs[freq, 2 * m, o], coefs[freq, 2 * m + 1, o]
                        v_re, v_im = totals[0][m], totals[1][m]
                        if field == 0:
                            part_re, part_im = g_re * v_re + g_im * v_im, g_re * v_im - g_im * v_re
                        else:
                            part_re, part_im = g_re * v_re - g_im * v_im, g_re * v_im + g_im * v_re
                        re = part_re if re is None else re + part_re
                        im = part_im if im is None else im + part_im
                    results[pair[0], o] = re
                    results[pair[1], o] = im
                    if field == 1:
                        term = re * results[freq, o] + im * results[freqs + freq, o]
                        images[depth, o] = term if freq == 0 else images[depth, o] + term
                    return kept

                lax.fori_loop(0, rows, step, held, unroll=8)

    sweep(0, start, middle, first, rows_one)

    def spread_middle(p, carry):
        for m, value in enumerate(y_powers(middle[p], matrix)):
            powers[p, m, pl.ds(0, rows_one)] = value
        return carry

    lax.fori_loop(0, count, spread_middle, 0)
    sweep(1, middle, start, later, stored)

    def put(slot, load_row, store_tile):
        for r in range(stored):
            at = (r // 8) * 64 + r % 8
            flat[slot, pl.ds(at, 8, stride=8), :] = jnp.where(r < width, load_row(r), 0.0)
        for i in range(row_tiles):
            for j in range(8):
                store_tile(i, j, flat[slot, pl.ds((i * 8 + j) * 8, 8), :])

    columns = image_out.shape[3]
    for depth in range(NDEPTH):
        def store_image(i, j, value):
            image_out[
                128 * j // columns, depth, pl.ds(8 * i, 8), pl.ds(128 * j % columns, 128)
            ] = value

        put(depth, lambda r: images[depth, r + ORDER * (1 - depth)], store_image)
    for part in range(2):
        for freq in range(freqs):
            def store_receiver(i, j, value):
                receiver_out[part, freq, pl.ds(8 * i, 8), pl.ds(128 * j, 128)] = value

            p = (2 + part) * freqs + freq
            put(p % 2, lambda r: start[p, r], store_receiver)


def passed_along(value, axis, steps):
    count = lax.axis_size(axis)
    initial, last = (max(0, -steps), min(count, count - steps))
    return lax.ppermute(value, axis, [(source, source + steps) for source in range(initial, last)])


def kernel(body, out_shape, in_specs, scratch, name, cost):
    return pl.pallas_call(
        body,
        out_shape=out_shape,
        in_specs=in_specs,
        out_specs=jax.tree.map(lambda _: VMEM, out_shape),
        scratch_shapes=scratch,
        compiler_params=pltpu.CompilerParams(vmem_limit_bytes=28 << 20),
        cost_estimate=pl.CostEstimate(flops=cost, bytes_accessed=cost // 100, transcendentals=0),
        name=name,
    )


def shards(source_field, receiver_field, slowness, frequency, order_table, filter_coeffs, aperture):
    freqs, stored = source_field.shape[1:3]
    count = 4 * freqs
    parts = 2 * (ORDER + 1)
    rows_one, rows_all = stored + 2 * ORDER, stored + 2 * HALO

    def rows(*lead):
        return jax.ShapeDtypeStruct(lead + (8, 128), F32)

    def scratch(*lead):
        return pltpu.VMEM(lead + (8, 128), F32)

    flat = pltpu.VMEM((stored * 8, 128), F32)
    ahead, slowness = kernel(
        ahead_kernel,
        (rows(count * HALO), jax.ShapeDtypeStruct(slowness.shape, F32)),
        [SMEM] + [VMEM] * 3,
        [flat] * count,
        "ahead",
        1 << 20,
    )(aperture, source_field, receiver_field, slowness)
    from_before = passed_along(ahead, "tile", 1)
    planes = lax.all_gather(slowness, "freq", axis=0)
    behind, slow_ahead = kernel(
        behind_kernel,
        (rows(count * HALO + ORDER), rows(ORDER)),
        [SMEM] + [VMEM] * 3,
        [flat] * (count + 1),
        "behind",
        1 << 20,
    )(aperture, source_field, receiver_field, planes)
    from_after = passed_along(behind, "tile", -1)
    slow_before = passed_along(slow_ahead, "tile", 1)

    y_matrix = jnp.asarray(y_weights(), BF16)
    powers = filter_coeffs.shape[2]
    own = kernel(
        own_kernel,
        (
            rows(count, stored),
            rows(count, ORDER, stored),
            rows(NDEPTH, stored),
            rows(freqs, parts * powers),
            rows(freqs, parts, stored),
        ),
        [SMEM] * 3 + [VMEM] * 4,
        [pltpu.VMEM((2, stored * 8, 128), F32), scratch(freqs, parts * powers)],
        "own",
        1 << 30,
    )(frequency, order_table, filter_coeffs, source_field, receiver_field, planes, y_matrix)
    image_parts, receiver_out = kernel(
        main_kernel,
        (
            jax.ShapeDtypeStruct((lax.axis_size("freq"),) + slowness.shape, F32),
            jax.ShapeDtypeStruct(receiver_field.shape, F32),
        ),
        [SMEM] + [VMEM] * 9,
        [
            pltpu.VMEM((2, stored * 8, 128), F32),
            scratch(count, 2 * HALO),
            scratch(count, rows_all),
            scratch(count, rows_one),
            scratch(count, ORDER, rows_all),
            scratch(rows_one),
            scratch(freqs, parts, rows_one),
            scratch(NDEPTH, rows_one),
        ],
        "migrate",
        1 << 30,
    )(aperture, *own, y_matrix, from_before, slow_before, from_after)
    exchanged = lax.all_to_all(image_parts, "freq", 0, 0)
    return jnp.sum(exchanged, axis=0), receiver_out


def solution(mesh):
    placed = (
        P(None, "freq", "tile", None),
        P(None, "freq", "tile", None),
        P(None, "tile", "freq"),
        P("freq"),
        P(None, "freq"),
        P(),
        P(),
    )
    return jax.shard_map(
        shards,
        mesh=mesh,
        in_specs=placed,
        out_specs=(P(None, "tile", "freq"), P(None, "freq", "tile", None)),
        check_vma=False,
    )
```

time: 192 us -> 51.2 us (0.27)
  other arithmetic: 62.5 us -> 0.63 us
  starting transfers between devices: 50.9 us -> 10.4 us
  waiting for transfers between devices: 35.9 us -> 0.01 us
  between operations: 17.7 us -> 0.72 us
  Pallas kernels: 0 us -> 15.7 us
  local copies, waits for them, and re-layouts: 18.2 us -> 8.49 us
  blocking collectives: 5.59 us -> 14.7 us
    add x20 -> x0, other arithmetic: 42.9 us -> none  [the longest x10 39.8 us: weighted(): src_re = coef_re * cheb_term[0, 0] + coef_im * cheb_term[0, 1]]
    ppermute x16 -> x3, starting transfers between devices: 50.9 us -> 10.4 us  [passed_along(): lax.ppermute(value, axis, [(source, source + steps) for source in range(i...]
    psum x1 -> x0, waiting for transfers between devices: 34.8 us -> none  [shards(): summed = lax.psum(stacked, 'freq')]
    pallas_call x0 -> x4, Pallas kernels: none -> 15.7 us  [the longest x1 10.2 us: shards(): kernel(main_kernel, (jax.ShapeDtypeStruct((lax.axis_size('freq'),) + slow...]
    another operation x21 -> x0, other arithmetic: 10.3 us -> none  [the longest x20 9.64 us: weighted(): return jnp.stack([jnp.stack([src_re, src_im]), jnp.stack([rec_re, rec_im])])]
    all_to_all x0 -> x1, blocking collectives: none -> 7.88 us  [shards(): exchanged = lax.all_to_all(image_parts, 'freq', 0, 0)]
    slice x18 -> x0, local copies, waits for them, and re-layouts: 6.63 us -> none  [the longest x8 4.84 us: mcclellan(): padded_cols[..., :-2] + padded_cols[..., 2:]]
    mul x9 -> x0, other arithmetic: 6.35 us -> none  [the longest x6 4.05 us: shards(): following = live_rows * (2.0 * spread - previous)]
  transfers between devices with their start and end apart: 17 -> 3, of which waited for: 2 -> 0; matrix products, arithmetic and copies ran while one was open for 24% -> 2% of each run, Pallas kernels for 0% -> 8%
where the time goes in v3:
time: 51.2 us; the launch traced here: 50.7 us
  Pallas kernels  15.7 us (31%)
  blocking collectives  14.7 us (29%)
  starting transfers between devices  10.4 us (20%)
  local copies, waits for them, and re-layouts  8.49 us (17%)
  between operations  0.72 us (1%)
  other arithmetic  0.63 us (1%)
    ppermute x3, starting transfers between devices, passed_along(): lax.ppermute(value, axis, [(source, source + steps) for source in range(i...  10.4 us
    pallas_call x1, Pallas kernels, shards(): kernel(main_kernel, (jax.ShapeDtypeStruct((lax.axis_size('freq'),) + slow...  10.2 us
    unnamed x21, local copies, waits for them, and re-layouts  8.49 us
    all_to_all x1, blocking collectives, shards(): exchanged = lax.all_to_all(image_parts, 'freq', 0, 0)  7.88 us
    all_gather x1, blocking collectives, shards(): planes = lax.all_gather(slowness, 'freq', axis=0)  6.84 us
    pallas_call x1, Pallas kernels, shards(): kernel(own_kernel, (rows(count, stored), rows(count, ORDER, stored), rows...  4.22 us
  transfers between devices with their start and end apart: 3, of which 0 were waited for; matrix products, arithmetic and copies ran while one was open for 2% of the time, Pallas kernels for 8%

profile of v3, /device:TPU:0, one launch (start us, length us, event | category | flops | bytes accessed | tf_op | source)
XLA Modules:
  0.0 50.7 jit_solution(906765333643476675)
XLA Ops:
  0.6 0.0 copy-start
  0.6 1.0 %copy-done = f32[2,2,24,1024]{3,2,1,0:T(8,128)S(1)} copy-done((f32[2,2,24,1024]{3,2,1,0:T(8,128)S(1)}, f32[2,2,24,1024]{3,2,1,0:T(8,128)}, u32[]{:S(2)}) %copy-start) | copy-done | bytes 393240
  1.6 1.0 %copy-done.2 = f32[2,2,24,1024]{3,2,1,0:T(8,128)S(1)} copy-done((f32[2,2,24,1024]{3,2,1,0:T(8,128)S(1)}, f32[2,2,24,1024]{3,2,1,0:T(8,128)}, u32[]{:S(2)}) %copy-start.2) | copy-done | bytes 393240
  2.6 0.8 %copy-done.5 = f32[2,24,256]{2,1,0:T(8,128)S(1)} copy-done((f32[2,24,256]{2,1,0:T(8,128)S(1)}, f32[2,24,256]{2,1,0:T(8,128)}, u32[]{:S(2)}) %copy-start.5) | copy-done | bytes 49176
  3.4 0.7 %copy-done.6 = s32[8]{0:T(128)S(1)} copy-done((s32[8]{0:T(128)S(1)}, s32[8]{0:T(128)}, u32[]{:S(2)}) %copy-start.6) | copy-done | bytes 56
  4.1 0.7 %ahead.1 = (f32[64,8,128]{2,1,0:T(8,128)S(1)}, f32[2,24,256]{2,1,0:T(8,128)S(1)}) custom-call(s32[8]{0:T(128)S(1)} %copy-done.6, f32[2,2,24,1024]{3,2,1,0:T(8,128)S(1)} %copy-done, f32[2,2,24,1024]{3,2,1,0:T(8,128)S(1)} %copy-done.2, f32[2,24,256]{2,1,0:T(8,128)S(1)} %copy-done.5), custom_call_target="tpu_custom_call" | custom-call | flops 1048576 | bytes 10485 | tf_op jit(solution)/shard_map/ahead/pallas_call | solution.py:369
  4.8 6.8 %all-gather = f32[8,24,256]{2,1,0:T(8,128)S(1)} all-gather(f32[2,24,256]{2,1,0:T(8,128)S(1)} %get-tuple-element.13), channel_id=2, replica_groups=mesh['tile'=8,'freq'=4] {'freq'}, dimensions={0}, use_global_device_ids=true | all-gather | bytes 245760 | tf_op jit(solution)/shard_map/all_gather | solution.py:378
  11.6 0.6 %behind.1 = (f32[68,8,128]{2,1,0:T(8,128)S(1)}, f32[4,8,128]{2,1,0:T(8,128)S(1)}) custom-call(s32[8]{0:T(128)S(1)} %copy-done.6, f32[2,2,24,1024]{3,2,1,0:T(8,128)S(1)} %copy-done, f32[2,2,24,1024]{3,2,1,0:T(8,128)S(1)} %copy-done.2, f32[4,2,24,256]{3,2,1,0:T(8,128)S(1)} %bitcast.1), custom_call_target="tpu_custom_call" | custom-call | flops 1048576 | bytes 10485 | tf_op jit(solution)/shard_map/behind/pallas_call | solution.py:379
  12.2 1.3 %collective-permute-start.2 = (f32[68,8,128]{2,1,0:T(8,128)S(1)}, f32[68,8,128]{2,1,0:T(8,128)S(1)}, u32[]{:S(2)}, u32[]{:S(2)}) collective-permute-start(f32[68,8,128]{2,1,0:T(8,128)S(1)} %get-tuple-element.21), channel_id=1, source_target_pairs={{4,0},{8,4},{12,8},{16,12},{20,16},{24,20},{28,24},{5,1},{9,5},{13... | collective-permute-start | bytes 835592 | tf_op jit(solution)/shard_map/ppermute | solution.py:340
  13.5 4.6 %collective-permute-start = (f32[64,8,128]{2,1,0:T(8,128)S(1)}, f32[64,8,128]{2,1,0:T(8,128)S(1)}, u32[]{:S(2)}, u32[]{:S(2)}) collective-permute-start(f32[64,8,128]{2,1,0:T(8,128)S(1)} %get-tuple-element.19), channel_id=1, source_target_pairs={{0,4},{4,8},{8,12},{12,16},{16,20},{20,24},{24,28},{1,5},{5,9},{9,... | collective-permute-start | bytes 786440 | tf_op jit(solution)/shard_map/ppermute | solution.py:340
  18.1 4.5 %collective-permute-start.1 = (f32[4,8,128]{2,1,0:T(8,128)S(1)}, f32[4,8,128]{2,1,0:T(8,128)S(1)}, u32[]{:S(2)}, u32[]{:S(2)}) collective-permute-start(f32[4,8,128]{2,1,0:T(8,128)S(1)} %get-tuple-element.20), channel_id=1, source_target_pairs={{0,4},{4,8},{8,12},{12,16},{16,20},{20,24},{24,28},{1,5},{5,9},{9,... | collective-permute-start | bytes 49160 | tf_op jit(solution)/shard_map/ppermute | solution.py:340
  22.6 0.8 %copy.11.filter_coeffs = f32[2,5,3]{2,1,0:T(8,128)S(1)} copy(f32[2,5,3]{1,0,2:T(2,128)} %param.13) | data formatting | bytes 240 | tf_op args[5]
  23.4 1.0 %copy-done.1 = f32[2,2,24,1024]{3,2,1,0:T(8,128)S(1)} copy-done((f32[2,2,24,1024]{3,2,1,0:T(8,128)S(1)}, f32[2,2,24,1024]{3,2,1,0:T(8,128)}, u32[]{:S(2)}) %copy-start.1) | copy-done | bytes 393240
  24.4 1.0 %copy-done.3 = f32[2,2,24,1024]{3,2,1,0:T(8,128)S(1)} copy-done((f32[2,2,24,1024]{3,2,1,0:T(8,128)S(1)}, f32[2,2,24,1024]{3,2,1,0:T(8,128)}, u32[]{:S(2)}) %copy-start.3) | copy-done | bytes 393240
  25.4 0.9 %copy-done.4 = bf16[256,512]{1,0:T(8,128)(2,1)S(1)} copy-done((bf16[256,512]{1,0:T(8,128)(2,1)S(1)}, bf16[256,512]{1,0:T(8,128)(2,1)}, u32[]{:S(2)}) %copy-start.4) | copy-done | bytes 262168
  26.4 0.7 %copy-done.8 = s32[2,2]{1,0:T(2,128)S(1)} copy-done((s32[2,2]{1,0:T(2,128)S(1)}, s32[2,2]{1,0:T(2,128)}, u32[]{:S(2)}) %copy-start.8) | copy-done | bytes 40
  27.0 0.7 %copy-done.9 = f32[2]{0:T(128)S(1)} copy-done((f32[2]{0:T(128)S(1)}, f32[2]{0:T(128)}, u32[]{:S(2)}) %copy-start.9) | copy-done | bytes 32
  27.7 4.2 %own.1 = (f32[8,24,8,128]{3,2,1,0:T(8,128)S(1)}, f32[8,4,24,8,128]{4,3,2,1,0:T(8,128)S(1)}, f32[2,24,8,128]{3,2,1,0:T(8,128)S(1)}, f32[2,30,8,128]{3,2,1,0:T(8,128)S(1)}, f32[2,10,24,8,128]{4,3,2,1,0:T(8,128)S(1)}) custom-call(f32[2]{0:T(128)S(1)} %copy-done.9, s32[2,2]{1,0:T(2,128)S(1)} %copy-done.8, f32[2,5,3]{2,1,0:T(8,128)S(1)} %copy.11.filter_coeffs, ...), custom_call_target="tpu_custom_call" | custom-call | flops 1073741824 | bytes 10737418 | tf_op jit(solution)/shard_map/own/pallas_call | solution.py:392
  31.9 0.0 collective-permute-done.1.slow_before
  31.9 0.0 collective-permute-done.from_before
  31.9 0.0 collective-permute-done.2.from_after
  32.0 10.2 %migrate.1 = (f32[4,2,24,256]{3,2,1,0:T(8,128)S(1)}, f32[2,2,24,1024]{3,2,1,0:T(8,128)}) custom-call(s32[8]{0:T(128)S(1)} %copy-done.7, f32[8,24,8,128]{3,2,1,0:T(8,128)S(1)} %get-tuple-element.14.rows_in, f32[8,4,24,8,128]{4,3,2,1,0:T(8,128)S(1)} %get-tuple-element.15.powers_in, f32[2,24,8,128]{3,2,1,0:T(8,128)S(1)} %get-tuple-element.16.slow_in, ...), custom_call_target="tpu_custom_call" | custom-call | flops 1073741824 | bytes 10737418 | tf_op jit(solution)/shard_map/migrate/pallas_call | solution.py:406
  42.2 7.9 %all_to_all.5 = f32[4,2,24,256]{3,2,1,0:T(8,128)S(1)} all-to-all(f32[4,2,24,256]{3,2,1,0:T(8,128)S(1)} %get-tuple-element.22), channel_id=1, replica_groups=mesh['tile'=8,'freq'=4] {'freq'}, dimensions={0} | all-to-all | bytes 393216 | tf_op jit(solution)/shard_map/all_to_all | solution.py:426
  50.1 0.6 %reduce_sum.9 = f32[2,24,256]{2,1,0:T(8,128)} reduce(f32[4,2,24,256]{3,2,1,0:T(8,128)S(1)} %all_to_all.5, f32[]{:T(128)} %constant.1.clone.1), dimensions={0}, to_apply=%region_0.0 | reduce | flops 36864 | bytes 245764 | tf_op jit(solution)/shard_map/reduce_sum | solution.py:427
  (10 shorter events, 0.0 us)
Async XLA Ops:
  0.6 1.0 %copy-start = (f32[2,2,24,1024]{3,2,1,0:T(8,128)S(1)}, f32[2,2,24,1024]{3,2,1,0:T(8,128)}, u32[]{:S(2)}) copy-start(f32[2,2,24,1024]{3,2,1,0:T(8,128)} %source.5) | copy-start | bytes 1179652
  1.6 1.0 %copy-start.2 = (f32[2,2,24,1024]{3,2,1,0:T(8,128)S(1)}, f32[2,2,24,1024]{3,2,1,0:T(8,128)}, u32[]{:S(2)}) copy-start(f32[2,2,24,1024]{3,2,1,0:T(8,128)} %receiver.5) | copy-start | bytes 1179652
  2.6 0.8 %copy-start.5 = (f32[2,24,256]{2,1,0:T(8,128)S(1)}, f32[2,24,256]{2,1,0:T(8,128)}, u32[]{:S(2)}) copy-start(f32[2,24,256]{2,1,0:T(8,128)} %slowness.1) | copy-start | bytes 147460
  3.4 0.7 %copy-start.6 = (s32[8]{0:T(128)S(1)}, s32[8]{0:T(128)}, u32[]{:S(2)}) copy-start(s32[8]{0:T(128)} %aperture.5) | copy-start | bytes 100
  4.1 27.9 %copy-start.7 = (s32[8]{0:T(128)S(1)}, s32[8]{0:T(128)}, u32[]{:S(2)}) copy-start(s32[8]{0:T(128)} %aperture.5) | copy-start | bytes 100
  12.2 19.7 %collective-permute-start.2 = (f32[68,8,128]{2,1,0:T(8,128)S(1)}, f32[68,8,128]{2,1,0:T(8,128)S(1)}, u32[]{:S(2)}, u32[]{:S(2)}) collective-permute-start(f32[68,8,128]{2,1,0:T(8,128)S(1)} %get-tuple-element.21), channel_id=1, source_target_pairs={{4,0},{8,4},{12,8},{16,12},{20,16},{24,20},{28,24},{5,1},{9,5},{13... | collective-permute-start | bytes 835592 | tf_op jit(solution)/shard_map/ppermute | solution.py:340
  13.5 18.4 %collective-permute-start = (f32[64,8,128]{2,1,0:T(8,128)S(1)}, f32[64,8,128]{2,1,0:T(8,128)S(1)}, u32[]{:S(2)}, u32[]{:S(2)}) collective-permute-start(f32[64,8,128]{2,1,0:T(8,128)S(1)} %get-tuple-element.19), channel_id=1, source_target_pairs={{0,4},{4,8},{8,12},{12,16},{16,20},{20,24},{24,28},{1,5},{5,9},{9,... | collective-permute-start | bytes 786440 | tf_op jit(solution)/shard_map/ppermute | solution.py:340
  18.1 13.8 %collective-permute-start.1 = (f32[4,8,128]{2,1,0:T(8,128)S(1)}, f32[4,8,128]{2,1,0:T(8,128)S(1)}, u32[]{:S(2)}, u32[]{:S(2)}) collective-permute-start(f32[4,8,128]{2,1,0:T(8,128)S(1)} %get-tuple-element.20), channel_id=1, source_target_pairs={{0,4},{4,8},{8,12},{12,16},{16,20},{20,24},{24,28},{1,5},{5,9},{9,... | collective-permute-start | bytes 49160 | tf_op jit(solution)/shard_map/ppermute | solution.py:340
  23.4 1.0 %copy-start.1 = (f32[2,2,24,1024]{3,2,1,0:T(8,128)S(1)}, f32[2,2,24,1024]{3,2,1,0:T(8,128)}, u32[]{:S(2)}) copy-start(f32[2,2,24,1024]{3,2,1,0:T(8,128)} %source.5) | copy-start | bytes 1179652
  24.4 1.0 %copy-start.3 = (f32[2,2,24,1024]{3,2,1,0:T(8,128)S(1)}, f32[2,2,24,1024]{3,2,1,0:T(8,128)}, u32[]{:S(2)}) copy-start(f32[2,2,24,1024]{3,2,1,0:T(8,128)} %receiver.5) | copy-start | bytes 1179652
  25.4 0.9 %copy-start.4 = (bf16[256,512]{1,0:T(8,128)(2,1)S(1)}, bf16[256,512]{1,0:T(8,128)(2,1)}, u32[]{:S(2)}) copy-start(bf16[256,512]{1,0:T(8,128)(2,1)} %constant.4.clone.y_matrix) | copy-start | bytes 786436
  26.4 0.7 %copy-start.8 = (s32[2,2]{1,0:T(2,128)S(1)}, s32[2,2]{1,0:T(2,128)}, u32[]{:S(2)}) copy-start(s32[2,2]{1,0:T(2,128)} %order_table.1) | copy-start | bytes 52
  27.0 0.7 %copy-start.9 = (f32[2]{0:T(128)S(1)}, f32[2]{0:T(128)}, u32[]{:S(2)}) copy-start(f32[2]{0:T(128)} %frequency.1) | copy-start | bytes 28

commit v4 on v3

v4 whole, which is shorter than its diff:
```python
from math import comb

import jax
import jax.numpy as jnp
import numpy as np
from jax import lax
from jax.experimental import pallas as pl
from jax.experimental.pallas import tpu as pltpu
from jax.sharding import PartitionSpec as P

ORDER = 4
NDEPTH = 2
HALO = ORDER * NDEPTH
F32 = jnp.float32
BF16 = jnp.bfloat16
VMEM = pl.BlockSpec(memory_space=pltpu.VMEM)
HBM = pl.BlockSpec(memory_space=pltpu.HBM)

SHIFTED = ((1,), (-1, 2), (1, -8, 8), (-1, 18, -48, 32), (1, -32, 160, -256, 128))


def y_weights():
    out = np.zeros((256, ORDER * 128), np.float32)

    def add(k, column, sign):
        for m in range(1, ORDER + 1):
            for lane in range(max(0, column - m), min(128, column + m + 1)):
                out[k, (m - 1) * 128 + lane] += sign * comb(2 * m, m + lane - column) / 16.0**m

    for lane in range(128):
        add(lane, lane, 1)
    for lane in range(4):
        add(128 + lane, 128 + lane, 1)
        add(128 + 124 + lane, lane - 4, 1)
    for k in range(3):
        add(128 + 8 + k, -2 - k, -1)
        add(128 + 5 + k, 131 - k, -1)
    return out


def seam(values):
    lane = lax.broadcasted_iota(jnp.int32, (1, 8, 128), 2)
    sub = lax.broadcasted_iota(jnp.int32, (1, 8, 128), 1)
    inner = ((lane < 4) & (sub < 7)) | ((lane >= 124) & (sub > 0))
    edge = ((sub == 0) & (lane >= 8) & (lane <= 10)) | ((sub == 7) & (lane >= 5) & (lane <= 7))
    beside = jnp.where(lane < 64, pltpu.roll(values, 7, 1), pltpu.roll(values, 1, 1))
    return jnp.where(inner, beside, jnp.where(edge, pltpu.roll(values, 8, 2), 0.0))


def split_rows(values, left, at):
    rows = values.shape[0]
    for column, x in enumerate((values, seam(values))):
        x = x.reshape(rows * 8, 128)
        high = x.astype(BF16)
        left[pl.ds(at, rows * 8), pl.ds(128 * column, 128)] = high
        left[pl.ds(at, rows * 8), pl.ds(256 + 128 * column, 128)] = (x - high.astype(F32)).astype(BF16)


def multiply(left, rows, y_matrix):
    matrix = y_matrix[...]
    right = jnp.concatenate([matrix, matrix], axis=0)
    return jnp.dot(left[pl.ds(0, rows), :], right, preferred_element_type=F32)


def fetch(sems, *pairs):
    copies = [pltpu.make_async_copy(a, b, sems.at[k]) for k, (a, b) in enumerate(pairs)]
    for copy in copies:
        copy.start()
    for copy in copies:
        copy.wait()


def to_rows(flat, load_tile, row_tiles):
    for i in range(row_tiles):
        for j in range(8):
            flat[pl.ds((i * 8 + j) * 8, 8), :] = load_tile(i, j)


def row_of(flat, row):
    start = (row // 8) * 64 + row % 8
    return flat[pl.ds(start, 8, stride=8), :]


def planes_of(source, receiver):
    for field in (source, receiver):
        for part in range(2):
            for freq in range(source.shape[1]):
                yield lambda i, j: field[part, freq, pl.ds(8 * i, 8), pl.ds(128 * j, 128)]


def ahead_kernel(
    aperture_hbm, source_hbm, receiver_hbm, slowness_hbm, ahead, slowness_out,
    aperture, source, receiver, sems, *flats,
):
    fetch(
        sems,
        (aperture_hbm, aperture),
        (source_hbm, source),
        (receiver_hbm, receiver),
        (slowness_hbm, slowness_out),
    )
    width = aperture[lax.axis_index("tile")]
    row_tiles = source.shape[2] // 8
    for plane, load in enumerate(planes_of(source, receiver)):
        to_rows(flats[plane], load, row_tiles)
        for k in range(HALO):
            ahead[plane * HALO + k] = row_of(flats[plane], width - HALO + k)


def slow_tile(planes, depth):
    columns = planes.shape[3]
    return lambda i, j: planes[
        128 * j // columns, depth, pl.ds(8 * i, 8), pl.ds(128 * j % columns, 128)
    ]


def behind_kernel(
    aperture_hbm, source_hbm, receiver_hbm, planes, behind, slow_ahead,
    aperture, source, receiver, sems, *flats,
):
    top = pl.ds(0, HALO)
    fetch(
        sems,
        (aperture_hbm, aperture),
        (source_hbm.at[:, :, top, :], source),
        (receiver_hbm.at[:, :, top, :], receiver),
    )
    width = aperture[lax.axis_index("tile")]
    count = 4 * source.shape[1]
    for plane, load in enumerate(planes_of(source, receiver)):
        to_rows(flats[plane], load, HALO // 8)
        for k in range(HALO):
            behind[plane * HALO + k] = row_of(flats[plane], k)
    to_rows(flats[count], slow_tile(planes, 0), planes.shape[2] // 8)
    for k in range(ORDER):
        slow_ahead[k] = row_of(flats[count], width - ORDER + k)
        behind[count * HALO + k] = row_of(flats[count], k)


def coefficients(weights, freq, slow_row, store):
    powers = weights.shape[1] // (2 * (ORDER + 1))
    for part in range(2 * (ORDER + 1)):
        value = weights[freq, part * powers + powers - 1]
        for power in range(powers - 2, -1, -1):
            value = value * slow_row + weights[freq, part * powers + power]
        store(part, value)


def own_kernel(
    frequency_hbm, order_hbm, coeffs_hbm, source_hbm, receiver_hbm, planes, y_matrix_hbm,
    rows_out, powers_out, slow_out, weights_out, later_out,
    frequency, order_table, filter_coeffs, source, receiver, y_matrix, sems,
    flat, left, later_weights,
):
    fetch(
        sems,
        (frequency_hbm, frequency),
        (order_hbm, order_table),
        (coeffs_hbm, filter_coeffs),
        (source_hbm, source),
        (receiver_hbm, receiver),
        (y_matrix_hbm, y_matrix),
    )
    freqs, stored = source.shape[1:3]
    row_tiles = stored // 8
    powers = filter_coeffs.shape[0]
    for plane, load in enumerate(planes_of(source, receiver)):
        to_rows(flat.at[plane], load, row_tiles)
        for r in range(stored):
            rows_out[plane, r] = row_of(flat.at[plane], r)
    for plane in range(4 * freqs):
        split_rows(rows_out[plane], left, plane * stored * 8)
    powers_out[...] = multiply(left, 4 * freqs * stored * 8, y_matrix)

    for depth in range(NDEPTH):
        to_rows(flat.at[depth], slow_tile(planes, depth), row_tiles)
        for r in range(stored):
            slow_out[depth, r] = row_of(flat.at[depth], r)

    for depth, weights in enumerate((weights_out, later_weights)):
        for freq in range(freqs):
            omega = jnp.full((8, 128), frequency[freq], F32)
            active = [
                jnp.full((8, 128), jnp.where(order_table[depth, freq] >= n, 1.0, 0.0), F32)
                for n in range(ORDER + 1)
            ]
            for c in range(2):
                scale = None
                for j in range(powers):
                    scaled = [filter_coeffs[j, c, n] * active[n] for n in range(ORDER + 1)]
                    for m in range(ORDER + 1):
                        total = None
                        for n in range(m, ORDER + 1):
                            term = scaled[n] * float(SHIFTED[n][m])
                            total = term if total is None else total + term
                        if scale is not None:
                            total = total * scale
                        weights[freq, (m * 2 + c) * powers + j] = total
                    scale = omega if scale is None else scale * omega

    def later(r, carry):
        for freq in range(freqs):
            def store(part, value):
                later_out[freq, part, r] = value

            coefficients(later_weights, freq, slow_out[1, r], store)
        return carry

    lax.fori_loop(0, stored, later, 0, unroll=4)


def main_kernel(
    aperture_hbm, rows_in, powers_in, slow_in, weights, later, y_matrix_hbm,
    from_before, slow_before, from_after,
    image_out, receiver_out,
    aperture, y_matrix, sems,
    flat, edges, start, middle, left, powers, slow, first, images, partial,
):
    fetch(sems, (aperture_hbm, aperture), (y_matrix_hbm, y_matrix))
    tile = lax.axis_index("tile")
    width = aperture[tile]
    count, stored = rows_in.shape[:2]
    freqs = count // 4
    row_tiles = stored // 8
    rows_one = stored + 2 * ORDER

    for p in range(count):
        start[p, pl.ds(HALO, stored)] = rows_in[p]
        powers[p, pl.ds(8 * HALO, 8 * stored), :] = powers_in[pl.ds(p * stored * 8, stored * 8), :]
    slow[pl.ds(ORDER, stored)] = slow_in[0]

    @pl.when(tile == 0)
    def _():
        for p in range(count):
            edges[p, HALO - 1] = jnp.zeros((8, 128), F32)
            for k in range(1, HALO):
                edges[p, HALO - 1 - k] = -rows_in[p, k - 1]
        slow[ORDER - 1] = slow_in[0, 0]
        for k in range(1, ORDER):
            slow[ORDER - 1 - k] = slow_in[0, k - 1]

    @pl.when(tile > 0)
    def _():
        for p in range(count):
            edges[p, pl.ds(0, HALO)] = from_before[pl.ds(p * HALO, HALO)]
        slow[pl.ds(0, ORDER)] = slow_before[...]

    @pl.when(tile == lax.axis_size("tile") - 1)
    def _():
        for p in range(count):
            edges[p, HALO] = jnp.zeros((8, 128), F32)
            for k in range(1, HALO):
                edges[p, HALO + k] = -rows_in[p, width - k]
        slow[ORDER + width] = slow_in[0, width - 1]
        for k in range(1, ORDER):
            slow[ORDER + width + k] = slow_in[0, width - k]

    @pl.when(tile < lax.axis_size("tile") - 1)
    def _():
        for p in range(count):
            edges[p, pl.ds(HALO, HALO)] = from_after[pl.ds(p * HALO, HALO)]
        slow[pl.ds(ORDER + width, ORDER)] = from_after[pl.ds(count * HALO, ORDER)]

    for p in range(count):
        values = edges[p]
        start[p, pl.ds(0, HALO)] = values[:HALO]
        start[p, pl.ds(HALO + width, HALO)] = values[HALO:]
        split_rows(values, left, p * 2 * HALO * 8)
    product = multiply(left, count * 2 * HALO * 8, y_matrix)
    after = pl.multiple_of(8 * (HALO + width), 8)
    for p in range(count):
        at = p * 2 * HALO * 8
        powers[p, pl.ds(0, 8 * HALO), :] = product[at : at + 8 * HALO]
        powers[p, pl.ds(after, 8 * HALO), :] = product[at + 8 * HALO : at + 16 * HALO]

    def first_row(r, carry):
        for freq in range(freqs):
            def store(part, value):
                first[freq, part, r] = value

            coefficients(weights, freq, slow[r], store)
        return carry

    lax.fori_loop(0, rows_one, first_row, 0, unroll=4)

    def sweep(depth, fields, results, coefs, rows):
        def feed(held, value):
            kept = []
            for last in held:
                kept.append(value)
                value = value + last
            return kept, value

        def power(p, m, row):
            return powers[p, pl.ds(pl.multiple_of(8 * row, 8), 8), pl.ds(128 * (m - 1), 128)]

        for freq in range(freqs):
            for field in range(2):
                for part in range(2):
                    p = (2 * field + part) * freqs + freq
                    held = []
                    for m in range(1, ORDER + 1):
                        chain = []
                        for k in range(2 * m):
                            value = power(p, m, ORDER - m + k)
                            chain, value = feed(chain, value)
                            chain.append(value)
                        held.append(chain)

                    def step(o, held, freq=freq, field=field, part=part, p=p):
                        kept, by_re, by_im = [], None, None
                        for m in range(ORDER + 1):
                            if m == 0:
                                value = fields[p, o + ORDER]
                            else:
                                chain, value = feed(held[m - 1], power(p, m, o + ORDER + m))
                                kept.append(chain)
                            re = coefs[freq, 2 * m, o] * value
                            im = coefs[freq, 2 * m + 1, o] * value
                            by_re = re if by_re is None else by_re + re
                            by_im = im if by_im is None else by_im + im
                        if part == 0:
                            partial[0, o] = by_re
                            partial[1, o] = by_im
                            return kept
                        if field == 0:
                            re, im = partial[0, o] + by_im, by_re - partial[1, o]
                        else:
                            re, im = partial[0, o] - by_im, by_re + partial[1, o]
                            term = re * results[freq, o] + im * results[freqs + freq, o]
                            images[depth, o] = term if freq == 0 else images[depth, o] + term
                        results[p - freqs, o] = re
                        results[p, o] = im
                        return kept

                    lax.fori_loop(0, rows, step, held, unroll=8)

    sweep(0, start, middle, first, rows_one)

    for p in range(count):
        split_rows(middle[p], left, p * rows_one * 8)
    product = multiply(left, count * rows_one * 8, y_matrix)
    for p in range(count):
        at = p * rows_one * 8
        powers[p, pl.ds(0, 8 * rows_one), :] = product[at : at + 8 * rows_one]
    sweep(1, middle, start, later, stored)

    def put(slot, load_row, store_tile):
        for r in range(stored):
            at = (r // 8) * 64 + r % 8
            flat[slot, pl.ds(at, 8, stride=8), :] = jnp.where(r < width, load_row(r), 0.0)
        for i in range(row_tiles):
            for j in range(8):
                store_tile(i, j, flat[slot, pl.ds((i * 8 + j) * 8, 8), :])

    columns = image_out.shape[3]
    for depth in range(NDEPTH):
        def store_image(i, j, value):
            image_out[
                128 * j // columns, depth, pl.ds(8 * i, 8), pl.ds(128 * j % columns, 128)
            ] = value

        put(depth, lambda r: images[depth, r + ORDER * (1 - depth)], store_image)
    for part in range(2):
        for freq in range(freqs):
            def store_receiver(i, j, value):
                receiver_out[part, freq, pl.ds(8 * i, 8), pl.ds(128 * j, 128)] = value

            p = (2 + part) * freqs + freq
            put(p % 2, lambda r: start[p, r], store_receiver)


def passed_along(value, axis, steps):
    count = lax.axis_size(axis)
    initial, last = (max(0, -steps), min(count, count - steps))
    return lax.ppermute(value, axis, [(source, source + steps) for source in range(initial, last)])


def kernel(body, out_shape, in_specs, scratch, name):
    return pl.pallas_call(
        body,
        out_shape=out_shape,
        in_specs=in_specs,
        out_specs=jax.tree.map(lambda _: VMEM, out_shape),
        scratch_shapes=scratch,
        compiler_params=pltpu.CompilerParams(vmem_limit_bytes=32 << 20),
        cost_estimate=pl.CostEstimate(flops=1000, bytes_accessed=1000, transcendentals=0),
        name=name,
    )


def shards(source_field, receiver_field, slowness, frequency, order_table, filter_coeffs, aperture):
    freqs, stored = source_field.shape[1:3]
    count = 4 * freqs
    parts = 2 * (ORDER + 1)
    rows_one, rows_all = stored + 2 * ORDER, stored + 2 * HALO

    def rows(*lead):
        return jax.ShapeDtypeStruct(lead + (8, 128), F32)

    def scratch(*lead):
        return pltpu.VMEM(lead + (8, 128), F32)

    def same(value):
        return pltpu.VMEM(value.shape, value.dtype)

    def scalars(value):
        return pltpu.SMEM(value.shape, value.dtype)

    flat = pltpu.VMEM((stored * 8, 128), F32)
    ahead, slowness = kernel(
        ahead_kernel,
        (rows(count * HALO), jax.ShapeDtypeStruct(slowness.shape, F32)),
        [HBM] * 4,
        [scalars(aperture), same(source_field), same(receiver_field), pltpu.SemaphoreType.DMA((4,))]
        + [flat] * count,
        "ahead",
    )(aperture, source_field, receiver_field, slowness)
    from_before = passed_along(ahead, "tile", 1)
    planes = lax.all_gather(slowness, "freq", axis=0)
    top = pltpu.VMEM(source_field.shape[:2] + (HALO,) + source_field.shape[3:], F32)
    behind, slow_ahead = kernel(
        behind_kernel,
        (rows(count * HALO + ORDER), rows(ORDER)),
        [HBM] * 3 + [VMEM],
        [scalars(aperture), top, top, pltpu.SemaphoreType.DMA((3,))] + [flat] * (count + 1),
        "behind",
    )(aperture, source_field, receiver_field, planes)
    from_after = passed_along(behind, "tile", -1)
    slow_before = passed_along(slow_ahead, "tile", 1)

    y_matrix = jnp.asarray(y_weights(), BF16)
    coeffs = jnp.transpose(filter_coeffs, (2, 0, 1))
    powers = coeffs.shape[0]
    own = kernel(
        own_kernel,
        (
            rows(count, stored),
            jax.ShapeDtypeStruct((count * stored * 8, ORDER * 128), F32),
            rows(NDEPTH, stored),
            rows(freqs, parts * powers),
            rows(freqs, parts, stored),
        ),
        [HBM] * 5 + [VMEM, HBM],
        [
            scalars(frequency),
            scalars(order_table),
            scalars(coeffs),
            same(source_field),
            same(receiver_field),
            same(y_matrix),
            pltpu.SemaphoreType.DMA((6,)),
            pltpu.VMEM((count, stored * 8, 128), F32),
            pltpu.VMEM((count * stored * 8, 512), BF16),
            scratch(freqs, parts * powers),
        ],
        "own",
    )(frequency, order_table, coeffs, source_field, receiver_field, planes, y_matrix)
    image_parts, receiver_out = kernel(
        main_kernel,
        (
            jax.ShapeDtypeStruct((lax.axis_size("freq"),) + slowness.shape, F32),
            jax.ShapeDtypeStruct(receiver_field.shape, F32),
        ),
        [HBM] + [VMEM] * 5 + [HBM] + [VMEM] * 3,
        [
            scalars(aperture),
            same(y_matrix),
            pltpu.SemaphoreType.DMA((2,)),
            pltpu.VMEM((2, stored * 8, 128), F32),
            scratch(count, 2 * HALO),
            scratch(count, rows_all),
            scratch(count, rows_one),
            pltpu.VMEM((count * rows_one * 8, 512), BF16),
            pltpu.VMEM((count, rows_all * 8, ORDER * 128), F32),
            scratch(rows_one),
            scratch(freqs, parts, rows_one),
            scratch(NDEPTH, rows_one),
            scratch(2, rows_one),
        ],
        "migrate",
    )(aperture, *own, y_matrix, from_before, slow_before, from_after)
    exchanged = lax.all_to_all(image_parts, "freq", 0, 0)
    return jnp.sum(exchanged, axis=0), receiver_out


def solution(mesh):
    placed = (
        P(None, "freq", "tile", None),
        P(None, "freq", "tile", None),
        P(None, "tile", "freq"),
        P("freq"),
        P(None, "freq"),
        P(),
        P(),
    )
    return jax.shard_map(
        shards,
        mesh=mesh,
        in_specs=placed,
        out_specs=(P(None, "tile", "freq"), P(None, "freq", "tile", None)),
        check_vma=False,
    )
```

time: 51.2 us -> 46.7 us (0.912)
  Pallas kernels: 15.7 us -> 11.2 us
    pallas_call x1, Pallas kernels: 10.2 us -> 7.61 us  [shards(): kernel(main_kernel, (jax.ShapeDtypeStruct((lax.axis_size('freq'),) + slow...]
    pallas_call x2, Pallas kernels: 4.84 us -> 2.91 us  [the longest x1 2.26 us: shards(): kernel(own_kernel, (rows(count, stored), jax.ShapeDtypeStruct((count * st...]
    unnamed x21 -> x24, local copies, waits for them, and re-layouts: 8.49 us -> 8.4 us
  transfers between devices with their start and end apart: 3 -> 3, of which waited for: 0 -> 0; matrix products, arithmetic and copies ran while one was open for 2% -> 0% of each run, Pallas kernels for 8% -> 5%
where the time goes in v4:
time: 46.7 us; the launch traced here: 46.1 us
  blocking collectives  14.7 us (31%)
  Pallas kernels  11.2 us (24%)
  starting transfers between devices  10.4 us (22%)
  local copies, waits for them, and re-layouts  8.4 us (18%)
  between operations  0.75 us (2%)
  other arithmetic  0.63 us (1%)
    ppermute x3, starting transfers between devices, passed_along(): lax.ppermute(value, axis, [(source, source + steps) for source in range(i...  10.4 us
    unnamed x24, local copies, waits for them, and re-layouts  8.4 us
    all_to_all x1, blocking collectives, shards(): exchanged = lax.all_to_all(image_parts, 'freq', 0, 0)  7.9 us
    pallas_call x1, Pallas kernels, shards(): kernel(main_kernel, (jax.ShapeDtypeStruct((lax.axis_size('freq'),) + slow...  7.61 us
    all_gather x1, blocking collectives, shards(): planes = lax.all_gather(slowness, 'freq', axis=0)  6.84 us
    pallas_call x1, Pallas kernels, shards(): kernel(own_kernel, (rows(count, stored), jax.ShapeDtypeStruct((count * st...  2.26 us
  transfers between devices with their start and end apart: 3, of which 0 were waited for; matrix products, arithmetic and copies ran while one was open for 0% of the time, Pallas kernels for 5%

profile of v4, /device:TPU:0, one launch (start us, length us, event | category | flops | bytes accessed | tf_op | source)
XLA Modules:
  0.0 46.1 jit_solution(15438221594750690012)
XLA Ops:
  0.6 0.0 copy-start
  0.6 1.0 %copy-done = f32[2,2,24,1024]{3,2,1,0:T(8,128)S(1)} copy-done((f32[2,2,24,1024]{3,2,1,0:T(8,128)S(1)}, f32[2,2,24,1024]{3,2,1,0:T(8,128)}, u32[]{:S(2)}) %copy-start) | copy-done | bytes 393240
  1.6 1.0 %copy-done.2 = f32[2,2,24,1024]{3,2,1,0:T(8,128)S(1)} copy-done((f32[2,2,24,1024]{3,2,1,0:T(8,128)S(1)}, f32[2,2,24,1024]{3,2,1,0:T(8,128)}, u32[]{:S(2)}) %copy-start.2) | copy-done | bytes 393240
  2.6 0.8 %copy-done.6 = f32[2,24,256]{2,1,0:T(8,128)S(1)} copy-done((f32[2,24,256]{2,1,0:T(8,128)S(1)}, f32[2,24,256]{2,1,0:T(8,128)}, u32[]{:S(2)}) %copy-start.6) | copy-done | bytes 49176
  3.4 0.7 %copy-done.7 = s32[8]{0:T(128)S(1)} copy-done((s32[8]{0:T(128)S(1)}, s32[8]{0:T(128)}, u32[]{:S(2)}) %copy-start.7) | copy-done | bytes 56
  4.1 0.7 %ahead.1 = (f32[64,8,128]{2,1,0:T(8,128)S(1)}, f32[2,24,256]{2,1,0:T(8,128)S(1)}) custom-call(s32[8]{0:T(128)S(1)} %copy-done.7, f32[2,2,24,1024]{3,2,1,0:T(8,128)S(1)} %copy-done, f32[2,2,24,1024]{3,2,1,0:T(8,128)S(1)} %copy-done.2, f32[2,24,256]{2,1,0:T(8,128)S(1)} %copy-done.6), custom_call_target="tpu_custom_call" | custom-call | flops 1000 | bytes 1000 | tf_op jit(solution)/shard_map/ahead/pallas_call | solution.py:411
  4.8 6.8 %all-gather = f32[8,24,256]{2,1,0:T(8,128)S(1)} all-gather(f32[2,24,256]{2,1,0:T(8,128)S(1)} %get-tuple-element.13), channel_id=2, replica_groups=mesh['tile'=8,'freq'=4] {'freq'}, dimensions={0}, use_global_device_ids=true | all-gather | bytes 245760 | tf_op jit(solution)/shard_map/all_gather | solution.py:420
  11.6 0.7 %behind.1 = (f32[68,8,128]{2,1,0:T(8,128)S(1)}, f32[4,8,128]{2,1,0:T(8,128)S(1)}) custom-call(s32[8]{0:T(128)S(1)} %copy-done.7, f32[2,2,24,1024]{3,2,1,0:T(8,128)S(1)} %copy-done, f32[2,2,24,1024]{3,2,1,0:T(8,128)S(1)} %copy-done.2, f32[4,2,24,256]{3,2,1,0:T(8,128)S(1)} %bitcast.2), custom_call_target="tpu_custom_call" | custom-call | flops 1000 | bytes 1000 | tf_op jit(solution)/shard_map/behind/pallas_call | solution.py:422
  12.3 1.3 %collective-permute-start.2 = (f32[68,8,128]{2,1,0:T(8,128)S(1)}, f32[68,8,128]{2,1,0:T(8,128)S(1)}, u32[]{:S(2)}, u32[]{:S(2)}) collective-permute-start(f32[68,8,128]{2,1,0:T(8,128)S(1)} %get-tuple-element.21), channel_id=1, source_target_pairs={{4,0},{8,4},{12,8},{16,12},{20,16},{24,20},{28,24},{5,1},{9,5},{13... | collective-permute-start | bytes 835592 | tf_op jit(solution)/shard_map/ppermute | solution.py:376
  13.6 4.6 %collective-permute-start = (f32[64,8,128]{2,1,0:T(8,128)S(1)}, f32[64,8,128]{2,1,0:T(8,128)S(1)}, u32[]{:S(2)}, u32[]{:S(2)}) collective-permute-start(f32[64,8,128]{2,1,0:T(8,128)S(1)} %get-tuple-element.19), channel_id=1, source_target_pairs={{0,4},{4,8},{8,12},{12,16},{16,20},{20,24},{24,28},{1,5},{5,9},{9,... | collective-permute-start | bytes 786440 | tf_op jit(solution)/shard_map/ppermute | solution.py:376
  18.2 4.5 %collective-permute-start.1 = (f32[4,8,128]{2,1,0:T(8,128)S(1)}, f32[4,8,128]{2,1,0:T(8,128)S(1)}, u32[]{:S(2)}, u32[]{:S(2)}) collective-permute-start(f32[4,8,128]{2,1,0:T(8,128)S(1)} %get-tuple-element.20), channel_id=1, source_target_pairs={{0,4},{4,8},{8,12},{12,16},{16,20},{20,24},{24,28},{1,5},{5,9},{9,... | collective-permute-start | bytes 49160 | tf_op jit(solution)/shard_map/ppermute | solution.py:376
  22.7 0.0 copy-start.1
  22.7 1.0 %copy-done.1 = f32[2,2,24,1024]{3,2,1,0:T(8,128)S(1)} copy-done((f32[2,2,24,1024]{3,2,1,0:T(8,128)S(1)}, f32[2,2,24,1024]{3,2,1,0:T(8,128)}, u32[]{:S(2)}) %copy-start.1) | copy-done | bytes 393240
  23.7 1.0 %copy-done.3 = f32[2,2,24,1024]{3,2,1,0:T(8,128)S(1)} copy-done((f32[2,2,24,1024]{3,2,1,0:T(8,128)S(1)}, f32[2,2,24,1024]{3,2,1,0:T(8,128)}, u32[]{:S(2)}) %copy-start.3) | copy-done | bytes 393240
  24.7 0.9 %copy-done.4 = bf16[256,512]{1,0:T(8,128)(2,1)S(1)} copy-done((bf16[256,512]{1,0:T(8,128)(2,1)S(1)}, bf16[256,512]{1,0:T(8,128)(2,1)}, u32[]{:S(2)}) %copy-start.4) | copy-done | bytes 262168
  25.6 0.7 %copy-done.9 = f32[2,5,3]{1,0,2:T(2,128)S(1)} copy-done((f32[2,5,3]{1,0,2:T(2,128)S(1)}, f32[2,5,3]{1,0,2:T(2,128)}, u32[]{:S(2)}) %copy-start.9) | copy-done | bytes 144
  26.3 0.7 %copy-done.10 = s32[2,2]{1,0:T(2,128)S(1)} copy-done((s32[2,2]{1,0:T(2,128)S(1)}, s32[2,2]{1,0:T(2,128)}, u32[]{:S(2)}) %copy-start.10) | copy-done | bytes 40
  27.0 0.7 %copy-done.11 = f32[2]{0:T(128)S(1)} copy-done((f32[2]{0:T(128)S(1)}, f32[2]{0:T(128)}, u32[]{:S(2)}) %copy-start.11) | copy-done | bytes 32
  27.7 2.3 %own.1 = (f32[8,24,8,128]{3,2,1,0:T(8,128)S(1)}, f32[1536,512]{1,0:T(8,128)S(1)}, f32[2,24,8,128]{3,2,1,0:T(8,128)S(1)}, f32[2,30,8,128]{3,2,1,0:T(8,128)S(1)}, f32[2,10,24,8,128]{4,3,2,1,0:T(8,128)S(1)}) custom-call(f32[2]{0:T(128)S(1)} %copy-done.11, s32[2,2]{1,0:T(2,128)S(1)} %copy-done.10, f32[3,2,5]{2,1,0:T(2,128)S(1)} %bitcast.4, ...), custom_call_target="tpu_custom_call" | custom-call | flops 1000 | bytes 1000 | tf_op jit(solution)/shard_map/own/pallas_call | solution.py:435
  29.9 0.0 collective-permute-done.1.slow_before
  29.9 0.0 collective-permute-done.from_before
  30.0 7.6 %migrate.1 = (f32[4,2,24,256]{3,2,1,0:T(8,128)S(1)}, f32[2,2,24,1024]{3,2,1,0:T(8,128)}) custom-call(s32[8]{0:T(128)S(1)} %copy-done.8, f32[8,24,8,128]{3,2,1,0:T(8,128)S(1)} %get-tuple-element.14.rows_in, f32[1536,512]{1,0:T(8,128)S(1)} %get-tuple-element.15.powers_in, f32[2,24,8,128]{3,2,1,0:T(8,128)S(1)} %get-tuple-element.16.slow_in, ...), custom_call_target="tpu_custom_call" | custom-call | flops 1000 | bytes 1000 | tf_op jit(solution)/shard_map/migrate/pallas_call | solution.py:459
  37.6 7.9 %all_to_all.5 = f32[4,2,24,256]{3,2,1,0:T(8,128)S(1)} all-to-all(f32[4,2,24,256]{3,2,1,0:T(8,128)S(1)} %get-tuple-element.22), channel_id=1, replica_groups=mesh['tile'=8,'freq'=4] {'freq'}, dimensions={0} | all-to-all | bytes 393216 | tf_op jit(solution)/shard_map/all_to_all | solution.py:483
  45.5 0.6 %reduce_sum.9 = f32[2,24,256]{2,1,0:T(8,128)} reduce(f32[4,2,24,256]{3,2,1,0:T(8,128)S(1)} %all_to_all.5, f32[]{:T(128)} %constant.1.clone.1), dimensions={0}, to_apply=%region_0.0 | reduce | flops 36864 | bytes 245764 | tf_op jit(solution)/shard_map/reduce_sum | solution.py:484
  (13 shorter events, 0.0 us)
Async XLA Ops:
  0.6 1.0 %copy-start = (f32[2,2,24,1024]{3,2,1,0:T(8,128)S(1)}, f32[2,2,24,1024]{3,2,1,0:T(8,128)}, u32[]{:S(2)}) copy-start(f32[2,2,24,1024]{3,2,1,0:T(8,128)} %source_hbm.5) | copy-start | bytes 1179652
  1.6 1.0 %copy-start.2 = (f32[2,2,24,1024]{3,2,1,0:T(8,128)S(1)}, f32[2,2,24,1024]{3,2,1,0:T(8,128)}, u32[]{:S(2)}) copy-start(f32[2,2,24,1024]{3,2,1,0:T(8,128)} %receiver_hbm.5) | copy-start | bytes 1179652
  2.6 0.8 %copy-start.6 = (f32[2,24,256]{2,1,0:T(8,128)S(1)}, f32[2,24,256]{2,1,0:T(8,128)}, u32[]{:S(2)}) copy-start(f32[2,24,256]{2,1,0:T(8,128)} %slowness_hbm.1) | copy-start | bytes 147460
  3.4 0.7 %copy-start.7 = (s32[8]{0:T(128)S(1)}, s32[8]{0:T(128)}, u32[]{:S(2)}) copy-start(s32[8]{0:T(128)} %aperture_hbm.5) | copy-start | bytes 100
  4.1 25.9 %copy-start.5 = (bf16[256,512]{1,0:T(8,128)(2,1)S(1)}, bf16[256,512]{1,0:T(8,128)(2,1)}, u32[]{:S(2)}) copy-start(bf16[256,512]{1,0:T(8,128)(2,1)} %constant.4.clone.y_matrix_hbm) | copy-start | bytes 786436
  4.1 25.9 %copy-start.8 = (s32[8]{0:T(128)S(1)}, s32[8]{0:T(128)}, u32[]{:S(2)}) copy-start(s32[8]{0:T(128)} %aperture_hbm.5) | copy-start | bytes 100
  12.3 17.7 %collective-permute-start.2 = (f32[68,8,128]{2,1,0:T(8,128)S(1)}, f32[68,8,128]{2,1,0:T(8,128)S(1)}, u32[]{:S(2)}, u32[]{:S(2)}) collective-permute-start(f32[68,8,128]{2,1,0:T(8,128)S(1)} %get-tuple-element.21), channel_id=1, source_target_pairs={{4,0},{8,4},{12,8},{16,12},{20,16},{24,20},{28,24},{5,1},{9,5},{13... | collective-permute-start | bytes 835592 | tf_op jit(solution)/shard_map/ppermute | solution.py:376
  13.6 16.4 %collective-permute-start = (f32[64,8,128]{2,1,0:T(8,128)S(1)}, f32[64,8,128]{2,1,0:T(8,128)S(1)}, u32[]{:S(2)}, u32[]{:S(2)}) collective-permute-start(f32[64,8,128]{2,1,0:T(8,128)S(1)} %get-tuple-element.19), channel_id=1, source_target_pairs={{0,4},{4,8},{8,12},{12,16},{16,20},{20,24},{24,28},{1,5},{5,9},{9,... | collective-permute-start | bytes 786440 | tf_op jit(solution)/shard_map/ppermute | solution.py:376
  18.2 11.8 %collective-permute-start.1 = (f32[4,8,128]{2,1,0:T(8,128)S(1)}, f32[4,8,128]{2,1,0:T(8,128)S(1)}, u32[]{:S(2)}, u32[]{:S(2)}) collective-permute-start(f32[4,8,128]{2,1,0:T(8,128)S(1)} %get-tuple-element.20), channel_id=1, source_target_pairs={{0,4},{4,8},{8,12},{12,16},{16,20},{20,24},{24,28},{1,5},{5,9},{9,... | collective-permute-start | bytes 49160 | tf_op jit(solution)/shard_map/ppermute | solution.py:376
  22.7 1.0 %copy-start.1 = (f32[2,2,24,1024]{3,2,1,0:T(8,128)S(1)}, f32[2,2,24,1024]{3,2,1,0:T(8,128)}, u32[]{:S(2)}) copy-start(f32[2,2,24,1024]{3,2,1,0:T(8,128)} %source_hbm.5) | copy-start | bytes 1179652
  23.7 1.0 %copy-start.3 = (f32[2,2,24,1024]{3,2,1,0:T(8,128)S(1)}, f32[2,2,24,1024]{3,2,1,0:T(8,128)}, u32[]{:S(2)}) copy-start(f32[2,2,24,1024]{3,2,1,0:T(8,128)} %receiver_hbm.5) | copy-start | bytes 1179652
  24.7 0.9 %copy-start.4 = (bf16[256,512]{1,0:T(8,128)(2,1)S(1)}, bf16[256,512]{1,0:T(8,128)(2,1)}, u32[]{:S(2)}) copy-start(bf16[256,512]{1,0:T(8,128)(2,1)} %constant.4.clone.y_matrix_hbm) | copy-start | bytes 786436
  25.6 0.7 %copy-start.9 = (f32[2,5,3]{1,0,2:T(2,128)S(1)}, f32[2,5,3]{1,0,2:T(2,128)}, u32[]{:S(2)}) copy-start(f32[2,5,3]{1,0,2:T(2,128)} %param.13) | copy-start | bytes 364
  26.3 0.7 %copy-start.10 = (s32[2,2]{1,0:T(2,128)S(1)}, s32[2,2]{1,0:T(2,128)}, u32[]{:S(2)}) copy-start(s32[2,2]{1,0:T(2,128)} %order_hbm.1) | copy-start | bytes 52
  27.0 0.7 %copy-start.11 = (f32[2]{0:T(128)S(1)}, f32[2]{0:T(128)}, u32[]{:S(2)}) copy-start(f32[2]{0:T(128)} %frequency_hbm.1) | copy-start | bytes 28

commit v5 on v4

--- a/solution.py
+++ b/solution.py
@@ -11,6 +11,7 @@
 ORDER = 4
 NDEPTH = 2
 HALO = ORDER * NDEPTH
+EXTRA = 8
 F32 = jnp.float32
 BF16 = jnp.bfloat16
 VMEM = pl.BlockSpec(memory_space=pltpu.VMEM)
@@ -62,12 +63,20 @@
     return jnp.dot(left[pl.ds(0, rows), :], right, preferred_element_type=F32)
 
 
-def fetch(sems, *pairs):
+def begin(sems, *pairs):
     copies = [pltpu.make_async_copy(a, b, sems.at[k]) for k, (a, b) in enumerate(pairs)]
     for copy in copies:
         copy.start()
+    return copies
+
+
+def finish(copies):
     for copy in copies:
         copy.wait()
+
+
+def fetch(sems, *pairs):
+    finish(begin(sems, *pairs))
 
 
 def to_rows(flat, load_tile, row_tiles):
@@ -89,15 +98,13 @@
 
 
 def ahead_kernel(
-    aperture_hbm, source_hbm, receiver_hbm, slowness_hbm, ahead, slowness_out,
-    aperture, source, receiver, sems, *flats,
+    aperture_hbm, source_hbm, receiver_hbm, ahead, aperture, source, receiver, sems, *flats
 ):
     fetch(
         sems,
         (aperture_hbm, aperture),
         (source_hbm, source),
         (receiver_hbm, receiver),
-        (slowness_hbm, slowness_out),
     )
     width = aperture[lax.axis_index("tile")]
     row_tiles = source.shape[2] // 8
@@ -105,6 +112,8 @@
         to_rows(flats[plane], load, row_tiles)
         for k in range(HALO):
             ahead[plane * HALO + k] = row_of(flats[plane], width - HALO + k)
+    used = 4 * source.shape[1] * HALO
+    ahead[pl.ds(used, EXTRA)] = jnp.zeros((EXTRA, 8, 128), F32)
 
 
 def slow_tile(planes, depth):
@@ -115,8 +124,8 @@
 
 
 def behind_kernel(
-    aperture_hbm, source_hbm, receiver_hbm, planes, behind, slow_ahead,
-    aperture, source, receiver, sems, *flats,
+    aperture_hbm, source_hbm, receiver_hbm, planes_hbm, behind, slow_ahead,
+    aperture, source, receiver, planes, sems, *flats,
 ):
     top = pl.ds(0, HALO)
     fetch(
@@ -124,6 +133,7 @@
         (aperture_hbm, aperture),
         (source_hbm.at[:, :, top, :], source),
         (receiver_hbm.at[:, :, top, :], receiver),
+        (planes_hbm.at[:, pl.ds(0, 1)], planes),
     )
     width = aperture[lax.axis_index("tile")]
     count = 4 * source.shape[1]
@@ -147,9 +157,10 @@
 
 
 def own_kernel(
-    frequency_hbm, order_hbm, coeffs_hbm, source_hbm, receiver_hbm, planes, y_matrix_hbm,
-    rows_out, powers_out, slow_out, weights_out, later_out,
-    frequency, order_table, filter_coeffs, source, receiver, y_matrix, sems,
+    frequency_hbm, order_hbm, coeffs_hbm, source_hbm, receiver_hbm, planes_hbm, y_matrix_hbm,
+    rows_hbm, powers_hbm, slow_hbm, weights_hbm, later_hbm,
+    frequency, order_table, filter_coeffs, source, receiver, planes, y_matrix,
+    rows_out, powers_out, slow_out, weights_out, later_out, sems, sent,
     flat, left, later_weights,
 ):
     fetch(
@@ -159,6 +170,7 @@
         (coeffs_hbm, filter_coeffs),
         (source_hbm, source),
         (receiver_hbm, receiver),
+        (planes_hbm, planes),
         (y_matrix_hbm, y_matrix),
     )
     freqs, stored = source.shape[1:3]
@@ -168,9 +180,12 @@
         to_rows(flat.at[plane], load, row_tiles)
         for r in range(stored):
             rows_out[plane, r] = row_of(flat.at[plane], r)
+    copies = begin(sent.at[pl.ds(0, 1)], (rows_out, rows_hbm))
     for plane in range(4 * freqs):
         split_rows(rows_out[plane], left, plane * stored * 8)
-    powers_out[...] = multiply(left, 4 * freqs * stored * 8, y_matrix)
+    product = multiply(left, 4 * freqs * stored * 8, y_matrix)
+    powers_out[...] = product.reshape(powers_out.shape)
+    copies += begin(sent.at[pl.ds(1, 1)], (powers_out, powers_hbm))
 
     for depth in range(NDEPTH):
         to_rows(flat.at[depth], slow_tile(planes, depth), row_tiles)
@@ -207,37 +222,53 @@
         return carry
 
     lax.fori_loop(0, stored, later, 0, unroll=4)
+    copies += begin(
+        sent.at[pl.ds(2, 3)],
+        (slow_out, slow_hbm),
+        (weights_out, weights_hbm),
+        (later_out, later_hbm),
+    )
+    finish(copies)
 
 
 def main_kernel(
-    aperture_hbm, rows_in, powers_in, slow_in, weights, later, y_matrix_hbm,
-    from_before, slow_before, from_after,
+    aperture_hbm, rows_hbm, powers_hbm, slow_hbm, weights_hbm, later_hbm, y_matrix_hbm,
+    before_hbm, slow_before_hbm, after_hbm,
     image_out, receiver_out,
-    aperture, y_matrix, sems,
-    flat, edges, start, middle, left, powers, slow, first, images, partial,
+    aperture, weights, later, y_matrix, from_before, from_after, sems,
+    flat, edges, start, middle, left, powers, slow, slow_before, first, images, partial,
 ):
-    fetch(sems, (aperture_hbm, aperture), (y_matrix_hbm, y_matrix))
-    tile = lax.axis_index("tile")
-    width = aperture[tile]
-    count, stored = rows_in.shape[:2]
+    count, stored = rows_hbm.shape[:2]
     freqs = count // 4
     row_tiles = stored // 8
     rows_one = stored + 2 * ORDER
 
-    for p in range(count):
-        start[p, pl.ds(HALO, stored)] = rows_in[p]
-        powers[p, pl.ds(8 * HALO, 8 * stored), :] = powers_in[pl.ds(p * stored * 8, stored * 8), :]
-    slow[pl.ds(ORDER, stored)] = slow_in[0]
+    copies = begin(
+        sems,
+        (aperture_hbm, aperture),
+        (before_hbm.at[pl.ds(0, count * HALO)], from_before),
+        (after_hbm, from_after),
+        (slow_before_hbm, slow_before),
+        (rows_hbm, start.at[:, pl.ds(HALO, stored)]),
+        (slow_hbm.at[0], slow.at[pl.ds(ORDER, stored)]),
+        (y_matrix_hbm, y_matrix),
+        (weights_hbm, weights),
+        (powers_hbm, powers.at[:, pl.ds(8 * HALO, 8 * stored), :]),
+        (later_hbm, later),
+    )
+    finish(copies[:8])
+    tile = lax.axis_index("tile")
+    width = aperture[tile]
 
     @pl.when(tile == 0)
     def _():
         for p in range(count):
             edges[p, HALO - 1] = jnp.zeros((8, 128), F32)
             for k in range(1, HALO):
-                edges[p, HALO - 1 - k] = -rows_in[p, k - 1]
-        slow[ORDER - 1] = slow_in[0, 0]
+                edges[p, HALO - 1 - k] = -start[p, HALO + k - 1]
+        slow[ORDER - 1] = slow[ORDER]
         for k in range(1, ORDER):
-            slow[ORDER - 1 - k] = slow_in[0, k - 1]
+            slow[ORDER - 1 - k] = slow[ORDER + k - 1]
 
     @pl.when(tile > 0)
     def _():
@@ -250,10 +281,10 @@
         for p in range(count):
             edges[p, HALO] = jnp.zeros((8, 128), F32)
             for k in range(1, HALO):
-                edges[p, HALO + k] = -rows_in[p, width - k]
-        slow[ORDER + width] = slow_in[0, width - 1]
+                edges[p, HALO + k] = -start[p, HALO + width - k]
+        slow[ORDER + width] = slow[ORDER + width - 1]
         for k in range(1, ORDER):
-            slow[ORDER + width + k] = slow_in[0, width - k]
+            slow[ORDER + width + k] = slow[ORDER + width - k]
 
     @pl.when(tile < lax.axis_size("tile") - 1)
     def _():
@@ -267,6 +298,7 @@
         start[p, pl.ds(HALO + width, HALO)] = values[HALO:]
         split_rows(values, left, p * 2 * HALO * 8)
     product = multiply(left, count * 2 * HALO * 8, y_matrix)
+    finish(copies[8:])
     after = pl.multiple_of(8 * (HALO + width), 8)
     for p in range(count):
         at = p * 2 * HALO * 8
@@ -376,17 +408,17 @@
     return lax.ppermute(value, axis, [(source, source + steps) for source in range(initial, last)])
 
 
-def kernel(body, out_shape, in_specs, scratch, name):
+def kernel(body, out_shape, out_specs, operands, scratch, name):
     return pl.pallas_call(
         body,
         out_shape=out_shape,
-        in_specs=in_specs,
-        out_specs=jax.tree.map(lambda _: VMEM, out_shape),
+        in_specs=[HBM] * len(operands),
+        out_specs=out_specs,
         scratch_shapes=scratch,
-        compiler_params=pltpu.CompilerParams(vmem_limit_bytes=32 << 20),
+        compiler_params=pltpu.CompilerParams(vmem_limit_bytes=60 << 20),
         cost_estimate=pl.CostEstimate(flops=1000, bytes_accessed=1000, transcendentals=0),
         name=name,
-    )
+    )(*operands)
 
 
 def shards(source_field, receiver_field, slowness, frequency, order_table, filter_coeffs, aperture):
@@ -395,78 +427,89 @@
     parts = 2 * (ORDER + 1)
     rows_one, rows_all = stored + 2 * ORDER, stored + 2 * HALO
 
+    def shape(*dims):
+        return jax.ShapeDtypeStruct(dims, F32)
+
     def rows(*lead):
-        return jax.ShapeDtypeStruct(lead + (8, 128), F32)
-
-    def scratch(*lead):
-        return pltpu.VMEM(lead + (8, 128), F32)
+        return shape(*lead, 8, 128)
 
     def same(value):
         return pltpu.VMEM(value.shape, value.dtype)
 
+    def scratch(*lead):
+        return same(rows(*lead))
+
     def scalars(value):
         return pltpu.SMEM(value.shape, value.dtype)
 
+    def copies(number):
+        return pltpu.SemaphoreType.DMA((number,))
+
     flat = pltpu.VMEM((stored * 8, 128), F32)
-    ahead, slowness = kernel(
+    ahead = kernel(
         ahead_kernel,
-        (rows(count * HALO), jax.ShapeDtypeStruct(slowness.shape, F32)),
-        [HBM] * 4,
-        [scalars(aperture), same(source_field), same(receiver_field), pltpu.SemaphoreType.DMA((4,))]
-        + [flat] * count,
+        rows(count * HALO + EXTRA),
+        VMEM,
+        (aperture, source_field, receiver_field),
+        [scalars(aperture), same(source_field), same(receiver_field), copies(3)] + [flat] * count,
         "ahead",
-    )(aperture, source_field, receiver_field, slowness)
+    )
     from_before = passed_along(ahead, "tile", 1)
     planes = lax.all_gather(slowness, "freq", axis=0)
     top = pltpu.VMEM(source_field.shape[:2] + (HALO,) + source_field.shape[3:], F32)
     behind, slow_ahead = kernel(
         behind_kernel,
         (rows(count * HALO + ORDER), rows(ORDER)),
-        [HBM] * 3 + [VMEM],
-        [scalars(aperture), top, top, pltpu.SemaphoreType.DMA((3,))] + [flat] * (count + 1),
+        (VMEM, VMEM),
+        (aperture, source_field, receiver_field, planes),
+        [scalars(aperture), top, top, pltpu.VMEM((planes.shape[0], 1) + planes.shape[2:], F32)]
+        + [copies(4)]
+        + [flat] * (count + 1),
         "behind",
-    )(aperture, source_field, receiver_field, planes)
+    )
     from_after = passed_along(behind, "tile", -1)
     slow_before = passed_along(slow_ahead, "tile", 1)
 
     y_matrix = jnp.asarray(y_weights(), BF16)
     coeffs = jnp.transpose(filter_coeffs, (2, 0, 1))
-    powers = coeffs.shape[0]
+    weights = parts * coeffs.shape[0]
+    results = (
+        rows(count, stored),
+        shape(count, stored * 8, ORDER * 128),
+        rows(NDEPTH, stored),
+        rows(freqs, weights),
+        rows(freqs, parts, stored),
+    )
+    tables = (frequency, order_table, coeffs)
+    arrays = (source_field, receiver_field, planes, y_matrix)
     own = kernel(
         own_kernel,
-        (
-            rows(count, stored),
-            jax.ShapeDtypeStruct((count * stored * 8, ORDER * 128), F32),
-            rows(NDEPTH, stored),
-            rows(freqs, parts * powers),
-            rows(freqs, parts, stored),
-        ),
-        [HBM] * 5 + [VMEM, HBM],
-        [
-            scalars(frequency),
-            scalars(order_table),
-            scalars(coeffs),
-            same(source_field),
-            same(receiver_field),
-            same(y_matrix),
-            pltpu.SemaphoreType.DMA((6,)),
+        results,
+        (HBM,) * len(results),
+        tables + arrays,
+        [scalars(value) for value in tables]
+        + [same(value) for value in arrays + results]
+        + [copies(len(tables + arrays)), copies(len(results))]
+        + [
             pltpu.VMEM((count, stored * 8, 128), F32),
             pltpu.VMEM((count * stored * 8, 512), BF16),
-            scratch(freqs, parts * powers),
+            scratch(freqs, weights),
         ],
         "own",
-    )(frequency, order_table, coeffs, source_field, receiver_field, planes, y_matrix)
+    )
     image_parts, receiver_out = kernel(
         main_kernel,
-        (
-            jax.ShapeDtypeStruct((lax.axis_size("freq"),) + slowness.shape, F32),
-            jax.ShapeDtypeStruct(receiver_field.shape, F32),
-        ),
-        [HBM] + [VMEM] * 5 + [HBM] + [VMEM] * 3,
+        (shape(lax.axis_size("freq"), *slowness.shape), shape(*receiver_field.shape)),
+        (VMEM, VMEM),
+        (aperture, *own, y_matrix, from_before, slow_before, from_after),
         [
             scalars(aperture),
+            scratch(freqs, weights),
+            scratch(freqs, parts, stored),
             same(y_matrix),
-            pltpu.SemaphoreType.DMA((2,)),
+            scratch(count * HALO),
+            same(from_after),
+            copies(10),
             pltpu.VMEM((2, stored * 8, 128), F32),
             scratch(count, 2 * HALO),
             scratch(count, rows_all),
@@ -474,12 +517,13 @@
             pltpu.VMEM((count * rows_one * 8, 512), BF16),
             pltpu.VMEM((count, rows_all * 8, ORDER * 128), F32),
             scratch(rows_one),
+            scratch(ORDER),
             scratch(freqs, parts, rows_one),
             scratch(NDEPTH, rows_one),
             scratch(2, rows_one),
         ],
         "migrate",
-    )(aperture, *own, y_matrix, from_before, slow_before, from_after)
+    )
     exchanged = lax.all_to_all(image_parts, "freq", 0, 0)
     return jnp.sum(exchanged, axis=0), receiver_out
 

time: 46.7 us -> 47.5 us (1.017)
  local copies, waits for them, and re-layouts: 8.4 us -> 0.81 us
  Pallas kernels: 11.2 us -> 18 us
  blocking collectives: 14.7 us -> 15.8 us
    unnamed x24 -> x6, local copies, waits for them, and re-layouts: 8.4 us -> 0.81 us
    pallas_call x4, Pallas kernels: 11.2 us -> 18 us  [kernel(): pl.pallas_call(body, out_shape=out_shape, in_specs=[HBM] * len(operands),...]
    all_to_all x1, blocking collectives: 7.9 us -> 8.68 us  [shards(): exchanged = lax.all_to_all(image_parts, 'freq', 0, 0)]
  transfers between devices with their start and end apart: 3 -> 3, of which waited for: 0 -> 1; matrix products, arithmetic and copies ran while one was open for 0% -> 0% of each run, Pallas kernels for 5% -> 15%
where the time goes in v5:
time: 47.5 us; the launch traced here: 47.1 us
  Pallas kernels  18 us (38%)
  blocking collectives  15.8 us (33%)
  starting transfers between devices  10.7 us (23%)
  local copies, waits for them, and re-layouts  0.81 us (2%)
  between operations  0.7 us (1%)
  other arithmetic  0.63 us (1%)
    pallas_call x4, Pallas kernels, kernel(): pl.pallas_call(body, out_shape=out_shape, in_specs=[HBM] * len(operands),...  18 us
    ppermute x3, starting transfers between devices, passed_along(): lax.ppermute(value, axis, [(source, source + steps) for source in range(i...  10.7 us
    all_to_all x1, blocking collectives, shards(): exchanged = lax.all_to_all(image_parts, 'freq', 0, 0)  8.68 us
    all_gather x1, blocking collectives, shards(): planes = lax.all_gather(slowness, 'freq', axis=0)  7.14 us
  transfers between devices with their start and end apart: 3, of which 1 were waited for; matrix products, arithmetic and copies ran while one was open for 0% of the time, Pallas kernels for 15%

profile of v5, /device:TPU:0, one launch (start us, length us, event | category | flops | bytes accessed | tf_op | source)
XLA Modules:
  0.0 47.1 jit_solution(9326411084819207851)
XLA Ops:
  0.6 2.0 %ahead.1 = f32[72,8,128]{2,1,0:T(8,128)} custom-call(s32[8]{0:T(128)} %aperture_hbm.5, f32[2,2,24,1024]{3,2,1,0:T(8,128)} %source_hbm.5, f32[2,2,24,1024]{3,2,1,0:T(8,128)} %receiver_hbm.5), custom_call_target="tpu_custom_call" | custom-call | flops 1000 | bytes 1000 | tf_op jit(solution)/shard_map/ahead/pallas_call | solution.py:412
  2.6 4.9 %collective-permute-start = (f32[72,8,128]{2,1,0:T(8,128)}, f32[72,8,128]{2,1,0:T(8,128)S(1)}, u32[]{:S(2)}, u32[]{:S(2)}) collective-permute-start(f32[72,8,128]{2,1,0:T(8,128)} %ahead.1), channel_id=1, source_target_pairs={{0,4},{4,8},{8,12},{12,16},{16,20},{20,24},{24,28},{1,5},{5,9},{9,... | collective-permute-start | bytes 884744 | tf_op jit(solution)/shard_map/ppermute | solution.py:408
  7.5 7.1 %all-gather = f32[8,24,256]{2,1,0:T(8,128)} all-gather(f32[2,24,256]{2,1,0:T(8,128)} %param.10), channel_id=2, replica_groups=mesh['tile'=8,'freq'=4] {'freq'}, dimensions={0}, use_global_device_ids=true | all-gather | bytes 245760 | tf_op jit(solution)/shard_map/all_gather | solution.py:458
  14.7 1.9 %behind.1 = (f32[68,8,128]{2,1,0:T(8,128)}, f32[4,8,128]{2,1,0:T(8,128)}) custom-call(s32[8]{0:T(128)} %aperture_hbm.5, f32[2,2,24,1024]{3,2,1,0:T(8,128)} %source_hbm.5, f32[2,2,24,1024]{3,2,1,0:T(8,128)} %receiver_hbm.5, f32[4,2,24,256]{3,2,1,0:T(8,128)} %bitcast.2), custom_call_target="tpu_custom_call" | custom-call | flops 1000 | bytes 1000 | tf_op jit(solution)/shard_map/behind/pallas_call | solution.py:412
  16.5 1.3 %collective-permute-start.2 = (f32[68,8,128]{2,1,0:T(8,128)}, f32[68,8,128]{2,1,0:T(8,128)S(1)}, u32[]{:S(2)}, u32[]{:S(2)}) collective-permute-start(f32[68,8,128]{2,1,0:T(8,128)} %get-tuple-element.17), channel_id=1, source_target_pairs={{4,0},{8,4},{12,8},{16,12},{20,16},{24,20},{28,24},{5,1},{9,5},{13... | collective-permute-start | bytes 835592 | tf_op jit(solution)/shard_map/ppermute | solution.py:408
  17.8 4.5 %collective-permute-start.1 = (f32[4,8,128]{2,1,0:T(8,128)}, f32[4,8,128]{2,1,0:T(8,128)S(1)}, u32[]{:S(2)}, u32[]{:S(2)}) collective-permute-start(f32[4,8,128]{2,1,0:T(8,128)} %get-tuple-element.16), channel_id=1, source_target_pairs={{0,4},{4,8},{8,12},{12,16},{16,20},{20,24},{24,28},{1,5},{5,9},{9,... | collective-permute-start | bytes 49160 | tf_op jit(solution)/shard_map/ppermute | solution.py:408
  22.4 5.0 %own.1 = (f32[8,24,8,128]{3,2,1,0:T(8,128)}, f32[8,192,512]{2,1,0:T(8,128)}, f32[2,24,8,128]{3,2,1,0:T(8,128)}, f32[2,30,8,128]{3,2,1,0:T(8,128)}, f32[2,10,24,8,128]{4,3,2,1,0:T(8,128)}) custom-call(f32[2]{0:T(128)} %frequency_hbm.1, s32[2,2]{1,0:T(2,128)} %order_hbm.1, f32[3,2,5]{2,1,0:T(2,128)} %bitcast.4, f32[2,2,24,1024]{3,2,1,0:T(8,128)} %source_hbm.5, ...), custom_call_target="tpu_custom_call" | custom-call | flops 1000 | bytes 1000 | tf_op jit(solution)/shard_map/own/pallas_call | solution.py:412
  27.4 0.5 collective-permute-done.1.slow_before_hbm
  27.8 0.0 copy-start.2
  27.8 0.0 collective-permute-done.2.after_hbm
  27.8 0.0 copy-start.1
  27.8 0.0 collective-permute-done.before_hbm
  27.8 0.0 copy-start
  27.9 0.6 %copy-done.2 = f32[4,8,128]{2,1,0:T(8,128)} copy-done((f32[4,8,128]{2,1,0:T(8,128)}, f32[4,8,128]{2,1,0:T(8,128)S(1)}, u32[]{:S(2)}) %copy-start.2) | copy-done | bytes 16408
  28.4 0.1 copy-done.1
  28.6 0.1 copy-done
  28.7 9.1 %migrate.1 = (f32[4,2,24,256]{3,2,1,0:T(8,128)}, f32[2,2,24,1024]{3,2,1,0:T(8,128)}) custom-call(s32[8]{0:T(128)} %aperture_hbm.5, f32[8,24,8,128]{3,2,1,0:T(8,128)} %get-tuple-element.11.rows_hbm, f32[8,192,512]{2,1,0:T(8,128)} %get-tuple-element.12.powers_hbm, f32[2,24,8,128]{3,2,1,0:T(8,128)} %get-tuple-element.13.slow_hbm, ...), custom_call_target="tpu_custom_call" | custom-call | flops 1000 | bytes 1000 | tf_op jit(solution)/shard_map/migrate/pallas_call | solution.py:412
  37.8 8.7 %all_to_all.5 = f32[4,2,24,256]{3,2,1,0:T(8,128)S(1)} all-to-all(f32[4,2,24,256]{3,2,1,0:T(8,128)} %get-tuple-element.18), channel_id=1, replica_groups=mesh['tile'=8,'freq'=4] {'freq'}, dimensions={0} | all-to-all | bytes 393216 | tf_op jit(solution)/shard_map/all_to_all | solution.py:527
  46.5 0.6 %reduce_sum.9 = f32[2,24,256]{2,1,0:T(8,128)} reduce(f32[4,2,24,256]{3,2,1,0:T(8,128)S(1)} %all_to_all.5, f32[]{:T(128)} %constant.1.clone.1), dimensions={0}, to_apply=%region_0.0 | reduce | flops 36864 | bytes 245764 | tf_op jit(solution)/shard_map/reduce_sum | solution.py:528
Async XLA Ops:
  2.6 25.2 %collective-permute-start = (f32[72,8,128]{2,1,0:T(8,128)}, f32[72,8,128]{2,1,0:T(8,128)S(1)}, u32[]{:S(2)}, u32[]{:S(2)}) collective-permute-start(f32[72,8,128]{2,1,0:T(8,128)} %ahead.1), channel_id=1, source_target_pairs={{0,4},{4,8},{8,12},{12,16},{16,20},{20,24},{24,28},{1,5},{5,9},{9,... | collective-permute-start | bytes 884744 | tf_op jit(solution)/shard_map/ppermute | solution.py:408
  16.5 11.3 %collective-permute-start.2 = (f32[68,8,128]{2,1,0:T(8,128)}, f32[68,8,128]{2,1,0:T(8,128)S(1)}, u32[]{:S(2)}, u32[]{:S(2)}) collective-permute-start(f32[68,8,128]{2,1,0:T(8,128)} %get-tuple-element.17), channel_id=1, source_target_pairs={{4,0},{8,4},{12,8},{16,12},{20,16},{24,20},{28,24},{5,1},{9,5},{13... | collective-permute-start | bytes 835592 | tf_op jit(solution)/shard_map/ppermute | solution.py:408
  17.8 10.0 %collective-permute-start.1 = (f32[4,8,128]{2,1,0:T(8,128)}, f32[4,8,128]{2,1,0:T(8,128)S(1)}, u32[]{:S(2)}, u32[]{:S(2)}) collective-permute-start(f32[4,8,128]{2,1,0:T(8,128)} %get-tuple-element.16), channel_id=1, source_target_pairs={{0,4},{4,8},{8,12},{12,16},{16,20},{20,24},{24,28},{1,5},{5,9},{9,... | collective-permute-start | bytes 49160 | tf_op jit(solution)/shard_map/ppermute | solution.py:408
  27.8 0.6 %copy-start.2 = (f32[4,8,128]{2,1,0:T(8,128)}, f32[4,8,128]{2,1,0:T(8,128)S(1)}, u32[]{:S(2)}) copy-start(f32[4,8,128]{2,1,0:T(8,128)S(1)} %collective-permute-done.1.slow_before_hbm) | copy-start | bytes 49156
  27.8 0.7 %copy-start.1 = (f32[68,8,128]{2,1,0:T(8,128)}, f32[68,8,128]{2,1,0:T(8,128)S(1)}, u32[]{:S(2)}) copy-start(f32[68,8,128]{2,1,0:T(8,128)S(1)} %collective-permute-done.2.after_hbm) | copy-start | bytes 835588
  27.8 0.8 %copy-start = (f32[72,8,128]{2,1,0:T(8,128)}, f32[72,8,128]{2,1,0:T(8,128)S(1)}, u32[]{:S(2)}) copy-start(f32[72,8,128]{2,1,0:T(8,128)S(1)} %collective-permute-done.before_hbm) | copy-start | bytes 884740

commit v6 on v4

v6 whole, which is shorter than its diff:
```python
from math import comb

import jax
import jax.numpy as jnp
import numpy as np
from jax import lax
from jax.experimental import pallas as pl
from jax.experimental.pallas import tpu as pltpu
from jax.sharding import PartitionSpec as P

ORDER = 4
NDEPTH = 2
HALO = ORDER * NDEPTH
F32 = jnp.float32
BF16 = jnp.bfloat16
VMEM = pl.BlockSpec(memory_space=pltpu.VMEM)
HBM = pl.BlockSpec(memory_space=pltpu.HBM)
SMEM = pl.BlockSpec(memory_space=pltpu.SMEM)

SHIFTED = ((1,), (-1, 2), (1, -8, 8), (-1, 18, -48, 32), (1, -32, 160, -256, 128))


def y_weights():
    out = np.zeros((256, ORDER * 128), np.float32)

    def add(k, column, sign):
        for m in range(1, ORDER + 1):
            for lane in range(max(0, column - m), min(128, column + m + 1)):
                out[k, (m - 1) * 128 + lane] += sign * comb(2 * m, m + lane - column) / 16.0**m

    for lane in range(128):
        add(lane, lane, 1)
    for lane in range(4):
        add(128 + lane, 128 + lane, 1)
        add(128 + 124 + lane, lane - 4, 1)
    for k in range(3):
        add(128 + 8 + k, -2 - k, -1)
        add(128 + 5 + k, 131 - k, -1)
    return out


def seam(values):
    lane = lax.broadcasted_iota(jnp.int32, (1, 8, 128), 2)
    sub = lax.broadcasted_iota(jnp.int32, (1, 8, 128), 1)
    inner = ((lane < 4) & (sub < 7)) | ((lane >= 124) & (sub > 0))
    edge = ((sub == 0) & (lane >= 8) & (lane <= 10)) | ((sub == 7) & (lane >= 5) & (lane <= 7))
    beside = jnp.where(lane < 64, pltpu.roll(values, 7, 1), pltpu.roll(values, 1, 1))
    return jnp.where(inner, beside, jnp.where(edge, pltpu.roll(values, 8, 2), 0.0))


def split_rows(values, left, at):
    rows = values.shape[0]
    for column, x in enumerate((values, seam(values))):
        x = x.reshape(rows * 8, 128)
        high = x.astype(BF16)
        left[pl.ds(at, rows * 8), pl.ds(128 * column, 128)] = high
        left[pl.ds(at, rows * 8), pl.ds(256 + 128 * column, 128)] = (x - high.astype(F32)).astype(BF16)


def multiply(left, rows, y_matrix):
    matrix = y_matrix[...]
    right = jnp.concatenate([matrix, matrix], axis=0)
    return jnp.dot(left[pl.ds(0, rows), :], right, preferred_element_type=F32)


def fetch(sems, *pairs):
    copies = [pltpu.make_async_copy(a, b, sems.at[k]) for k, (a, b) in enumerate(pairs)]
    for copy in copies:
        copy.start()
    for copy in copies:
        copy.wait()


def to_rows(flat, load_tile, row_tiles):
    for i in range(row_tiles):
        for j in range(8):
            flat[pl.ds((i * 8 + j) * 8, 8), :] = load_tile(i, j)


def row_of(flat, row):
    start = (row // 8) * 64 + row % 8
    return flat[pl.ds(start, 8, stride=8), :]


def planes_of(source, receiver):
    def loader(field, part, freq):
        return lambda i, j: field[part, freq, pl.ds(8 * i, 8), pl.ds(128 * j, 128)]

    return [
        loader(field, part, freq)
        for field in (source, receiver)
        for part in range(2)
        for freq in range(source.shape[1])
    ]


def slow_tile(planes, depth):
    columns = planes.shape[3]
    return lambda i, j: planes[
        128 * j // columns, depth, pl.ds(8 * i, 8), pl.ds(128 * j % columns, 128)
    ]


def pack_kernel(
    aperture_hbm, source_hbm, receiver_hbm, planes_hbm, ahead, behind,
    aperture, source, receiver, planes, sems, *flats,
):
    fetch(
        sems,
        (aperture_hbm, aperture),
        (source_hbm, source),
        (receiver_hbm, receiver),
        (planes_hbm.at[:, pl.ds(0, 1)], planes),
    )
    width = aperture[lax.axis_index("tile")]
    row_tiles = source.shape[2] // 8
    count = 4 * source.shape[1]
    loads = planes_of(source, receiver) + [slow_tile(planes, 0)]
    for plane, load in enumerate(loads):
        to_rows(flats[plane], load, row_tiles)
    for plane in range(count + 1):
        rows = HALO if plane < count else ORDER
        for k in range(rows):
            ahead[plane * HALO + k] = row_of(flats[plane], width - rows + k)
            behind[plane * HALO + k] = row_of(flats[plane], k)


def coefficients(weights, freq, slow_row, store):
    powers = weights.shape[1] // (2 * (ORDER + 1))
    for part in range(2 * (ORDER + 1)):
        value = weights[freq, part * powers + powers - 1]
        for power in range(powers - 2, -1, -1):
            value = value * slow_row + weights[freq, part * powers + power]
        store(part, value)


def sweep(freqs, fields, power, coefficient, write, partial, rows):
    def feed(held, value):
        kept = []
        for last in held:
            kept.append(value)
            value = value + last
        return kept, value

    for freq in range(freqs):
        for field in range(2):
            for part in range(2):
                p = (2 * field + part) * freqs + freq
                held = []
                for m in range(1, ORDER + 1):
                    chain = []
                    for k in range(2 * m):
                        value = power(p, m, ORDER - m + k)
                        chain, value = feed(chain, value)
                        chain.append(value)
                    held.append(chain)
                for o in range(rows):
                    kept, by_re, by_im = [], None, None
                    for m in range(ORDER + 1):
                        if m == 0:
                            value = fields(p, o)
                        else:
                            chain, value = feed(held[m - 1], power(p, m, o + ORDER + m))
                            kept.append(chain)
                        re = coefficient(freq, 2 * m, o) * value
                        im = coefficient(freq, 2 * m + 1, o) * value
                        by_re = re if by_re is None else by_re + re
                        by_im = im if by_im is None else by_im + im
                    held = kept
                    if part == 0:
                        partial[0, o] = by_re
                        partial[1, o] = by_im
                    elif field == 0:
                        write(p - freqs, o, partial[0, o] + by_im)
                        write(p, o, by_re - partial[1, o])
                    else:
                        write(p - freqs, o, partial[0, o] - by_im)
                        write(p, o, by_re + partial[1, o])


def image_row(freqs, load):
    total = None
    for k in range(2 * freqs):
        term = load(k) * load(2 * freqs + k)
        total = term if total is None else total + term
    return total


def power_of(ref, stride):
    def power(p, m, row):
        at = (p * stride + row) * 8
        at = at if isinstance(at, int) else pl.multiple_of(at, 8)
        return ref[pl.ds(at, 8), pl.ds(128 * (m - 1), 128)]

    return power


def own_kernel(
    frequency, order_table, filter_coeffs, source, receiver, planes, y_matrix,
    rows_out, powers_out, slow_out, weights_out, first_out, later_out,
    middle_out, middle_powers_out, last_out, first_image, last_image,
    flat, left, later_weights, partial,
):
    freqs, stored = source.shape[1:3]
    count = 4 * freqs
    row_tiles = stored // 8
    powers = filter_coeffs.shape[0]
    for plane, load in enumerate(planes_of(source, receiver)):
        to_rows(flat.at[plane], load, row_tiles)
        for r in range(stored):
            rows_out[plane, r] = row_of(flat.at[plane], r)
    for plane in range(count):
        split_rows(rows_out[plane], left, plane * stored * 8)
    powers_out[...] = multiply(left, count * stored * 8, y_matrix)

    for depth in range(NDEPTH):
        to_rows(flat.at[depth], slow_tile(planes, depth), row_tiles)
        for r in range(stored):
            slow_out[depth, r] = row_of(flat.at[depth], r)

    for depth, weights in enumerate((weights_out, later_weights)):
        for freq in range(freqs):
            omega = jnp.full((8, 128), frequency[freq], F32)
            active = [
                jnp.full((8, 128), jnp.where(order_table[depth, freq] >= n, 1.0, 0.0), F32)
                for n in range(ORDER + 1)
            ]
            for c in range(2):
                scale = None
                for j in range(powers):
                    scaled = [filter_coeffs[j, c, n] * active[n] for n in range(ORDER + 1)]
                    for m in range(ORDER + 1):
                        total = None
                        for n in range(m, ORDER + 1):
                            term = scaled[n] * float(SHIFTED[n][m])
                            total = term if total is None else total + term
                        if scale is not None:
                            total = total * scale
                        weights[freq, (m * 2 + c) * powers + j] = total
                    scale = omega if scale is None else scale * omega

    def tables(r, carry):
        for depth, (weights, out) in enumerate(((weights_out, first_out), (later_weights, later_out))):
            for freq in range(freqs):
                def store(part, value):
                    out[freq, part, r] = value

                coefficients(weights, freq, slow_out[depth, r], store)
        return carry

    lax.fori_loop(0, stored, tables, 0, unroll=2)

    inner = stored - 2 * ORDER

    def write_middle(p, o, value):
        middle_out[p, o] = value

    sweep(
        freqs,
        lambda p, o: rows_out[p, o + ORDER],
        power_of(powers_out, stored),
        lambda freq, part, o: first_out[freq, part, o + ORDER],
        write_middle,
        partial,
        inner,
    )
    for o in range(inner):
        first_image[o] = image_row(freqs, lambda p: middle_out[p, o])
    for plane in range(count):
        split_rows(middle_out[plane], left, plane * inner * 8)
    middle_powers_out[...] = multiply(left, count * inner * 8, y_matrix)

    def write_last(p, o, value):
        last_out[p, o] = value

    sweep(
        freqs,
        lambda p, o: middle_out[p, o + ORDER],
        power_of(middle_powers_out, inner),
        lambda freq, part, o: later_out[freq, part, o + HALO],
        write_last,
        partial,
        inner - 2 * ORDER,
    )
    for o in range(inner - 2 * ORDER):
        last_image[o] = image_row(freqs, lambda p: last_out[p, o])


def main_kernel(
    aperture, rows_in, powers_in, slow_in, weights, first_in, later,
    middle_in, middle_powers_in, last_in, first_image, last_image, y_matrix,
    from_before, from_after,
    image_out, receiver_out,
    flat, edges, left, edge_powers, slow, first, middle, middle_powers, last, images, partial,
):
    tile = lax.axis_index("tile")
    width = aperture[tile]
    count, stored = rows_in.shape[:2]
    freqs = count // 4
    row_tiles = stored // 8
    rows_one = stored + 2 * ORDER
    inner = stored - 2 * ORDER

    @pl.when(tile == 0)
    def _():
        for p in range(count):
            edges[p, HALO - 1] = jnp.zeros((8, 128), F32)
            for k in range(1, HALO):
                edges[p, HALO - 1 - k] = -rows_in[p, k - 1]
        slow[ORDER - 1] = slow_in[0, 0]
        for k in range(1, ORDER):
            slow[ORDER - 1 - k] = slow_in[0, k - 1]

    @pl.when(tile > 0)
    def _():
        for p in range(count):
            edges[p, pl.ds(0, HALO)] = from_before[pl.ds(p * HALO, HALO)]
        slow[pl.ds(0, ORDER)] = from_before[pl.ds(count * HALO, ORDER)]

    @pl.when(tile == lax.axis_size("tile") - 1)
    def _():
        for p in range(count):
            edges[p, HALO] = jnp.zeros((8, 128), F32)
            for k in range(1, HALO):
                edges[p, HALO + k] = -rows_in[p, width - k]
        slow[ORDER] = slow_in[0, width - 1]
        for k in range(1, ORDER):
            slow[ORDER + k] = slow_in[0, width - k]

    @pl.when(tile < lax.axis_size("tile") - 1)
    def _():
        for p in range(count):
            edges[p, pl.ds(HALO, HALO)] = from_after[pl.ds(p * HALO, HALO)]
        slow[pl.ds(ORDER, ORDER)] = from_after[pl.ds(count * HALO, ORDER)]

    for p in range(count):
        split_rows(edges[p], left, p * 2 * HALO * 8)
    edge_powers[...] = multiply(left, count * 2 * HALO * 8, y_matrix)
    for r in range(2 * ORDER):
        for freq in range(freqs):
            def store(part, value):
                first[freq, part, r] = value

            coefficients(weights, freq, slow[r], store)

    for p in range(count):
        middle[p, pl.ds(2 * ORDER, inner)] = middle_in[p]
    outer = power_of(edge_powers, 2 * HALO)
    own = power_of(powers_in, stored)

    def above(p, m, row):
        return outer(p, m, row) if row < HALO else own(p, m, row - HALO)

    def below(p, m, row):
        return own(p, m, row + width - HALO) if row < HALO else outer(p, m, row)

    def write_above(p, o, value):
        middle[p, o] = value

    def write_below(p, o, value):
        middle[p, o + width] = value

    sweep(
        freqs,
        lambda p, o: edges[p, o + ORDER] if o < ORDER else rows_in[p, o - ORDER],
        above,
        lambda freq, part, o: (
            first[freq, part, o] if o < ORDER else first_in[freq, part, o - ORDER]
        ),
        write_above,
        partial,
        2 * ORDER,
    )
    sweep(
        freqs,
        lambda p, o: rows_in[p, o + width - ORDER] if o < ORDER else edges[p, o + ORDER],
        below,
        lambda freq, part, o: (
            first_in[freq, part, o + width - ORDER] if o < ORDER else first[freq, part, o]
        ),
        write_below,
        partial,
        2 * ORDER,
    )
    for p in range(count):
        split_rows(middle[p, pl.ds(0, 2 * ORDER)], left, p * 4 * ORDER * 8)
        split_rows(middle[p, pl.ds(width, 2 * ORDER)], left, (p * 4 + 2) * ORDER * 8)
        middle_powers[pl.ds((p * rows_one + 2 * ORDER) * 8, inner * 8), :] = middle_powers_in[
            pl.ds(p * inner * 8, inner * 8), :
        ]
    edge_powers[...] = multiply(left, count * 4 * ORDER * 8, y_matrix)
    for p in range(count):
        size = 2 * ORDER * 8
        middle_powers[pl.ds(p * rows_one * 8, size), :] = edge_powers[pl.ds(2 * p * size, size), :]
        at = pl.multiple_of((p * rows_one + width) * 8, 8)
        middle_powers[pl.ds(at, size), :] = edge_powers[pl.ds((2 * p + 1) * size, size), :]
    for p in range(count):
        last[p, pl.ds(HALO, inner - 2 * ORDER)] = last_in[p]
    everywhere = power_of(middle_powers, rows_one)

    def write_first(p, o, value):
        last[p, o] = value

    def write_last(p, o, value):
        last[p, o + width - HALO] = value

    sweep(
        freqs,
        lambda p, o: middle[p, o + ORDER],
        everywhere,
        lambda freq, part, o: later[freq, part, o],
        write_first,
        partial,
        HALO,
    )
    sweep(
        freqs,
        lambda p, o: middle[p, o + width - ORDER],
        lambda p, m, row: everywhere(p, m, row + width - HALO),
        lambda freq, part, o: later[freq, part, o + width - HALO],
        write_last,
        partial,
        HALO,
    )

    images[0, pl.ds(ORDER, inner)] = first_image[...]
    images[1, pl.ds(HALO, inner - 2 * ORDER)] = last_image[...]
    for k in range(ORDER):
        images[0, k] = image_row(freqs, lambda p: middle[p, k + ORDER])
        images[0, width - ORDER + k] = image_row(freqs, lambda p: middle[p, width + k])
    for k in range(HALO):
        images[1, k] = image_row(freqs, lambda p: last[p, k])
        images[1, width - HALO + k] = image_row(freqs, lambda p: last[p, width - HALO + k])

    def put(slot, load_row, store_tile):
        for r in range(stored):
            at = (r // 8) * 64 + r % 8
            flat[slot, pl.ds(at, 8, stride=8), :] = jnp.where(r < width, load_row(r), 0.0)
        for i in range(row_tiles):
            for j in range(8):
                store_tile(i, j, flat[slot, pl.ds((i * 8 + j) * 8, 8), :])

    columns = image_out.shape[3]
    for depth in range(NDEPTH):
        def store_image(i, j, value):
            image_out[
                128 * j // columns, depth, pl.ds(8 * i, 8), pl.ds(128 * j % columns, 128)
            ] = value

        put(depth, lambda r: images[depth, r], store_image)
    for part in range(2):
        for freq in range(freqs):
            def store_receiver(i, j, value):
                receiver_out[part, freq, pl.ds(8 * i, 8), pl.ds(128 * j, 128)] = value

            p = (2 + part) * freqs + freq
            put(NDEPTH + part * freqs + freq, lambda r: last[p, r], store_receiver)


def passed_along(value, axis, steps):
    count = lax.axis_size(axis)
    initial, last = (max(0, -steps), min(count, count - steps))
    return lax.ppermute(value, axis, [(source, source + steps) for source in range(initial, last)])


def kernel(body, out_shape, in_specs, scratch, grant, name):
    return pl.pallas_call(
        body,
        out_shape=out_shape,
        in_specs=in_specs,
        out_specs=(VMEM,) * len(out_shape),
        scratch_shapes=scratch,
        compiler_params=pltpu.CompilerParams(vmem_limit_bytes=grant << 20),
        cost_estimate=pl.CostEstimate(flops=1000, bytes_accessed=1000, transcendentals=0),
        name=name,
    )


def shards(source_field, receiver_field, slowness, frequency, order_table, filter_coeffs, aperture):
    freqs, stored = source_field.shape[1:3]
    count = 4 * freqs
    parts = 2 * (ORDER + 1)
    rows_one = stored + 2 * ORDER
    inner = stored - 2 * ORDER
    wide = ORDER * 128

    def shape(*dims):
        return jax.ShapeDtypeStruct(dims, F32)

    def rows(*lead):
        return shape(*lead, 8, 128)

    def same(value):
        return pltpu.VMEM(value.shape, value.dtype)

    def scratch(*lead):
        return same(rows(*lead))

    planes = lax.all_gather(slowness, "freq", axis=0)
    halo = rows(count * HALO + ORDER)
    ahead, behind = kernel(
        pack_kernel,
        (halo, halo),
        [HBM] * 4,
        [
            pltpu.SMEM(aperture.shape, aperture.dtype),
            same(source_field),
            same(receiver_field),
            pltpu.VMEM((planes.shape[0], 1) + planes.shape[2:], F32),
            pltpu.SemaphoreType.DMA((4,)),
        ]
        + [pltpu.VMEM((stored * 8, 128), F32)] * (count + 1),
        60,
        "pack",
    )(aperture, source_field, receiver_field, planes)
    from_before = passed_along(ahead, "tile", 1)
    from_after = passed_along(behind, "tile", -1)

    y_matrix = jnp.asarray(y_weights(), BF16)
    coeffs = jnp.transpose(filter_coeffs, (2, 0, 1))
    weights = parts * coeffs.shape[0]
    own = kernel(
        own_kernel,
        (
            rows(count, stored),
            shape(count * stored * 8, wide),
            rows(NDEPTH, stored),
            rows(freqs, weights),
            rows(freqs, parts, stored),
            rows(freqs, parts, stored),
            rows(count, inner),
            shape(count * inner * 8, wide),
            rows(count, inner - 2 * ORDER),
            rows(inner),
            rows(inner - 2 * ORDER),
        ),
        [SMEM] * 3 + [VMEM] * 4,
        [
            pltpu.VMEM((count, stored * 8, 128), F32),
            pltpu.VMEM((count * stored * 8, 512), BF16),
            scratch(freqs, weights),
            scratch(2, inner),
        ],
        24,
        "own",
    )(frequency, order_table, coeffs, source_field, receiver_field, planes, y_matrix)
    image_parts, receiver_out = kernel(
        main_kernel,
        (shape(lax.axis_size("freq"), *slowness.shape), shape(*receiver_field.shape)),
        [SMEM] + [VMEM] * (len(own) + 3),
        [
            pltpu.VMEM((NDEPTH + 2 * freqs, stored * 8, 128), F32),
            scratch(count, 2 * HALO),
            pltpu.VMEM((count * 2 * HALO * 8, 512), BF16),
            pltpu.VMEM((count * 2 * HALO * 8, wide), F32),
            scratch(2 * ORDER),
            scratch(freqs, parts, 2 * ORDER),
            scratch(count, rows_one),
            pltpu.VMEM((count * rows_one * 8, wide), F32),
            scratch(count, stored),
            scratch(NDEPTH, stored),
            scratch(2, HALO),
        ],
        24,
        "migrate",
    )(aperture, *own, y_matrix, from_before, from_after)
    exchanged = lax.all_to_all(image_parts, "freq", 0, 0)
    return jnp.sum(exchanged, axis=0), receiver_out


def solution(mesh):
    placed = (
        P(None, "freq", "tile", None),
        P(None, "freq", "tile", None),
        P(None, "tile", "freq"),
        P("freq"),
        P(None, "freq"),
        P(),
        P(),
    )
    return jax.shard_map(
        shards,
        mesh=mesh,
        in_specs=placed,
        out_specs=(P(None, "tile", "freq"), P(None, "freq", "tile", None)),
        check_vma=False,
    )
```

time: 46.7 us -> 41.5 us (0.89)
  starting transfers between devices: 10.4 us -> 4.73 us
  local copies, waits for them, and re-layouts: 8.4 us -> 5.89 us
  blocking collectives: 14.7 us -> 16.4 us
  waiting for transfers between devices: 0.01 us -> 0.96 us
    ppermute x3 -> x2, starting transfers between devices: 10.4 us -> 4.73 us  [passed_along(): lax.ppermute(value, axis, [(source, source + steps) for source in range(i...]
    unnamed x24 -> x18, local copies, waits for them, and re-layouts: 8.4 us -> 5.89 us
    all_gather x1, blocking collectives: 6.84 us -> 8.71 us  [shards(): planes = lax.all_gather(slowness, 'freq', axis=0)]
    ppermute x3 -> x2, waiting for transfers between devices: 0.01 us -> 0.96 us  [passed_along(): lax.ppermute(value, axis, [(source, source + steps) for source in range(i...]
    pallas_call x4 -> x3, Pallas kernels: 11.2 us -> 11.4 us  [the longest x1 4.72 us: shards(): kernel(main_kernel, (shape(lax.axis_size('freq'), *slowness.shape), shape...]
  transfers between devices with their start and end apart: 3 -> 2, of which waited for: 0 -> 1; matrix products, arithmetic and copies ran while one was open for 0% -> 0% of each run, Pallas kernels for 5% -> 11%
where the time goes in v6:
time: 41.5 us; the launch traced here: 40.7 us
  blocking collectives  16.4 us (40%)
  Pallas kernels  11.4 us (27%)
  local copies, waits for them, and re-layouts  5.89 us (14%)
  starting transfers between devices  4.73 us (11%)
  waiting for transfers between devices  0.96 us (2%)
  between operations  0.69 us (2%)
  other arithmetic  0.63 us (2%)
    all_gather x1, blocking collectives, shards(): planes = lax.all_gather(slowness, 'freq', axis=0)  8.71 us
    all_to_all x1, blocking collectives, shards(): exchanged = lax.all_to_all(image_parts, 'freq', 0, 0)  7.69 us
    unnamed x18, local copies, waits for them, and re-layouts  5.89 us
    ppermute x2, starting transfers between devices, passed_along(): lax.ppermute(value, axis, [(source, source + steps) for source in range(i...  4.73 us
    pallas_call x1, Pallas kernels, shards(): kernel(main_kernel, (shape(lax.axis_size('freq'), *slowness.shape), shape...  4.72 us
    pallas_call x1, Pallas kernels, shards(): kernel(own_kernel, (rows(count, stored), shape(count * stored * 8, wide),...  4.52 us
    pallas_call x1, Pallas kernels, shards(): kernel(pack_kernel, (halo, halo), [HBM] * 4, [pltpu.SMEM(aperture.shape,...  2.12 us
    ppermute x2, waiting for transfers between devices, passed_along(): lax.ppermute(value, axis, [(source, source + steps) for source in range(i...  0.96 us
  transfers between devices with their start and end apart: 2, of which 1 were waited for; matrix products, arithmetic and copies ran while one was open for 0% of the time, Pallas kernels for 11%

profile of v6, /device:TPU:0, one launch (start us, length us, event | category | flops | bytes accessed | tf_op | source)
XLA Modules:
  0.0 40.7 jit_solution(7470699621439949340)
XLA Ops:
  0.6 0.0 copy-start.4
  0.6 0.0 copy-start.6
  0.7 8.7 %all-gather = f32[8,24,256]{2,1,0:T(8,128)} all-gather(f32[2,24,256]{2,1,0:T(8,128)} %param.10), channel_id=2, replica_groups=mesh['tile'=8,'freq'=4] {'freq'}, dimensions={0}, use_global_device_ids=true | all-gather | bytes 245760 | tf_op jit(solution)/shard_map/all_gather | solution.py:499
  9.4 2.1 %pack.1 = (f32[68,8,128]{2,1,0:T(8,128)}, f32[68,8,128]{2,1,0:T(8,128)}) custom-call(s32[8]{0:T(128)} %aperture.1, f32[2,2,24,1024]{3,2,1,0:T(8,128)} %source_hbm.1, f32[2,2,24,1024]{3,2,1,0:T(8,128)} %receiver_hbm.1, f32[4,2,24,256]{3,2,1,0:T(8,128)} %bitcast.2), custom_call_target="tpu_custom_call" | custom-call | flops 1000 | bytes 1000 | tf_op jit(solution)/shard_map/pack/pallas_call | solution.py:501
  11.5 3.4 %collective-permute-start = (f32[68,8,128]{2,1,0:T(8,128)}, f32[68,8,128]{2,1,0:T(8,128)S(1)}, u32[]{:S(2)}, u32[]{:S(2)}) collective-permute-start(f32[68,8,128]{2,1,0:T(8,128)} %get-tuple-element.28), channel_id=1, source_target_pairs={{0,4},{4,8},{8,12},{12,16},{16,20},{20,24},{24,28},{1,5},{5,9},{9,... | collective-permute-start | bytes 835592 | tf_op jit(solution)/shard_map/ppermute | solution.py:463
  14.9 1.3 %collective-permute-start.1 = (f32[68,8,128]{2,1,0:T(8,128)}, f32[68,8,128]{2,1,0:T(8,128)S(1)}, u32[]{:S(2)}, u32[]{:S(2)}) collective-permute-start(f32[68,8,128]{2,1,0:T(8,128)} %get-tuple-element.29), channel_id=1, source_target_pairs={{4,0},{8,4},{12,8},{16,12},{20,16},{24,20},{28,24},{5,1},{9,5},{13... | collective-permute-start | bytes 835592 | tf_op jit(solution)/shard_map/ppermute | solution.py:463
  16.2 0.0 copy-start
  16.2 0.9 %copy-done = f32[8,24,256]{2,1,0:T(8,128)S(1)} copy-done((f32[8,24,256]{2,1,0:T(8,128)S(1)}, f32[8,24,256]{2,1,0:T(8,128)}, u32[]{:S(2)}) %copy-start) | copy-done | bytes 196632
  17.2 0.0 copy-start.1
  17.2 1.0 %copy-done.1 = f32[2,2,24,1024]{3,2,1,0:T(8,128)S(1)} copy-done((f32[2,2,24,1024]{3,2,1,0:T(8,128)S(1)}, f32[2,2,24,1024]{3,2,1,0:T(8,128)}, u32[]{:S(2)}) %copy-start.1) | copy-done | bytes 393240
  18.2 0.0 copy-start.2
  18.2 1.0 %copy-done.2 = f32[2,2,24,1024]{3,2,1,0:T(8,128)S(1)} copy-done((f32[2,2,24,1024]{3,2,1,0:T(8,128)S(1)}, f32[2,2,24,1024]{3,2,1,0:T(8,128)}, u32[]{:S(2)}) %copy-start.2) | copy-done | bytes 393240
  19.2 0.9 %copy-done.3 = bf16[256,512]{1,0:T(8,128)(2,1)S(1)} copy-done((bf16[256,512]{1,0:T(8,128)(2,1)S(1)}, bf16[256,512]{1,0:T(8,128)(2,1)}, u32[]{:S(2)}) %copy-start.3) | copy-done | bytes 262168
  20.1 0.7 %copy-done.5 = f32[2,5,3]{1,0,2:T(2,128)S(1)} copy-done((f32[2,5,3]{1,0,2:T(2,128)S(1)}, f32[2,5,3]{1,0,2:T(2,128)}, u32[]{:S(2)}) %copy-start.5) | copy-done | bytes 144
  20.8 0.7 %copy-done.7 = s32[2,2]{1,0:T(2,128)S(1)} copy-done((s32[2,2]{1,0:T(2,128)S(1)}, s32[2,2]{1,0:T(2,128)}, u32[]{:S(2)}) %copy-start.7) | copy-done | bytes 40
  21.5 0.7 %copy-done.8 = f32[2]{0:T(128)S(1)} copy-done((f32[2]{0:T(128)S(1)}, f32[2]{0:T(128)}, u32[]{:S(2)}) %copy-start.8) | copy-done | bytes 32
  22.1 4.5 %own.1 = (f32[8,24,8,128]{3,2,1,0:T(8,128)S(1)}, f32[1536,512]{1,0:T(8,128)S(1)}, f32[2,24,8,128]{3,2,1,0:T(8,128)S(1)}, f32[2,30,8,128]{3,2,1,0:T(8,128)S(1)}, ...) custom-call(f32[2]{0:T(128)S(1)} %copy-done.8, ...), custom_call_target="tpu_custom_call" | custom-call | flops 1000 | bytes 1000 | tf_op jit(solution)/shard_map/own/pallas_call | solution.py:522
  26.7 1.0 %collective-permute-done.from_before = f32[68,8,128]{2,1,0:T(8,128)S(1)} collective-permute-done((f32[68,8,128]{2,1,0:T(8,128)}, f32[68,8,128]{2,1,0:T(8,128)S(1)}, u32[]{:S(2)}, u32[]{:S(2)}) %collective-permute-start) | collective-permute-done | bytes 278560 | tf_op jit(solution)/shard_map/ppermute | solution.py:463
  27.6 0.0 collective-permute-done.1.from_after
  27.6 0.0 copy-done.4
  27.6 0.0 copy-done.6
  27.6 4.7 %migrate.1 = (f32[4,2,24,256]{3,2,1,0:T(8,128)S(1)}, f32[2,2,24,1024]{3,2,1,0:T(8,128)}) custom-call(s32[8]{0:T(128)S(1)} %copy-done.6, f32[8,24,8,128]{3,2,1,0:T(8,128)S(1)} %get-tuple-element.17.rows_in, f32[1536,512]{1,0:T(8,128)S(1)} %get-tuple-element.18.powers_in, f32[2,24,8,128]{3,2,1,0:T(8,128)S(1)} %get-tuple-element.19.slow_in, ...), custom_call_target="tpu_custom_call" | custom-call | flops 1000 | bytes 1000 | tf_op jit(solution)/shard_map/migrate/pallas_call | solution.py:547
  32.3 7.7 %all_to_all.5 = f32[4,2,24,256]{3,2,1,0:T(8,128)S(1)} all-to-all(f32[4,2,24,256]{3,2,1,0:T(8,128)S(1)} %get-tuple-element.30), channel_id=1, replica_groups=mesh['tile'=8,'freq'=4] {'freq'}, dimensions={0} | all-to-all | bytes 393216 | tf_op jit(solution)/shard_map/all_to_all | solution.py:567
  40.0 0.6 %reduce_sum.9 = f32[2,24,256]{2,1,0:T(8,128)} reduce(f32[4,2,24,256]{3,2,1,0:T(8,128)S(1)} %all_to_all.5, f32[]{:T(128)} %constant.1.clone.1), dimensions={0}, to_apply=%region_0.0 | reduce | flops 36864 | bytes 245764 | tf_op jit(solution)/shard_map/reduce_sum | solution.py:568
  (4 shorter events, 0.0 us)
Async XLA Ops:
  0.6 27.0 %copy-start.4 = (bf16[256,512]{1,0:T(8,128)(2,1)S(1)}, bf16[256,512]{1,0:T(8,128)(2,1)}, u32[]{:S(2)}) copy-start(bf16[256,512]{1,0:T(8,128)(2,1)} %constant.4.clone.y_matrix) | copy-start | bytes 786436
  0.6 27.0 %copy-start.6 = (s32[8]{0:T(128)S(1)}, s32[8]{0:T(128)}, u32[]{:S(2)}) copy-start(s32[8]{0:T(128)} %aperture.1) | copy-start | bytes 100
  11.5 16.1 %collective-permute-start = (f32[68,8,128]{2,1,0:T(8,128)}, f32[68,8,128]{2,1,0:T(8,128)S(1)}, u32[]{:S(2)}, u32[]{:S(2)}) collective-permute-start(f32[68,8,128]{2,1,0:T(8,128)} %get-tuple-element.28), channel_id=1, source_target_pairs={{0,4},{4,8},{8,12},{12,16},{16,20},{20,24},{24,28},{1,5},{5,9},{9,... | collective-permute-start | bytes 835592 | tf_op jit(solution)/shard_map/ppermute | solution.py:463
  14.9 12.7 %collective-permute-start.1 = (f32[68,8,128]{2,1,0:T(8,128)}, f32[68,8,128]{2,1,0:T(8,128)S(1)}, u32[]{:S(2)}, u32[]{:S(2)}) collective-permute-start(f32[68,8,128]{2,1,0:T(8,128)} %get-tuple-element.29), channel_id=1, source_target_pairs={{4,0},{8,4},{12,8},{16,12},{20,16},{24,20},{28,24},{5,1},{9,5},{13... | collective-permute-start | bytes 835592 | tf_op jit(solution)/shard_map/ppermute | solution.py:463
  16.2 0.9 %copy-start = (f32[8,24,256]{2,1,0:T(8,128)S(1)}, f32[8,24,256]{2,1,0:T(8,128)}, u32[]{:S(2)}) copy-start(f32[8,24,256]{2,1,0:T(8,128)} %all-gather) | copy-start | bytes 589828
  17.2 1.0 %copy-start.1 = (f32[2,2,24,1024]{3,2,1,0:T(8,128)S(1)}, f32[2,2,24,1024]{3,2,1,0:T(8,128)}, u32[]{:S(2)}) copy-start(f32[2,2,24,1024]{3,2,1,0:T(8,128)} %source_hbm.1) | copy-start | bytes 1179652
  18.2 1.0 %copy-start.2 = (f32[2,2,24,1024]{3,2,1,0:T(8,128)S(1)}, f32[2,2,24,1024]{3,2,1,0:T(8,128)}, u32[]{:S(2)}) copy-start(f32[2,2,24,1024]{3,2,1,0:T(8,128)} %receiver_hbm.1) | copy-start | bytes 1179652
  19.2 0.9 %copy-start.3 = (bf16[256,512]{1,0:T(8,128)(2,1)S(1)}, bf16[256,512]{1,0:T(8,128)(2,1)}, u32[]{:S(2)}) copy-start(bf16[256,512]{1,0:T(8,128)(2,1)} %constant.4.clone.y_matrix) | copy-start | bytes 786436
  20.1 0.7 %copy-start.5 = (f32[2,5,3]{1,0,2:T(2,128)S(1)}, f32[2,5,3]{1,0,2:T(2,128)}, u32[]{:S(2)}) copy-start(f32[2,5,3]{1,0,2:T(2,128)} %param.13) | copy-start | bytes 364
  20.8 0.7 %copy-start.7 = (s32[2,2]{1,0:T(2,128)S(1)}, s32[2,2]{1,0:T(2,128)}, u32[]{:S(2)}) copy-start(s32[2,2]{1,0:T(2,128)} %order_table.1) | copy-start | bytes 52
  21.5 0.7 %copy-start.8 = (f32[2]{0:T(128)S(1)}, f32[2]{0:T(128)}, u32[]{:S(2)}) copy-start(f32[2]{0:T(128)} %frequency.1) | copy-start | bytes 28

commit v7 on v6

--- a/solution.py
+++ b/solution.py
@@ -14,7 +14,6 @@
 F32 = jnp.float32
 BF16 = jnp.bfloat16
 VMEM = pl.BlockSpec(memory_space=pltpu.VMEM)
-HBM = pl.BlockSpec(memory_space=pltpu.HBM)
 SMEM = pl.BlockSpec(memory_space=pltpu.SMEM)
 
 SHIFTED = ((1,), (-1, 2), (1, -8, 8), (-1, 18, -48, 32), (1, -32, 160, -256, 128))
@@ -63,14 +62,6 @@
     return jnp.dot(left[pl.ds(0, rows), :], right, preferred_element_type=F32)
 
 
-def fetch(sems, *pairs):
-    copies = [pltpu.make_async_copy(a, b, sems.at[k]) for k, (a, b) in enumerate(pairs)]
-    for copy in copies:
-        copy.start()
-    for copy in copies:
-        copy.wait()
-
-
 def to_rows(flat, load_tile, row_tiles):
     for i in range(row_tiles):
         for j in range(8):
@@ -101,28 +92,16 @@
     ]
 
 
-def pack_kernel(
-    aperture_hbm, source_hbm, receiver_hbm, planes_hbm, ahead, behind,
-    aperture, source, receiver, planes, sems, *flats,
-):
-    fetch(
-        sems,
-        (aperture_hbm, aperture),
-        (source_hbm, source),
-        (receiver_hbm, receiver),
-        (planes_hbm.at[:, pl.ds(0, 1)], planes),
-    )
+def ahead_kernel(aperture, source, receiver, planes, ahead, *flats):
     width = aperture[lax.axis_index("tile")]
     row_tiles = source.shape[2] // 8
     count = 4 * source.shape[1]
-    loads = planes_of(source, receiver) + [slow_tile(planes, 0)]
-    for plane, load in enumerate(loads):
+    for plane, load in enumerate(planes_of(source, receiver) + [slow_tile(planes, 0)]):
         to_rows(flats[plane], load, row_tiles)
     for plane in range(count + 1):
         rows = HALO if plane < count else ORDER
         for k in range(rows):
             ahead[plane * HALO + k] = row_of(flats[plane], width - rows + k)
-            behind[plane * HALO + k] = row_of(flats[plane], k)
 
 
 def coefficients(weights, freq, slow_row, store):
@@ -195,29 +174,37 @@
     return power
 
 
-def own_kernel(
-    frequency, order_table, filter_coeffs, source, receiver, planes, y_matrix,
-    rows_out, powers_out, slow_out, weights_out, first_out, later_out,
-    middle_out, middle_powers_out, last_out, first_image, last_image,
-    flat, left, later_weights, partial,
+def rows_kernel(
+    source, receiver, planes, y_matrix, behind, rows_out, powers_out, slow_out, flat, left
 ):
     freqs, stored = source.shape[1:3]
     count = 4 * freqs
     row_tiles = stored // 8
-    powers = filter_coeffs.shape[0]
     for plane, load in enumerate(planes_of(source, receiver)):
         to_rows(flat.at[plane], load, row_tiles)
         for r in range(stored):
             rows_out[plane, r] = row_of(flat.at[plane], r)
-    for plane in range(count):
-        split_rows(rows_out[plane], left, plane * stored * 8)
-    powers_out[...] = multiply(left, count * stored * 8, y_matrix)
-
     for depth in range(NDEPTH):
         to_rows(flat.at[depth], slow_tile(planes, depth), row_tiles)
         for r in range(stored):
             slow_out[depth, r] = row_of(flat.at[depth], r)
-
+    for plane in range(count):
+        behind[pl.ds(plane * HALO, HALO)] = rows_out[plane, pl.ds(0, HALO)]
+    behind[pl.ds(count * HALO, ORDER)] = slow_out[0, pl.ds(0, ORDER)]
+    for plane in range(count):
+        split_rows(rows_out[plane], left, plane * stored * 8)
+    powers_out[...] = multiply(left, count * stored * 8, y_matrix)
+
+
+def own_kernel(
+    frequency, order_table, filter_coeffs, rows_in, powers_in, slow_in, y_matrix,
+    weights_out, first_out, later_out,
+    middle_out, middle_powers_out, last_out, first_image, last_image,
+    left, later_weights, partial,
+):
+    count, stored = rows_in.shape[:2]
+    freqs = count // 4
+    powers = filter_coeffs.shape[0]
     for depth, weights in enumerate((weights_out, later_weights)):
         for freq in range(freqs):
             omega = jnp.full((8, 128), frequency[freq], F32)
@@ -245,7 +232,7 @@
                 def store(part, value):
                     out[freq, part, r] = value
 
-                coefficients(weights, freq, slow_out[depth, r], store)
+                coefficients(weights, freq, slow_in[depth, r], store)
         return carry
 
     lax.fori_loop(0, stored, tables, 0, unroll=2)
@@ -257,8 +244,8 @@
 
     sweep(
         freqs,
-        lambda p, o: rows_out[p, o + ORDER],
-        power_of(powers_out, stored),
+        lambda p, o: rows_in[p, o + ORDER],
+        power_of(powers_in, stored),
         lambda freq, part, o: first_out[freq, part, o + ORDER],
         write_middle,
         partial,
@@ -286,20 +273,16 @@
         last_image[o] = image_row(freqs, lambda p: last_out[p, o])
 
 
-def main_kernel(
-    aperture, rows_in, powers_in, slow_in, weights, first_in, later,
-    middle_in, middle_powers_in, last_in, first_image, last_image, y_matrix,
-    from_before, from_after,
-    image_out, receiver_out,
-    flat, edges, left, edge_powers, slow, first, middle, middle_powers, last, images, partial,
+def upper_kernel(
+    rows_in, powers_in, slow_in, weights, first_in, later,
+    middle_in, middle_powers_in, last_in, first_image, last_image, y_matrix, from_before,
+    middle, middle_powers, last, images,
+    edges, left, edge_powers, slow, first, partial,
 ):
-    tile = lax.axis_index("tile")
-    width = aperture[tile]
     count, stored = rows_in.shape[:2]
     freqs = count // 4
-    row_tiles = stored // 8
-    rows_one = stored + 2 * ORDER
     inner = stored - 2 * ORDER
+    tile = lax.axis_index("tile")
 
     @pl.when(tile == 0)
     def _():
@@ -314,123 +297,150 @@
     @pl.when(tile > 0)
     def _():
         for p in range(count):
-            edges[p, pl.ds(0, HALO)] = from_before[pl.ds(p * HALO, HALO)]
-        slow[pl.ds(0, ORDER)] = from_before[pl.ds(count * HALO, ORDER)]
+            edges[p] = from_before[pl.ds(p * HALO, HALO)]
+        slow[...] = from_before[pl.ds(count * HALO, ORDER)]
+
+    for p in range(count):
+        split_rows(edges[p], left, p * HALO * 8)
+    edge_powers[...] = multiply(left, count * HALO * 8, y_matrix)
+    for r in range(ORDER):
+        for freq in range(freqs):
+            def store(part, value):
+                first[freq, part, r] = value
+
+            coefficients(weights, freq, slow[r], store)
+
+    outer = power_of(edge_powers, HALO)
+    own = power_of(powers_in, stored)
+
+    def write_middle(p, o, value):
+        middle[p, o] = value
+
+    sweep(
+        freqs,
+        lambda p, o: edges[p, o + ORDER] if o < ORDER else rows_in[p, o - ORDER],
+        lambda p, m, row: outer(p, m, row) if row < HALO else own(p, m, row - HALO),
+        lambda freq, part, o: (
+            first[freq, part, o] if o < ORDER else first_in[freq, part, o - ORDER]
+        ),
+        write_middle,
+        partial,
+        2 * ORDER,
+    )
+    for p in range(count):
+        middle[p, pl.ds(2 * ORDER, inner)] = middle_in[p]
+        split_rows(middle[p, pl.ds(0, 2 * ORDER)], left, p * HALO * 8)
+    edge_powers[...] = multiply(left, count * HALO * 8, y_matrix)
+    for p in range(count):
+        size = HALO * 8
+        middle_powers[pl.ds(p * stored * 8, size), :] = edge_powers[pl.ds(p * size, size), :]
+        middle_powers[pl.ds((p * stored + HALO) * 8, inner * 8), :] = middle_powers_in[
+            pl.ds(p * inner * 8, inner * 8), :
+        ]
+
+    def write_last(p, o, value):
+        last[p, o] = value
+
+    sweep(
+        freqs,
+        lambda p, o: middle[p, o + ORDER],
+        power_of(middle_powers, stored),
+        lambda freq, part, o: later[freq, part, o],
+        write_last,
+        partial,
+        HALO,
+    )
+    for p in range(count):
+        last[p, pl.ds(HALO, inner - HALO)] = last_in[p]
+    images[0, pl.ds(ORDER, inner)] = first_image[...]
+    images[1, pl.ds(HALO, inner - HALO)] = last_image[...]
+    for k in range(ORDER):
+        images[0, k] = image_row(freqs, lambda p: middle[p, k + ORDER])
+    for k in range(HALO):
+        images[1, k] = image_row(freqs, lambda p: last[p, k])
+
+
+def lower_kernel(
+    aperture, rows_in, powers_in, slow_in, weights, first_in, later,
+    middle_in, middle_powers_in, last_in, images_in, y_matrix, from_after,
+    image_out, receiver_hbm,
+    receiver_out, sem,
+    flat, edges, left, edge_powers, slow, first, middle, last, images, partial,
+):
+    tile = lax.axis_index("tile")
+    width = aperture[tile]
+    count, stored = rows_in.shape[:2]
+    freqs = count // 4
+    row_tiles = stored // 8
+    inner = stored - 2 * ORDER
 
     @pl.when(tile == lax.axis_size("tile") - 1)
     def _():
         for p in range(count):
-            edges[p, HALO] = jnp.zeros((8, 128), F32)
+            edges[p, 0] = jnp.zeros((8, 128), F32)
             for k in range(1, HALO):
-                edges[p, HALO + k] = -rows_in[p, width - k]
-        slow[ORDER] = slow_in[0, width - 1]
+                edges[p, k] = -rows_in[p, width - k]
+        slow[0] = slow_in[0, width - 1]
         for k in range(1, ORDER):
-            slow[ORDER + k] = slow_in[0, width - k]
+            slow[k] = slow_in[0, width - k]
 
     @pl.when(tile < lax.axis_size("tile") - 1)
     def _():
         for p in range(count):
-            edges[p, pl.ds(HALO, HALO)] = from_after[pl.ds(p * HALO, HALO)]
-        slow[pl.ds(ORDER, ORDER)] = from_after[pl.ds(count * HALO, ORDER)]
+            edges[p] = from_after[pl.ds(p * HALO, HALO)]
+        slow[...] = from_after[pl.ds(count * HALO, ORDER)]
 
     for p in range(count):
-        split_rows(edges[p], left, p * 2 * HALO * 8)
-    edge_powers[...] = multiply(left, count * 2 * HALO * 8, y_matrix)
-    for r in range(2 * ORDER):
+        split_rows(edges[p], left, p * HALO * 8)
+    edge_powers[...] = multiply(left, count * HALO * 8, y_matrix)
+    for r in range(ORDER):
         for freq in range(freqs):
             def store(part, value):
                 first[freq, part, r] = value
 
             coefficients(weights, freq, slow[r], store)
 
-    for p in range(count):
-        middle[p, pl.ds(2 * ORDER, inner)] = middle_in[p]
-    outer = power_of(edge_powers, 2 * HALO)
+    outer = power_of(edge_powers, HALO)
     own = power_of(powers_in, stored)
-
-    def above(p, m, row):
-        return outer(p, m, row) if row < HALO else own(p, m, row - HALO)
-
-    def below(p, m, row):
-        return own(p, m, row + width - HALO) if row < HALO else outer(p, m, row)
-
-    def write_above(p, o, value):
+    done = power_of(middle_powers_in, stored)
+
+    def write_middle(p, o, value):
         middle[p, o] = value
-
-    def write_below(p, o, value):
-        middle[p, o + width] = value
 
     sweep(
         freqs,
-        lambda p, o: edges[p, o + ORDER] if o < ORDER else rows_in[p, o - ORDER],
-        above,
+        lambda p, o: rows_in[p, o + width - ORDER] if o < ORDER else edges[p, o - ORDER],
+        lambda p, m, row: (
+            own(p, m, row + width - HALO) if row < HALO else outer(p, m, row - HALO)
+        ),
         lambda freq, part, o: (
-            first[freq, part, o] if o < ORDER else first_in[freq, part, o - ORDER]
+            first_in[freq, part, o + width - ORDER] if o < ORDER else first[freq, part, o - ORDER]
         ),
-        write_above,
+        write_middle,
         partial,
         2 * ORDER,
     )
+    for p in range(count):
+        split_rows(middle[p], left, p * HALO * 8)
+    edge_powers[...] = multiply(left, count * HALO * 8, y_matrix)
+
+    def write_last(p, o, value):
+        last[p, o + width - HALO] = value
+
+    for p in range(2 * freqs, count):
+        last[p, pl.ds(0, inner)] = last_in[p]
+    images[:, pl.ds(0, stored - ORDER)] = images_in[...]
     sweep(
         freqs,
-        lambda p, o: rows_in[p, o + width - ORDER] if o < ORDER else edges[p, o + ORDER],
-        below,
-        lambda freq, part, o: (
-            first_in[freq, part, o + width - ORDER] if o < ORDER else first[freq, part, o]
+        lambda p, o: middle_in[p, o + width - ORDER] if o < ORDER else middle[p, o - ORDER],
+        lambda p, m, row: (
+            done(p, m, row + width - HALO) if row < HALO else outer(p, m, row - HALO)
         ),
-        write_below,
-        partial,
-        2 * ORDER,
-    )
-    for p in range(count):
-        split_rows(middle[p, pl.ds(0, 2 * ORDER)], left, p * 4 * ORDER * 8)
-        split_rows(middle[p, pl.ds(width, 2 * ORDER)], left, (p * 4 + 2) * ORDER * 8)
-        middle_powers[pl.ds((p * rows_one + 2 * ORDER) * 8, inner * 8), :] = middle_powers_in[
-            pl.ds(p * inner * 8, inner * 8), :
-        ]
-    edge_powers[...] = multiply(left, count * 4 * ORDER * 8, y_matrix)
-    for p in range(count):
-        size = 2 * ORDER * 8
-        middle_powers[pl.ds(p * rows_one * 8, size), :] = edge_powers[pl.ds(2 * p * size, size), :]
-        at = pl.multiple_of((p * rows_one + width) * 8, 8)
-        middle_powers[pl.ds(at, size), :] = edge_powers[pl.ds((2 * p + 1) * size, size), :]
-    for p in range(count):
-        last[p, pl.ds(HALO, inner - 2 * ORDER)] = last_in[p]
-    everywhere = power_of(middle_powers, rows_one)
-
-    def write_first(p, o, value):
-        last[p, o] = value
-
-    def write_last(p, o, value):
-        last[p, o + width - HALO] = value
-
-    sweep(
-        freqs,
-        lambda p, o: middle[p, o + ORDER],
-        everywhere,
-        lambda freq, part, o: later[freq, part, o],
-        write_first,
-        partial,
-        HALO,
-    )
-    sweep(
-        freqs,
-        lambda p, o: middle[p, o + width - ORDER],
-        lambda p, m, row: everywhere(p, m, row + width - HALO),
         lambda freq, part, o: later[freq, part, o + width - HALO],
         write_last,
         partial,
         HALO,
     )
-
-    images[0, pl.ds(ORDER, inner)] = first_image[...]
-    images[1, pl.ds(HALO, inner - 2 * ORDER)] = last_image[...]
-    for k in range(ORDER):
-        images[0, k] = image_row(freqs, lambda p: middle[p, k + ORDER])
-        images[0, width - ORDER + k] = image_row(freqs, lambda p: middle[p, width + k])
-    for k in range(HALO):
-        images[1, k] = image_row(freqs, lambda p: last[p, k])
-        images[1, width - HALO + k] = image_row(freqs, lambda p: last[p, width - HALO + k])
 
     def put(slot, load_row, store_tile):
         for r in range(stored):
@@ -440,6 +450,20 @@
             for j in range(8):
                 store_tile(i, j, flat[slot, pl.ds((i * 8 + j) * 8, 8), :])
 
+    for part in range(2):
+        for freq in range(freqs):
+            def store_receiver(i, j, value):
+                receiver_out[part, freq, pl.ds(8 * i, 8), pl.ds(128 * j, 128)] = value
+
+            p = (2 + part) * freqs + freq
+            put(NDEPTH + part * freqs + freq, lambda r: last[p, r], store_receiver)
+    sent = pltpu.make_async_copy(receiver_out, receiver_hbm, sem)
+    sent.start()
+
+    for k in range(ORDER):
+        images[0, width - ORDER + k] = image_row(freqs, lambda p: middle[p, k])
+    for k in range(HALO):
+        images[1, width - HALO + k] = image_row(freqs, lambda p: last[p, width - HALO + k])
     columns = image_out.shape[3]
     for depth in range(NDEPTH):
         def store_image(i, j, value):
@@ -448,13 +472,7 @@
             ] = value
 
         put(depth, lambda r: images[depth, r], store_image)
-    for part in range(2):
-        for freq in range(freqs):
-            def store_receiver(i, j, value):
-                receiver_out[part, freq, pl.ds(8 * i, 8), pl.ds(128 * j, 128)] = value
-
-            p = (2 + part) * freqs + freq
-            put(NDEPTH + part * freqs + freq, lambda r: last[p, r], store_receiver)
+    sent.wait()
 
 
 def passed_along(value, axis, steps):
@@ -463,14 +481,14 @@
     return lax.ppermute(value, axis, [(source, source + steps) for source in range(initial, last)])
 
 
-def kernel(body, out_shape, in_specs, scratch, grant, name):
+def kernel(body, out_shape, in_specs, scratch, name):
     return pl.pallas_call(
         body,
         out_shape=out_shape,
         in_specs=in_specs,
         out_specs=(VMEM,) * len(out_shape),
         scratch_shapes=scratch,
-        compiler_params=pltpu.CompilerParams(vmem_limit_bytes=grant << 20),
+        compiler_params=pltpu.CompilerParams(vmem_limit_bytes=24 << 20),
         cost_estimate=pl.CostEstimate(flops=1000, bytes_accessed=1000, transcendentals=0),
         name=name,
     )
@@ -480,7 +498,6 @@
     freqs, stored = source_field.shape[1:3]
     count = 4 * freqs
     parts = 2 * (ORDER + 1)
-    rows_one = stored + 2 * ORDER
     inner = stored - 2 * ORDER
     wide = ORDER * 128
 
@@ -498,72 +515,89 @@
 
     planes = lax.all_gather(slowness, "freq", axis=0)
     halo = rows(count * HALO + ORDER)
-    ahead, behind = kernel(
-        pack_kernel,
-        (halo, halo),
-        [HBM] * 4,
-        [
-            pltpu.SMEM(aperture.shape, aperture.dtype),
-            same(source_field),
-            same(receiver_field),
-            pltpu.VMEM((planes.shape[0], 1) + planes.shape[2:], F32),
-            pltpu.SemaphoreType.DMA((4,)),
-        ]
-        + [pltpu.VMEM((stored * 8, 128), F32)] * (count + 1),
-        60,
-        "pack",
+    flat = pltpu.VMEM((stored * 8, 128), F32)
+    (ahead,) = kernel(
+        ahead_kernel, (halo,), [SMEM] + [VMEM] * 3, [flat] * (count + 1), "ahead"
     )(aperture, source_field, receiver_field, planes)
     from_before = passed_along(ahead, "tile", 1)
+
+    y_matrix = jnp.asarray(y_weights(), BF16)
+    behind, own_rows, own_powers, slow = kernel(
+        rows_kernel,
+        (halo, rows(count, stored), shape(count * stored * 8, wide), rows(NDEPTH, stored)),
+        [VMEM] * 4,
+        [
+            pltpu.VMEM((count, stored * 8, 128), F32),
+            pltpu.VMEM((count * stored * 8, 512), BF16),
+        ],
+        "rows",
+    )(source_field, receiver_field, planes, y_matrix)
     from_after = passed_along(behind, "tile", -1)
 
-    y_matrix = jnp.asarray(y_weights(), BF16)
     coeffs = jnp.transpose(filter_coeffs, (2, 0, 1))
-    weights = parts * coeffs.shape[0]
-    own = kernel(
+    terms = parts * coeffs.shape[0]
+    weights, first, later, *inside = kernel(
         own_kernel,
         (
-            rows(count, stored),
-            shape(count * stored * 8, wide),
-            rows(NDEPTH, stored),
-            rows(freqs, weights),
+            rows(freqs, terms),
             rows(freqs, parts, stored),
             rows(freqs, parts, stored),
             rows(count, inner),
             shape(count * inner * 8, wide),
-            rows(count, inner - 2 * ORDER),
+            rows(count, inner - HALO),
             rows(inner),
-            rows(inner - 2 * ORDER),
+            rows(inner - HALO),
         ),
         [SMEM] * 3 + [VMEM] * 4,
         [
-            pltpu.VMEM((count, stored * 8, 128), F32),
-            pltpu.VMEM((count * stored * 8, 512), BF16),
-            scratch(freqs, weights),
+            pltpu.VMEM((count * inner * 8, 512), BF16),
+            scratch(freqs, terms),
             scratch(2, inner),
         ],
-        24,
         "own",
-    )(frequency, order_table, coeffs, source_field, receiver_field, planes, y_matrix)
-    image_parts, receiver_out = kernel(
-        main_kernel,
-        (shape(lax.axis_size("freq"), *slowness.shape), shape(*receiver_field.shape)),
-        [SMEM] + [VMEM] * (len(own) + 3),
-        [
+    )(frequency, order_table, coeffs, own_rows, own_powers, slow, y_matrix)
+    edge = [
+        scratch(count, HALO),
+        pltpu.VMEM((count * HALO * 8, 512), BF16),
+        pltpu.VMEM((count * HALO * 8, wide), F32),
+        scratch(ORDER),
+        scratch(freqs, parts, ORDER),
+    ]
+    tables = (own_rows, own_powers, slow, weights, first, later)
+    upper = kernel(
+        upper_kernel,
+        (
+            rows(count, stored),
+            shape(count * stored * 8, wide),
+            rows(count, inner),
+            rows(NDEPTH, stored - ORDER),
+        ),
+        [VMEM] * (len(tables) + len(inside) + 2),
+        edge + [scratch(2, HALO)],
+        "upper",
+    )(*tables, *inside, y_matrix, from_before)
+    image_parts, receiver_out = pl.pallas_call(
+        lower_kernel,
+        out_shape=(
+            shape(lax.axis_size("freq"), *slowness.shape),
+            shape(*receiver_field.shape),
+        ),
+        in_specs=[SMEM] + [VMEM] * (len(tables) + len(upper) + 2),
+        out_specs=(VMEM, pl.BlockSpec(memory_space=pl.ANY)),
+        scratch_shapes=[
+            same(receiver_field),
+            pltpu.SemaphoreType.DMA,
             pltpu.VMEM((NDEPTH + 2 * freqs, stored * 8, 128), F32),
-            scratch(count, 2 * HALO),
-            pltpu.VMEM((count * 2 * HALO * 8, 512), BF16),
-            pltpu.VMEM((count * 2 * HALO * 8, wide), F32),
-            scratch(2 * ORDER),
-            scratch(freqs, parts, 2 * ORDER),
-            scratch(count, rows_one),
-            pltpu.VMEM((count * rows_one * 8, wide), F32),
+            *edge,
+            scratch(count, HALO),
             scratch(count, stored),
             scratch(NDEPTH, stored),
             scratch(2, HALO),
         ],
-        24,
-        "migrate",
-    )(aperture, *own, y_matrix, from_before, from_after)
+        compiler_params=pltpu.CompilerParams(vmem_limit_bytes=24 << 20),
+        cost_estimate=pl.CostEstimate(flops=1000, bytes_accessed=1000, transcendentals=0),
+        name="lower",
+    )(aperture, *tables, *upper, y_matrix, from_after)
     exchanged = lax.all_to_all(image_parts, "freq", 0, 0)
     return jnp.sum(exchanged, axis=0), receiver_out
 

time: 41.5 us -> 39.5 us (0.952)
  waiting for transfers between devices: 0.96 us -> 4.04 us
  local copies, waits for them, and re-layouts: 5.89 us -> 3.62 us
  Pallas kernels: 11.4 us -> 9.84 us
  blocking collectives: 16.4 us -> 15.1 us
    ppermute x2, waiting for transfers between devices: 0.96 us -> 4.04 us  [passed_along(): lax.ppermute(value, axis, [(source, source + steps) for source in range(i...]
    unnamed x18, local copies, waits for them, and re-layouts: 5.89 us -> 3.62 us
    all_gather x1, blocking collectives: 8.71 us -> 7.18 us  [shards(): planes = lax.all_gather(slowness, 'freq', axis=0)]
    pallas_call x3 -> x5, Pallas kernels: 11.4 us -> 9.84 us  [the longest x1 3.39 us: shards(): kernel(own_kernel, (rows(freqs, terms), rows(freqs, parts, stored), rows(...]
  transfers between devices with their start and end apart: 2 -> 2, of which waited for: 1 -> 1; matrix products, arithmetic and copies ran while one was open for 0% -> 0% of each run, Pallas kernels for 11% -> 16%
where the time goes in v7:
time: 39.5 us; the launch traced here: 38.9 us
  blocking collectives  15.1 us (38%)
  Pallas kernels  9.84 us (25%)
  starting transfers between devices  4.95 us (13%)
  waiting for transfers between devices  4.04 us (10%)
  local copies, waits for them, and re-layouts  3.62 us (9%)
  between operations  0.75 us (2%)
  other arithmetic  0.63 us (2%)
    all_to_all x1, blocking collectives, shards(): exchanged = lax.all_to_all(image_parts, 'freq', 0, 0)  7.89 us
    all_gather x1, blocking collectives, shards(): planes = lax.all_gather(slowness, 'freq', axis=0)  7.18 us
    ppermute x2, starting transfers between devices, passed_along(): lax.ppermute(value, axis, [(source, source + steps) for source in range(i...  4.95 us
    ppermute x2, waiting for transfers between devices, passed_along(): lax.ppermute(value, axis, [(source, source + steps) for source in range(i...  4.04 us
    unnamed x18, local copies, waits for them, and re-layouts  3.62 us
    pallas_call x1, Pallas kernels, shards(): kernel(own_kernel, (rows(freqs, terms), rows(freqs, parts, stored), rows(...  3.39 us
    pallas_call x1, Pallas kernels, shards(): pl.pallas_call(lower_kernel, out_shape=(shape(lax.axis_size('freq'), *slo...  2.91 us
    pallas_call x1, Pallas kernels, shards(): kernel(upper_kernel, (rows(count, stored), shape(count * stored * 8, wide...  1.73 us
  transfers between devices with their start and end apart: 2, of which 1 were waited for; matrix products, arithmetic and copies ran while one was open for 0% of the time, Pallas kernels for 16%

profile of v7, /device:TPU:0, one launch (start us, length us, event | category | flops | bytes accessed | tf_op | source)
XLA Modules:
  0.0 38.9 jit_solution(17727025384243039381)
XLA Ops:
  0.6 0.0 copy-start.1
  0.6 7.2 %all-gather = f32[8,24,256]{2,1,0:T(8,128)S(1)} all-gather(f32[2,24,256]{2,1,0:T(8,128)} %param.10), channel_id=2, replica_groups=mesh['tile'=8,'freq'=4] {'freq'}, dimensions={0}, use_global_device_ids=true | all-gather | bytes 245760 | tf_op jit(solution)/shard_map/all_gather | solution.py:516
  7.8 1.0 %copy-done.2 = f32[2,2,24,1024]{3,2,1,0:T(8,128)S(1)} copy-done((f32[2,2,24,1024]{3,2,1,0:T(8,128)S(1)}, f32[2,2,24,1024]{3,2,1,0:T(8,128)}, u32[]{:S(2)}) %copy-start.2) | copy-done | bytes 393240
  8.8 1.0 %copy-done.3 = f32[2,2,24,1024]{3,2,1,0:T(8,128)S(1)} copy-done((f32[2,2,24,1024]{3,2,1,0:T(8,128)S(1)}, f32[2,2,24,1024]{3,2,1,0:T(8,128)}, u32[]{:S(2)}) %copy-start.3) | copy-done | bytes 393240
  9.8 0.7 %copy-done.5 = s32[8]{0:T(128)S(1)} copy-done((s32[8]{0:T(128)S(1)}, s32[8]{0:T(128)}, u32[]{:S(2)}) %copy-start.5) | copy-done | bytes 56
  10.5 0.7 %ahead.1 = f32[68,8,128]{2,1,0:T(8,128)S(1)} custom-call(s32[8]{0:T(128)S(1)} %copy-done.5, f32[2,2,24,1024]{3,2,1,0:T(8,128)S(1)} %copy-done.2, f32[2,2,24,1024]{3,2,1,0:T(8,128)S(1)} %copy-done.3, f32[4,2,24,256]{3,2,1,0:T(8,128)S(1)} %bitcast.2), custom_call_target="tpu_custom_call" | custom-call | flops 1000 | bytes 1000 | tf_op jit(solution)/shard_map/ahead/pallas_call | solution.py:519
  11.2 3.7 %collective-permute-start = (f32[68,8,128]{2,1,0:T(8,128)S(1)}, f32[68,8,128]{2,1,0:T(8,128)S(1)}, u32[]{:S(2)}, u32[]{:S(2)}) collective-permute-start(f32[68,8,128]{2,1,0:T(8,128)S(1)} %ahead.1), channel_id=1, source_target_pairs={{0,4},{4,8},{8,12},{12,16},{16,20},{20,24},{24,28},{1,5},{5,9},{9,... | collective-permute-start | bytes 835592 | tf_op jit(solution)/shard_map/ppermute | solution.py:481
  14.8 0.0 copy-start
  14.8 0.9 %copy-done = bf16[256,512]{1,0:T(8,128)(2,1)S(1)} copy-done((bf16[256,512]{1,0:T(8,128)(2,1)S(1)}, bf16[256,512]{1,0:T(8,128)(2,1)}, u32[]{:S(2)}) %copy-start) | copy-done | bytes 262168
  15.8 1.1 %rows.1 = (f32[68,8,128]{2,1,0:T(8,128)S(1)}, f32[8,24,8,128]{3,2,1,0:T(8,128)S(1)}, f32[1536,512]{1,0:T(8,128)S(1)}, f32[2,24,8,128]{3,2,1,0:T(8,128)S(1)}) custom-call(f32[2,2,24,1024]{3,2,1,0:T(8,128)S(1)} %copy-done.2, f32[2,2,24,1024]{3,2,1,0:T(8,128)S(1)} %copy-done.3, f32[4,2,24,256]{3,2,1,0:T(8,128)S(1)} %bitcast.3, bf16[256,512]{1,0:T(8,128)(2,1)S(1)} %copy-done), custom_call_target="tpu_custom_call" | custom-call | flops 1000 | bytes 1000 | tf_op jit(solution)/shard_map/rows/pallas_call | solution.py:525
  16.9 1.3 %collective-permute-start.1 = (f32[68,8,128]{2,1,0:T(8,128)S(1)}, f32[68,8,128]{2,1,0:T(8,128)S(1)}, u32[]{:S(2)}, u32[]{:S(2)}) collective-permute-start(f32[68,8,128]{2,1,0:T(8,128)S(1)} %get-tuple-element.35), channel_id=1, source_target_pairs={{4,0},{8,4},{12,8},{16,12},{20,16},{24,20},{28,24},{5,1},{9,5},{13... | collective-permute-start | bytes 835592 | tf_op jit(solution)/shard_map/ppermute | solution.py:481
  18.2 0.0 copy-done.1
  18.2 0.0 copy-done.4
  18.2 0.0 copy-done.7
  18.3 0.0 copy-done.8
  18.3 3.4 %own.1 = (f32[2,30,8,128]{3,2,1,0:T(8,128)S(1)}, f32[2,10,24,8,128]{4,3,2,1,0:T(8,128)S(1)}, f32[2,10,24,8,128]{4,3,2,1,0:T(8,128)S(1)}, f32[8,16,8,128]{3,2,1,0...) custom-call(f32[2]{0:T(128)S(1)} %copy-done.8, ...), custom_call_target="tpu_custom_call" | custom-call | flops 1000 | bytes 1000 | tf_op jit(solution)/shard_map/own/pallas_call | solution.py:539
  21.7 0.0 collective-permute-done.from_before
  21.7 0.0 copy-start.6
  21.7 1.7 %upper.1 = (f32[8,24,8,128]{3,2,1,0:T(8,128)S(1)}, f32[1536,512]{1,0:T(8,128)S(1)}, f32[8,16,8,128]{3,2,1,0:T(8,128)S(1)}, f32[2,20,8,128]{3,2,1,0:T(8,128)S(1)}) custom-call(f32[8,24,8,128]{3,2,1,0:T(8,128)S(1)} %get-tuple-element.20.rows_in, f32[1536,512]{1,0:T(8,128)S(1)} %get-tuple-element.21.powers_in, f32[2,24,8,128]{3,2,1,0:T(8,128)S(1)} %get-tuple-element.22.slow_in, ...), custom_call_target="tpu_custom_call" | custom-call | flops 1000 | bytes 1000 | tf_op jit(solution)/shard_map/upper/pallas_call | solution.py:567
  23.4 4.0 %collective-permute-done.1.from_after = f32[68,8,128]{2,1,0:T(8,128)S(1)} collective-permute-done((f32[68,8,128]{2,1,0:T(8,128)S(1)}, f32[68,8,128]{2,1,0:T(8,128)S(1)}, u32[]{:S(2)}, u32[]{:S(2)}) %collective-permute-start.1) | collective-permute-done | bytes 278560 | tf_op jit(solution)/shard_map/ppermute | solution.py:481
  27.4 0.0 copy-done.6
  27.4 2.9 %lower.1 = (f32[4,2,24,256]{3,2,1,0:T(8,128)S(1)}, f32[2,2,24,1024]{3,2,1,0:T(8,128)}) custom-call(s32[8]{0:T(128)S(1)} %copy-done.6, f32[8,24,8,128]{3,2,1,0:T(8,128)S(1)} %get-tuple-element.20.rows_in, f32[1536,512]{1,0:T(8,128)S(1)} %get-tuple-element.21.powers_in, f32[2,24,8,128]{3,2,1,0:T(8,128)S(1)} %get-tuple-element.22.slow_in, ...), custom_call_target="tpu_custom_call" | custom-call | flops 1000 | bytes 1000 | tf_op jit(solution)/shard_map/lower/pallas_call | solution.py:579
  30.4 7.9 %all_to_all.5 = f32[4,2,24,256]{3,2,1,0:T(8,128)S(1)} all-to-all(f32[4,2,24,256]{3,2,1,0:T(8,128)S(1)} %get-tuple-element.36), channel_id=1, replica_groups=mesh['tile'=8,'freq'=4] {'freq'}, dimensions={0} | all-to-all | bytes 393216 | tf_op jit(solution)/shard_map/all_to_all | solution.py:601
  38.3 0.6 %reduce_sum.9 = f32[2,24,256]{2,1,0:T(8,128)} reduce(f32[4,2,24,256]{3,2,1,0:T(8,128)S(1)} %all_to_all.5, f32[]{:T(128)} %constant.1.clone.1), dimensions={0}, to_apply=%region_0.0 | reduce | flops 36864 | bytes 245764 | tf_op jit(solution)/shard_map/reduce_sum | solution.py:602
  (6 shorter events, 0.0 us)
Async XLA Ops:
  0.6 17.6 %copy-start.1 = (bf16[256,512]{1,0:T(8,128)(2,1)S(1)}, bf16[256,512]{1,0:T(8,128)(2,1)}, u32[]{:S(2)}) copy-start(bf16[256,512]{1,0:T(8,128)(2,1)} %constant.4.clone.y_matrix) | copy-start | bytes 786436
  7.8 1.0 %copy-start.2 = (f32[2,2,24,1024]{3,2,1,0:T(8,128)S(1)}, f32[2,2,24,1024]{3,2,1,0:T(8,128)}, u32[]{:S(2)}) copy-start(f32[2,2,24,1024]{3,2,1,0:T(8,128)} %source.3) | copy-start | bytes 1179652
  8.8 1.0 %copy-start.3 = (f32[2,2,24,1024]{3,2,1,0:T(8,128)S(1)}, f32[2,2,24,1024]{3,2,1,0:T(8,128)}, u32[]{:S(2)}) copy-start(f32[2,2,24,1024]{3,2,1,0:T(8,128)} %receiver.3) | copy-start | bytes 1179652
  9.8 0.7 %copy-start.5 = (s32[8]{0:T(128)S(1)}, s32[8]{0:T(128)}, u32[]{:S(2)}) copy-start(s32[8]{0:T(128)} %aperture.3) | copy-start | bytes 100
  10.5 7.8 %copy-start.4 = (f32[2,5,3]{1,0,2:T(2,128)S(1)}, f32[2,5,3]{1,0,2:T(2,128)}, u32[]{:S(2)}) copy-start(f32[2,5,3]{1,0,2:T(2,128)} %param.13) | copy-start | bytes 364
  10.5 7.8 %copy-start.7 = (s32[2,2]{1,0:T(2,128)S(1)}, s32[2,2]{1,0:T(2,128)}, u32[]{:S(2)}) copy-start(s32[2,2]{1,0:T(2,128)} %order_table.1) | copy-start | bytes 52
  10.5 7.8 %copy-start.8 = (f32[2]{0:T(128)S(1)}, f32[2]{0:T(128)}, u32[]{:S(2)}) copy-start(f32[2]{0:T(128)} %frequency.1) | copy-start | bytes 28
  11.2 10.5 %collective-permute-start = (f32[68,8,128]{2,1,0:T(8,128)S(1)}, f32[68,8,128]{2,1,0:T(8,128)S(1)}, u32[]{:S(2)}, u32[]{:S(2)}) collective-permute-start(f32[68,8,128]{2,1,0:T(8,128)S(1)} %ahead.1), channel_id=1, source_target_pairs={{0,4},{4,8},{8,12},{12,16},{16,20},{20,24},{24,28},{1,5},{5,9},{9,... | collective-permute-start | bytes 835592 | tf_op jit(solution)/shard_map/ppermute | solution.py:481
  14.8 1.0 %copy-start = (bf16[256,512]{1,0:T(8,128)(2,1)S(1)}, bf16[256,512]{1,0:T(8,128)(2,1)}, u32[]{:S(2)}) copy-start(bf16[256,512]{1,0:T(8,128)(2,1)} %constant.4.clone.y_matrix) | copy-start | bytes 786436
  16.9 10.5 %collective-permute-start.1 = (f32[68,8,128]{2,1,0:T(8,128)S(1)}, f32[68,8,128]{2,1,0:T(8,128)S(1)}, u32[]{:S(2)}, u32[]{:S(2)}) collective-permute-start(f32[68,8,128]{2,1,0:T(8,128)S(1)} %get-tuple-element.35), channel_id=1, source_target_pairs={{4,0},{8,4},{12,8},{16,12},{20,16},{24,20},{28,24},{5,1},{9,5},{13... | collective-permute-start | bytes 835592 | tf_op jit(solution)/shard_map/ppermute | solution.py:481
  21.7 5.8 %copy-start.6 = (s32[8]{0:T(128)S(1)}, s32[8]{0:T(128)}, u32[]{:S(2)}) copy-start(s32[8]{0:T(128)} %aperture.3) | copy-start | bytes 100

commit v8 on v7

--- a/solution.py
+++ b/solution.py
@@ -113,7 +113,7 @@
         store(part, value)
 
 
-def sweep(freqs, fields, power, coefficient, write, partial, rows):
+def sweep(freqs, fields, power, coefficient, write, partial, rows, which=(0, 1)):
     def feed(held, value):
         kept = []
         for last in held:
@@ -122,7 +122,7 @@
         return kept, value
 
     for freq in range(freqs):
-        for field in range(2):
+        for field in which:
             for part in range(2):
                 p = (2 * field + part) * freqs + freq
                 held = []
@@ -364,7 +364,7 @@
     aperture, rows_in, powers_in, slow_in, weights, first_in, later,
     middle_in, middle_powers_in, last_in, images_in, y_matrix, from_after,
     image_out, receiver_hbm,
-    receiver_out, sem,
+    receiver_out, sems,
     flat, edges, left, edge_powers, slow, first, middle, last, images, partial,
 ):
     tile = lax.axis_index("tile")
@@ -430,17 +430,20 @@
     for p in range(2 * freqs, count):
         last[p, pl.ds(0, inner)] = last_in[p]
     images[:, pl.ds(0, stored - ORDER)] = images_in[...]
-    sweep(
-        freqs,
-        lambda p, o: middle_in[p, o + width - ORDER] if o < ORDER else middle[p, o - ORDER],
-        lambda p, m, row: (
-            done(p, m, row + width - HALO) if row < HALO else outer(p, m, row - HALO)
-        ),
-        lambda freq, part, o: later[freq, part, o + width - HALO],
-        write_last,
-        partial,
-        HALO,
-    )
+
+    def finish(which):
+        sweep(
+            freqs,
+            lambda p, o: middle_in[p, o + width - ORDER] if o < ORDER else middle[p, o - ORDER],
+            lambda p, m, row: (
+                done(p, m, row + width - HALO) if row < HALO else outer(p, m, row - HALO)
+            ),
+            lambda freq, part, o: later[freq, part, o + width - HALO],
+            write_last,
+            partial,
+            HALO,
+            which,
+        )
 
     def put(slot, load_row, store_tile):
         for r in range(stored):
@@ -450,6 +453,8 @@
             for j in range(8):
                 store_tile(i, j, flat[slot, pl.ds((i * 8 + j) * 8, 8), :])
 
+    finish((1,))
+    sent = []
     for part in range(2):
         for freq in range(freqs):
             def store_receiver(i, j, value):
@@ -457,8 +462,15 @@
 
             p = (2 + part) * freqs + freq
             put(NDEPTH + part * freqs + freq, lambda r: last[p, r], store_receiver)
-    sent = pltpu.make_async_copy(receiver_out, receiver_hbm, sem)
-    sent.start()
+            sent.append(
+                pltpu.make_async_copy(
+                    receiver_out.at[part, freq],
+                    receiver_hbm.at[part, freq],
+                    sems.at[part * freqs + freq],
+                )
+            )
+            sent[-1].start()
+    finish((0,))
 
     for k in range(ORDER):
         images[0, width - ORDER + k] = image_row(freqs, lambda p: middle[p, k])
@@ -472,7 +484,8 @@
             ] = value
 
         put(depth, lambda r: images[depth, r], store_image)
-    sent.wait()
+    for copy in sent:
+        copy.wait()
 
 
 def passed_along(value, axis, steps):
@@ -586,7 +599,7 @@
         out_specs=(VMEM, pl.BlockSpec(memory_space=pl.ANY)),
         scratch_shapes=[
             same(receiver_field),
-            pltpu.SemaphoreType.DMA,
+            pltpu.SemaphoreType.DMA((2 * freqs,)),
             pltpu.VMEM((NDEPTH + 2 * freqs, stored * 8, 128), F32),
             *edge,
             scratch(count, HALO),

time: 39.5 us -> 39.5 us (level)
  no operation moved by 1% of the time
where the time goes in v8:
time: 39.5 us; the launch traced here: 38.9 us
  blocking collectives  15.1 us (38%)
  Pallas kernels  9.82 us (25%)
  starting transfers between devices  4.95 us (13%)
  waiting for transfers between devices  4.04 us (10%)
  local copies, waits for them, and re-layouts  3.62 us (9%)
  between operations  0.75 us (2%)
  other arithmetic  0.63 us (2%)
    all_to_all x1, blocking collectives, shards(): exchanged = lax.all_to_all(image_parts, 'freq', 0, 0)  7.89 us
    all_gather x1, blocking collectives, shards(): planes = lax.all_gather(slowness, 'freq', axis=0)  7.18 us
    ppermute x2, starting transfers between devices, passed_along(): lax.ppermute(value, axis, [(source, source + steps) for source in range(i...  4.95 us
    ppermute x2, waiting for transfers between devices, passed_along(): lax.ppermute(value, axis, [(source, source + steps) for source in range(i...  4.04 us
    unnamed x18, local copies, waits for them, and re-layouts  3.62 us
    pallas_call x1, Pallas kernels, shards(): kernel(own_kernel, (rows(freqs, terms), rows(freqs, parts, stored), rows(...  3.39 us
    pallas_call x1, Pallas kernels, shards(): pl.pallas_call(lower_kernel, out_shape=(shape(lax.axis_size('freq'), *slo...  2.89 us
    pallas_call x1, Pallas kernels, shards(): kernel(upper_kernel, (rows(count, stored), shape(count * stored * 8, wide...  1.73 us
  transfers between devices with their start and end apart: 2, of which 1 were waited for; matrix products, arithmetic and copies ran while one was open for 0% of the time, Pallas kernels for 16%

profile of v8, /device:TPU:0, one launch (start us, length us, event | category | flops | bytes accessed | tf_op | source)
XLA Modules:
  0.0 38.9 jit_solution(7980880035168481346)
XLA Ops:
  0.6 0.0 copy-start.1
  0.6 7.2 %all-gather = f32[8,24,256]{2,1,0:T(8,128)S(1)} all-gather(f32[2,24,256]{2,1,0:T(8,128)} %param.10), channel_id=2, replica_groups=mesh['tile'=8,'freq'=4] {'freq'}, dimensions={0}, use_global_device_ids=true | all-gather | bytes 245760 | tf_op jit(solution)/shard_map/all_gather | solution.py:529
  7.8 1.0 %copy-done.2 = f32[2,2,24,1024]{3,2,1,0:T(8,128)S(1)} copy-done((f32[2,2,24,1024]{3,2,1,0:T(8,128)S(1)}, f32[2,2,24,1024]{3,2,1,0:T(8,128)}, u32[]{:S(2)}) %copy-start.2) | copy-done | bytes 393240
  8.8 1.0 %copy-done.3 = f32[2,2,24,1024]{3,2,1,0:T(8,128)S(1)} copy-done((f32[2,2,24,1024]{3,2,1,0:T(8,128)S(1)}, f32[2,2,24,1024]{3,2,1,0:T(8,128)}, u32[]{:S(2)}) %copy-start.3) | copy-done | bytes 393240
  9.8 0.7 %copy-done.5 = s32[8]{0:T(128)S(1)} copy-done((s32[8]{0:T(128)S(1)}, s32[8]{0:T(128)}, u32[]{:S(2)}) %copy-start.5) | copy-done | bytes 56
  10.5 0.7 %ahead.1 = f32[68,8,128]{2,1,0:T(8,128)S(1)} custom-call(s32[8]{0:T(128)S(1)} %copy-done.5, f32[2,2,24,1024]{3,2,1,0:T(8,128)S(1)} %copy-done.2, f32[2,2,24,1024]{3,2,1,0:T(8,128)S(1)} %copy-done.3, f32[4,2,24,256]{3,2,1,0:T(8,128)S(1)} %bitcast.2), custom_call_target="tpu_custom_call" | custom-call | flops 1000 | bytes 1000 | tf_op jit(solution)/shard_map/ahead/pallas_call | solution.py:532
  11.2 3.7 %collective-permute-start = (f32[68,8,128]{2,1,0:T(8,128)S(1)}, f32[68,8,128]{2,1,0:T(8,128)S(1)}, u32[]{:S(2)}, u32[]{:S(2)}) collective-permute-start(f32[68,8,128]{2,1,0:T(8,128)S(1)} %ahead.1), channel_id=1, source_target_pairs={{0,4},{4,8},{8,12},{12,16},{16,20},{20,24},{24,28},{1,5},{5,9},{9,... | collective-permute-start | bytes 835592 | tf_op jit(solution)/shard_map/ppermute | solution.py:494
  14.8 0.0 copy-start
  14.8 0.9 %copy-done = bf16[256,512]{1,0:T(8,128)(2,1)S(1)} copy-done((bf16[256,512]{1,0:T(8,128)(2,1)S(1)}, bf16[256,512]{1,0:T(8,128)(2,1)}, u32[]{:S(2)}) %copy-start) | copy-done | bytes 262168
  15.8 1.1 %rows.1 = (f32[68,8,128]{2,1,0:T(8,128)S(1)}, f32[8,24,8,128]{3,2,1,0:T(8,128)S(1)}, f32[1536,512]{1,0:T(8,128)S(1)}, f32[2,24,8,128]{3,2,1,0:T(8,128)S(1)}) custom-call(f32[2,2,24,1024]{3,2,1,0:T(8,128)S(1)} %copy-done.2, f32[2,2,24,1024]{3,2,1,0:T(8,128)S(1)} %copy-done.3, f32[4,2,24,256]{3,2,1,0:T(8,128)S(1)} %bitcast.3, bf16[256,512]{1,0:T(8,128)(2,1)S(1)} %copy-done), custom_call_target="tpu_custom_call" | custom-call | flops 1000 | bytes 1000 | tf_op jit(solution)/shard_map/rows/pallas_call | solution.py:538
  16.9 1.3 %collective-permute-start.1 = (f32[68,8,128]{2,1,0:T(8,128)S(1)}, f32[68,8,128]{2,1,0:T(8,128)S(1)}, u32[]{:S(2)}, u32[]{:S(2)}) collective-permute-start(f32[68,8,128]{2,1,0:T(8,128)S(1)} %get-tuple-element.35), channel_id=1, source_target_pairs={{4,0},{8,4},{12,8},{16,12},{20,16},{24,20},{28,24},{5,1},{9,5},{13... | collective-permute-start | bytes 835592 | tf_op jit(solution)/shard_map/ppermute | solution.py:494
  18.2 0.0 copy-done.1
  18.2 0.0 copy-done.4
  18.2 0.0 copy-done.7
  18.3 0.0 copy-done.8
  18.3 3.4 %own.1 = (f32[2,30,8,128]{3,2,1,0:T(8,128)S(1)}, f32[2,10,24,8,128]{4,3,2,1,0:T(8,128)S(1)}, f32[2,10,24,8,128]{4,3,2,1,0:T(8,128)S(1)}, f32[8,16,8,128]{3,2,1,0...) custom-call(f32[2]{0:T(128)S(1)} %copy-done.8, ...), custom_call_target="tpu_custom_call" | custom-call | flops 1000 | bytes 1000 | tf_op jit(solution)/shard_map/own/pallas_call | solution.py:552
  21.7 0.0 collective-permute-done.from_before
  21.7 0.0 copy-start.6
  21.7 1.7 %upper.1 = (f32[8,24,8,128]{3,2,1,0:T(8,128)S(1)}, f32[1536,512]{1,0:T(8,128)S(1)}, f32[8,16,8,128]{3,2,1,0:T(8,128)S(1)}, f32[2,20,8,128]{3,2,1,0:T(8,128)S(1)}) custom-call(f32[8,24,8,128]{3,2,1,0:T(8,128)S(1)} %get-tuple-element.20.rows_in, f32[1536,512]{1,0:T(8,128)S(1)} %get-tuple-element.21.powers_in, f32[2,24,8,128]{3,2,1,0:T(8,128)S(1)} %get-tuple-element.22.slow_in, ...), custom_call_target="tpu_custom_call" | custom-call | flops 1000 | bytes 1000 | tf_op jit(solution)/shard_map/upper/pallas_call | solution.py:580
  23.4 4.0 %collective-permute-done.1.from_after = f32[68,8,128]{2,1,0:T(8,128)S(1)} collective-permute-done((f32[68,8,128]{2,1,0:T(8,128)S(1)}, f32[68,8,128]{2,1,0:T(8,128)S(1)}, u32[]{:S(2)}, u32[]{:S(2)}) %collective-permute-start.1) | collective-permute-done | bytes 278560 | tf_op jit(solution)/shard_map/ppermute | solution.py:494
  27.4 0.0 copy-done.6
  27.4 2.9 %lower.1 = (f32[4,2,24,256]{3,2,1,0:T(8,128)S(1)}, f32[2,2,24,1024]{3,2,1,0:T(8,128)}) custom-call(s32[8]{0:T(128)S(1)} %copy-done.6, f32[8,24,8,128]{3,2,1,0:T(8,128)S(1)} %get-tuple-element.20.rows_in, f32[1536,512]{1,0:T(8,128)S(1)} %get-tuple-element.21.powers_in, f32[2,24,8,128]{3,2,1,0:T(8,128)S(1)} %get-tuple-element.22.slow_in, ...), custom_call_target="tpu_custom_call" | custom-call | flops 1000 | bytes 1000 | tf_op jit(solution)/shard_map/lower/pallas_call | solution.py:592
  30.3 7.9 %all_to_all.5 = f32[4,2,24,256]{3,2,1,0:T(8,128)S(1)} all-to-all(f32[4,2,24,256]{3,2,1,0:T(8,128)S(1)} %get-tuple-element.36), channel_id=1, replica_groups=mesh['tile'=8,'freq'=4] {'freq'}, dimensions={0} | all-to-all | bytes 393216 | tf_op jit(solution)/shard_map/all_to_all | solution.py:614
  38.2 0.6 %reduce_sum.9 = f32[2,24,256]{2,1,0:T(8,128)} reduce(f32[4,2,24,256]{3,2,1,0:T(8,128)S(1)} %all_to_all.5, f32[]{:T(128)} %constant.1.clone.1), dimensions={0}, to_apply=%region_0.0 | reduce | flops 36864 | bytes 245764 | tf_op jit(solution)/shard_map/reduce_sum | solution.py:615
  (6 shorter events, 0.0 us)
Async XLA Ops:
  0.6 17.6 %copy-start.1 = (bf16[256,512]{1,0:T(8,128)(2,1)S(1)}, bf16[256,512]{1,0:T(8,128)(2,1)}, u32[]{:S(2)}) copy-start(bf16[256,512]{1,0:T(8,128)(2,1)} %constant.4.clone.y_matrix) | copy-start | bytes 786436
  7.8 1.0 %copy-start.2 = (f32[2,2,24,1024]{3,2,1,0:T(8,128)S(1)}, f32[2,2,24,1024]{3,2,1,0:T(8,128)}, u32[]{:S(2)}) copy-start(f32[2,2,24,1024]{3,2,1,0:T(8,128)} %source.3) | copy-start | bytes 1179652
  8.8 1.0 %copy-start.3 = (f32[2,2,24,1024]{3,2,1,0:T(8,128)S(1)}, f32[2,2,24,1024]{3,2,1,0:T(8,128)}, u32[]{:S(2)}) copy-start(f32[2,2,24,1024]{3,2,1,0:T(8,128)} %receiver.3) | copy-start | bytes 1179652
  9.8 0.7 %copy-start.5 = (s32[8]{0:T(128)S(1)}, s32[8]{0:T(128)}, u32[]{:S(2)}) copy-start(s32[8]{0:T(128)} %aperture.3) | copy-start | bytes 100
  10.5 7.8 %copy-start.4 = (f32[2,5,3]{1,0,2:T(2,128)S(1)}, f32[2,5,3]{1,0,2:T(2,128)}, u32[]{:S(2)}) copy-start(f32[2,5,3]{1,0,2:T(2,128)} %param.13) | copy-start | bytes 364
  10.5 7.8 %copy-start.7 = (s32[2,2]{1,0:T(2,128)S(1)}, s32[2,2]{1,0:T(2,128)}, u32[]{:S(2)}) copy-start(s32[2,2]{1,0:T(2,128)} %order_table.1) | copy-start | bytes 52
  10.5 7.8 %copy-start.8 = (f32[2]{0:T(128)S(1)}, f32[2]{0:T(128)}, u32[]{:S(2)}) copy-start(f32[2]{0:T(128)} %frequency.1) | copy-start | bytes 28
  11.2 10.5 %collective-permute-start = (f32[68,8,128]{2,1,0:T(8,128)S(1)}, f32[68,8,128]{2,1,0:T(8,128)S(1)}, u32[]{:S(2)}, u32[]{:S(2)}) collective-permute-start(f32[68,8,128]{2,1,0:T(8,128)S(1)} %ahead.1), channel_id=1, source_target_pairs={{0,4},{4,8},{8,12},{12,16},{16,20},{20,24},{24,28},{1,5},{5,9},{9,... | collective-permute-start | bytes 835592 | tf_op jit(solution)/shard_map/ppermute | solution.py:494
  14.8 1.0 %copy-start = (bf16[256,512]{1,0:T(8,128)(2,1)S(1)}, bf16[256,512]{1,0:T(8,128)(2,1)}, u32[]{:S(2)}) copy-start(bf16[256,512]{1,0:T(8,128)(2,1)} %constant.4.clone.y_matrix) | copy-start | bytes 786436
  16.9 10.5 %collective-permute-start.1 = (f32[68,8,128]{2,1,0:T(8,128)S(1)}, f32[68,8,128]{2,1,0:T(8,128)S(1)}, u32[]{:S(2)}, u32[]{:S(2)}) collective-permute-start(f32[68,8,128]{2,1,0:T(8,128)S(1)} %get-tuple-element.35), channel_id=1, source_target_pairs={{4,0},{8,4},{12,8},{16,12},{20,16},{24,20},{28,24},{5,1},{9,5},{13... | collective-permute-start | bytes 835592 | tf_op jit(solution)/shard_map/ppermute | solution.py:494
  21.7 5.8 %copy-start.6 = (s32[8]{0:T(128)S(1)}, s32[8]{0:T(128)}, u32[]{:S(2)}) copy-start(s32[8]{0:T(128)} %aperture.3) | copy-start | bytes 100

commit v9 on v8

--- a/solution.py
+++ b/solution.py
@@ -92,16 +92,23 @@
     ]
 
 
-def ahead_kernel(aperture, source, receiver, planes, ahead, *flats):
+def slow_kernel(planes, out, flat):
+    row_tiles = planes.shape[2] // 8
+    for depth in range(NDEPTH):
+        to_rows(flat.at[depth], slow_tile(planes, depth), row_tiles)
+        for r in range(planes.shape[2]):
+            out[depth, r] = row_of(flat.at[depth], r)
+
+
+def ahead_kernel(aperture, source, receiver, slow, ahead, *flats):
     width = aperture[lax.axis_index("tile")]
     row_tiles = source.shape[2] // 8
-    count = 4 * source.shape[1]
-    for plane, load in enumerate(planes_of(source, receiver) + [slow_tile(planes, 0)]):
+    for plane, load in enumerate(planes_of(source, receiver)):
         to_rows(flats[plane], load, row_tiles)
-    for plane in range(count + 1):
-        rows = HALO if plane < count else ORDER
-        for k in range(rows):
-            ahead[plane * HALO + k] = row_of(flats[plane], width - rows + k)
+        for k in range(HALO):
+            ahead[plane * HALO + k] = row_of(flats[plane], width - HALO + k)
+    end = 4 * source.shape[1] * HALO
+    ahead[pl.ds(end, ORDER)] = slow[0, pl.ds(width - ORDER, ORDER)]
 
 
 def coefficients(weights, freq, slow_row, store):
@@ -175,7 +182,7 @@
 
 
 def rows_kernel(
-    source, receiver, planes, y_matrix, behind, rows_out, powers_out, slow_out, flat, left
+    source, receiver, slow, y_matrix, behind, rows_out, powers_out, flat, left
 ):
     freqs, stored = source.shape[1:3]
     count = 4 * freqs
@@ -184,13 +191,9 @@
         to_rows(flat.at[plane], load, row_tiles)
         for r in range(stored):
             rows_out[plane, r] = row_of(flat.at[plane], r)
-    for depth in range(NDEPTH):
-        to_rows(flat.at[depth], slow_tile(planes, depth), row_tiles)
-        for r in range(stored):
-            slow_out[depth, r] = row_of(flat.at[depth], r)
     for plane in range(count):
         behind[pl.ds(plane * HALO, HALO)] = rows_out[plane, pl.ds(0, HALO)]
-    behind[pl.ds(count * HALO, ORDER)] = slow_out[0, pl.ds(0, ORDER)]
+    behind[pl.ds(count * HALO, ORDER)] = slow[0, pl.ds(0, ORDER)]
     for plane in range(count):
         split_rows(rows_out[plane], left, plane * stored * 8)
     powers_out[...] = multiply(left, count * stored * 8, y_matrix)
@@ -494,7 +497,7 @@
     return lax.ppermute(value, axis, [(source, source + steps) for source in range(initial, last)])
 
 
-def kernel(body, out_shape, in_specs, scratch, name):
+def kernel(body, out_shape, in_specs, scratch, name, cost=1000):
     return pl.pallas_call(
         body,
         out_shape=out_shape,
@@ -502,7 +505,7 @@
         out_specs=(VMEM,) * len(out_shape),
         scratch_shapes=scratch,
         compiler_params=pltpu.CompilerParams(vmem_limit_bytes=24 << 20),
-        cost_estimate=pl.CostEstimate(flops=1000, bytes_accessed=1000, transcendentals=0),
+        cost_estimate=pl.CostEstimate(flops=cost, bytes_accessed=cost, transcendentals=0),
         name=name,
     )
 
@@ -529,22 +532,30 @@
     planes = lax.all_gather(slowness, "freq", axis=0)
     halo = rows(count * HALO + ORDER)
     flat = pltpu.VMEM((stored * 8, 128), F32)
+    (slow,) = kernel(
+        slow_kernel,
+        (rows(NDEPTH, stored),),
+        [VMEM],
+        [pltpu.VMEM((NDEPTH, stored * 8, 128), F32)],
+        "slow",
+        1 << 30,
+    )(planes)
     (ahead,) = kernel(
-        ahead_kernel, (halo,), [SMEM] + [VMEM] * 3, [flat] * (count + 1), "ahead"
-    )(aperture, source_field, receiver_field, planes)
+        ahead_kernel, (halo,), [SMEM] + [VMEM] * 3, [flat] * count, "ahead"
+    )(aperture, source_field, receiver_field, slow)
     from_before = passed_along(ahead, "tile", 1)
 
     y_matrix = jnp.asarray(y_weights(), BF16)
-    behind, own_rows, own_powers, slow = kernel(
+    behind, own_rows, own_powers = kernel(
         rows_kernel,
-        (halo, rows(count, stored), shape(count * stored * 8, wide), rows(NDEPTH, stored)),
+        (halo, rows(count, stored), shape(count * stored * 8, wide)),
         [VMEM] * 4,
         [
             pltpu.VMEM((count, stored * 8, 128), F32),
             pltpu.VMEM((count * stored * 8, 512), BF16),
         ],
         "rows",
-    )(source_field, receiver_field, planes, y_matrix)
+    )(source_field, receiver_field, slow, y_matrix)
     from_after = passed_along(behind, "tile", -1)
 
     coeffs = jnp.transpose(filter_coeffs, (2, 0, 1))

time: 39.5 us -> 38.1 us (0.965); the launches traced: 38.9 us -> 37.9 us
  local copies, waits for them, and re-layouts: 3.62 us -> 0.04 us
  waiting for transfers between devices: 4.04 us -> 6.58 us
    unnamed x18 -> x14, local copies, waits for them, and re-layouts: 3.62 us -> 0.04 us
    ppermute x2, waiting for transfers between devices: 4.04 us -> 6.58 us  [passed_along(): lax.ppermute(value, axis, [(source, source + steps) for source in range(i...]
where the time goes in v9:
time: 38.1 us; the launch traced here: 37.9 us
  blocking collectives  15.1 us (40%)
  Pallas kernels  9.81 us (26%)
  waiting for transfers between devices  6.58 us (17%)
  starting transfers between devices  4.95 us (13%)
  between operations  0.8 us (2%)
  other arithmetic  0.63 us (2%)
    all_to_all x1, blocking collectives, shards(): exchanged = lax.all_to_all(image_parts, 'freq', 0, 0)  7.9 us
    all_gather x1, blocking collectives, shards(): planes = lax.all_gather(slowness, 'freq', axis=0)  7.18 us
    ppermute x2, waiting for transfers between devices, passed_along(): lax.ppermute(value, axis, [(source, source + steps) for source in range(i...  6.58 us
    ppermute x2, starting transfers between devices, passed_along(): lax.ppermute(value, axis, [(source, source + steps) for source in range(i...  4.95 us
    pallas_call x1, Pallas kernels, shards(): kernel(own_kernel, (rows(freqs, terms), rows(freqs, parts, stored), rows(...  3.33 us
    pallas_call x1, Pallas kernels, shards(): pl.pallas_call(lower_kernel, out_shape=(shape(lax.axis_size('freq'), *slo...  2.96 us
    pallas_call x1, Pallas kernels, shards(): kernel(upper_kernel, (rows(count, stored), shape(count * stored * 8, wide...  1.69 us
    pallas_call x1, Pallas kernels, shards(): kernel(rows_kernel, (halo, rows(count, stored), shape(count * stored * 8,...  1.1 us
  transfers between devices with their start and end apart: 2, of which 1 were waited for; matrix products, arithmetic and copies ran while one was open for 0% of the time, Pallas kernels for 16%

profile of v9, /device:TPU:0, one launch (start us, length us, event | category | flops | bytes accessed | tf_op | source)
XLA Modules:
  0.0 37.9 jit_solution(8999915737923580355)
XLA Ops:
  0.6 0.0 copy-start.4
  0.6 0.0 copy-start.2
  0.7 0.0 copy-start.1
  0.7 7.2 %all-gather = f32[8,24,256]{2,1,0:T(8,128)S(1)} all-gather(f32[2,24,256]{2,1,0:T(8,128)} %param.10), channel_id=2, replica_groups=mesh['tile'=8,'freq'=4] {'freq'}, dimensions={0}, use_global_device_ids=true | all-gather | bytes 245760 | tf_op jit(solution)/shard_map/all_gather | solution.py:532
  7.8 0.1 slow.1.slow_in
  7.9 0.0 copy-done.4
  7.9 0.0 copy-done.2
  7.9 0.0 copy-done.1
  7.9 0.0 copy-start.3
  7.9 0.0 copy-start.5
  8.0 0.0 copy-start.6
  8.0 0.7 %ahead.1 = f32[68,8,128]{2,1,0:T(8,128)S(1)} custom-call(s32[8]{0:T(128)S(1)} %copy-done.4, f32[2,2,24,1024]{3,2,1,0:T(8,128)S(1)} %copy-done.1, f32[2,2,24,1024]{3,2,1,0:T(8,128)S(1)} %copy-done.2, f32[2,24,8,128]{3,2,1,0:T(8,128)S(1)} %slow.1.slow_in), custom_call_target="tpu_custom_call" | custom-call | flops 1000 | bytes 1000 | tf_op jit(solution)/shard_map/ahead/pallas_call | solution.py:543
  8.6 3.7 %collective-permute-start = (f32[68,8,128]{2,1,0:T(8,128)S(1)}, f32[68,8,128]{2,1,0:T(8,128)S(1)}, u32[]{:S(2)}, u32[]{:S(2)}) collective-permute-start(f32[68,8,128]{2,1,0:T(8,128)S(1)} %ahead.1), channel_id=1, source_target_pairs={{0,4},{4,8},{8,12},{12,16},{16,20},{20,24},{24,28},{1,5},{5,9},{9,... | collective-permute-start | bytes 835592 | tf_op jit(solution)/shard_map/ppermute | solution.py:497
  12.3 0.0 copy-done
  12.3 1.1 %rows.1 = (f32[68,8,128]{2,1,0:T(8,128)S(1)}, f32[8,24,8,128]{3,2,1,0:T(8,128)S(1)}, f32[1536,512]{1,0:T(8,128)S(1)}) custom-call(f32[2,2,24,1024]{3,2,1,0:T(8,128)S(1)} %copy-done.1, f32[2,2,24,1024]{3,2,1,0:T(8,128)S(1)} %copy-done.2, f32[2,24,8,128]{3,2,1,0:T(8,128)S(1)} %slow.1.slow_in, bf16[256,512]{1,0:T(8,128)(2,1)S(1)} %copy-done), custom_call_target="tpu_custom_call" | custom-call | flops 1000 | bytes 1000 | tf_op jit(solution)/shard_map/rows/pallas_call | solution.py:549
  13.4 1.3 %collective-permute-start.1 = (f32[68,8,128]{2,1,0:T(8,128)S(1)}, f32[68,8,128]{2,1,0:T(8,128)S(1)}, u32[]{:S(2)}, u32[]{:S(2)}) collective-permute-start(f32[68,8,128]{2,1,0:T(8,128)S(1)} %get-tuple-element.33), channel_id=1, source_target_pairs={{4,0},{8,4},{12,8},{16,12},{20,16},{24,20},{28,24},{5,1},{9,5},{13... | collective-permute-start | bytes 835592 | tf_op jit(solution)/shard_map/ppermute | solution.py:497
  14.7 0.0 copy-done.3
  14.8 3.3 %own.1 = (f32[2,30,8,128]{3,2,1,0:T(8,128)S(1)}, f32[2,10,24,8,128]{4,3,2,1,0:T(8,128)S(1)}, f32[2,10,24,8,128]{4,3,2,1,0:T(8,128)S(1)}, f32[8,16,8,128]{3,2,1,0...) custom-call(f32[2]{0:T(128)S(1)} %copy-done.6, ...), custom_call_target="tpu_custom_call" | custom-call | flops 1000 | bytes 1000 | tf_op jit(solution)/shard_map/own/pallas_call | solution.py:563
  18.1 6.6 %collective-permute-done.from_before = f32[68,8,128]{2,1,0:T(8,128)S(1)} collective-permute-done((f32[68,8,128]{2,1,0:T(8,128)S(1)}, f32[68,8,128]{2,1,0:T(8,128)S(1)}, u32[]{:S(2)}, u32[]{:S(2)}) %collective-permute-start) | collective-permute-done | bytes 278560 | tf_op jit(solution)/shard_map/ppermute | solution.py:497
  24.7 1.7 %upper.1 = (f32[8,24,8,128]{3,2,1,0:T(8,128)S(1)}, f32[1536,512]{1,0:T(8,128)S(1)}, f32[8,16,8,128]{3,2,1,0:T(8,128)S(1)}, f32[2,20,8,128]{3,2,1,0:T(8,128)S(1)}) custom-call(f32[8,24,8,128]{3,2,1,0:T(8,128)S(1)} %get-tuple-element.19.rows_in, f32[1536,512]{1,0:T(8,128)S(1)} %get-tuple-element.20.powers_in, f32[2,24,8,128]{3,2,1,0:T(8,128)S(1)} %slow.1.slow_in, ...), custom_call_target="tpu_custom_call" | custom-call | flops 1000 | bytes 1000 | tf_op jit(solution)/shard_map/upper/pallas_call | solution.py:591
  26.4 0.0 collective-permute-done.1.from_after
  26.4 3.0 %lower.1 = (f32[4,2,24,256]{3,2,1,0:T(8,128)S(1)}, f32[2,2,24,1024]{3,2,1,0:T(8,128)}) custom-call(s32[8]{0:T(128)S(1)} %copy-done.4, f32[8,24,8,128]{3,2,1,0:T(8,128)S(1)} %get-tuple-element.19.rows_in, f32[1536,512]{1,0:T(8,128)S(1)} %get-tuple-element.20.powers_in, f32[2,24,8,128]{3,2,1,0:T(8,128)S(1)} %slow.1.slow_in, ...), custom_call_target="tpu_custom_call" | custom-call | flops 1000 | bytes 1000 | tf_op jit(solution)/shard_map/lower/pallas_call | solution.py:603
  29.3 7.9 %all_to_all.5 = f32[4,2,24,256]{3,2,1,0:T(8,128)S(1)} all-to-all(f32[4,2,24,256]{3,2,1,0:T(8,128)S(1)} %get-tuple-element.34), channel_id=1, replica_groups=mesh['tile'=8,'freq'=4] {'freq'}, dimensions={0} | all-to-all | bytes 393216 | tf_op jit(solution)/shard_map/all_to_all | solution.py:625
  37.2 0.6 %reduce_sum.9 = f32[2,24,256]{2,1,0:T(8,128)} reduce(f32[4,2,24,256]{3,2,1,0:T(8,128)S(1)} %all_to_all.5, f32[]{:T(128)} %constant.1.clone.1), dimensions={0}, to_apply=%region_0.0 | reduce | flops 36864 | bytes 245764 | tf_op jit(solution)/shard_map/reduce_sum | solution.py:626
  (3 shorter events, 0.0 us)
Async XLA Ops:
  0.6 7.3 %copy-start.4 = (s32[8]{0:T(128)S(1)}, s32[8]{0:T(128)}, u32[]{:S(2)}) copy-start(s32[8]{0:T(128)} %aperture.3) | copy-start | bytes 100
  0.6 7.3 %copy-start.2 = (f32[2,2,24,1024]{3,2,1,0:T(8,128)S(1)}, f32[2,2,24,1024]{3,2,1,0:T(8,128)}, u32[]{:S(2)}) copy-start(f32[2,2,24,1024]{3,2,1,0:T(8,128)} %receiver.3) | copy-start | bytes 1179652
  0.7 7.3 %copy-start.1 = (f32[2,2,24,1024]{3,2,1,0:T(8,128)S(1)}, f32[2,2,24,1024]{3,2,1,0:T(8,128)}, u32[]{:S(2)}) copy-start(f32[2,2,24,1024]{3,2,1,0:T(8,128)} %source.3) | copy-start | bytes 1179652
  7.8 4.5 %copy-start = (bf16[256,512]{1,0:T(8,128)(2,1)S(1)}, bf16[256,512]{1,0:T(8,128)(2,1)}, u32[]{:S(2)}) copy-start(bf16[256,512]{1,0:T(8,128)(2,1)} %constant.4.clone.y_matrix) | copy-start | bytes 786436
  7.9 6.8 %copy-start.3 = (f32[2,5,3]{1,0,2:T(2,128)S(1)}, f32[2,5,3]{1,0,2:T(2,128)}, u32[]{:S(2)}) copy-start(f32[2,5,3]{1,0,2:T(2,128)} %param.13) | copy-start | bytes 364
  7.9 6.8 %copy-start.5 = (s32[2,2]{1,0:T(2,128)S(1)}, s32[2,2]{1,0:T(2,128)}, u32[]{:S(2)}) copy-start(s32[2,2]{1,0:T(2,128)} %order_table.1) | copy-start | bytes 52
  8.0 6.8 %copy-start.6 = (f32[2]{0:T(128)S(1)}, f32[2]{0:T(128)}, u32[]{:S(2)}) copy-start(f32[2]{0:T(128)} %frequency.1) | copy-start | bytes 28
  8.6 16.0 %collective-permute-start = (f32[68,8,128]{2,1,0:T(8,128)S(1)}, f32[68,8,128]{2,1,0:T(8,128)S(1)}, u32[]{:S(2)}, u32[]{:S(2)}) collective-permute-start(f32[68,8,128]{2,1,0:T(8,128)S(1)} %ahead.1), channel_id=1, source_target_pairs={{0,4},{4,8},{8,12},{12,16},{16,20},{20,24},{24,28},{1,5},{5,9},{9,... | collective-permute-start | bytes 835592 | tf_op jit(solution)/shard_map/ppermute | solution.py:497
  13.4 12.9 %collective-permute-start.1 = (f32[68,8,128]{2,1,0:T(8,128)S(1)}, f32[68,8,128]{2,1,0:T(8,128)S(1)}, u32[]{:S(2)}, u32[]{:S(2)}) collective-permute-start(f32[68,8,128]{2,1,0:T(8,128)S(1)} %get-tuple-element.33), channel_id=1, source_target_pairs={{4,0},{8,4},{12,8},{16,12},{20,16},{24,20},{28,24},{5,1},{9,5},{13... | collective-permute-start | bytes 835592 | tf_op jit(solution)/shard_map/ppermute | solution.py:497

commit v10 on v9

--- a/solution.py
+++ b/solution.py
@@ -182,7 +182,7 @@
 
 
 def rows_kernel(
-    source, receiver, slow, y_matrix, behind, rows_out, powers_out, flat, left
+    source, receiver, y_matrix, rows_out, powers_out, flat, left
 ):
     freqs, stored = source.shape[1:3]
     count = 4 * freqs
@@ -192,21 +192,21 @@
         for r in range(stored):
             rows_out[plane, r] = row_of(flat.at[plane], r)
     for plane in range(count):
-        behind[pl.ds(plane * HALO, HALO)] = rows_out[plane, pl.ds(0, HALO)]
-    behind[pl.ds(count * HALO, ORDER)] = slow[0, pl.ds(0, ORDER)]
-    for plane in range(count):
         split_rows(rows_out[plane], left, plane * stored * 8)
     powers_out[...] = multiply(left, count * stored * 8, y_matrix)
 
 
 def own_kernel(
     frequency, order_table, filter_coeffs, rows_in, powers_in, slow_in, y_matrix,
-    weights_out, first_out, later_out,
+    behind, weights_out, first_out, later_out,
     middle_out, middle_powers_out, last_out, first_image, last_image,
     left, later_weights, partial,
 ):
     count, stored = rows_in.shape[:2]
     freqs = count // 4
+    for plane in range(count):
+        behind[pl.ds(plane * HALO, HALO)] = rows_in[plane, pl.ds(0, HALO)]
+    behind[pl.ds(count * HALO, ORDER)] = slow_in[0, pl.ds(0, ORDER)]
     powers = filter_coeffs.shape[0]
     for depth, weights in enumerate((weights_out, later_weights)):
         for freq in range(freqs):
@@ -546,23 +546,23 @@
     from_before = passed_along(ahead, "tile", 1)
 
     y_matrix = jnp.asarray(y_weights(), BF16)
-    behind, own_rows, own_powers = kernel(
+    own_rows, own_powers = kernel(
         rows_kernel,
-        (halo, rows(count, stored), shape(count * stored * 8, wide)),
-        [VMEM] * 4,
+        (rows(count, stored), shape(count * stored * 8, wide)),
+        [VMEM] * 3,
         [
             pltpu.VMEM((count, stored * 8, 128), F32),
             pltpu.VMEM((count * stored * 8, 512), BF16),
         ],
         "rows",
-    )(source_field, receiver_field, slow, y_matrix)
-    from_after = passed_along(behind, "tile", -1)
+    )(source_field, receiver_field, y_matrix)
 
     coeffs = jnp.transpose(filter_coeffs, (2, 0, 1))
     terms = parts * coeffs.shape[0]
-    weights, first, later, *inside = kernel(
+    behind, weights, first, later, *inside = kernel(
         own_kernel,
         (
+            halo,
             rows(freqs, terms),
             rows(freqs, parts, stored),
             rows(freqs, parts, stored),
@@ -580,6 +580,7 @@
         ],
         "own",
     )(frequency, order_table, coeffs, own_rows, own_powers, slow, y_matrix)
+    from_after = passed_along(behind, "tile", -1)
     edge = [
         scratch(count, HALO),
         pltpu.VMEM((count * HALO * 8, 512), BF16),

time: 38.1 us -> 39 us (1.024)
  waiting for transfers between devices: 6.58 us -> 7.61 us
    ppermute x2, waiting for transfers between devices: 6.58 us -> 7.61 us  [passed_along(): lax.ppermute(value, axis, [(source, source + steps) for source in range(i...]
  transfers between devices with their start and end apart: 2 -> 2, of which waited for: 1 -> 2; matrix products, arithmetic and copies ran while one was open for 0% -> 0% of each run, Pallas kernels for 16% -> 16%
where the time goes in v10:
time: 39 us; the launch traced here: 38.7 us
  blocking collectives  15.1 us (39%)
  Pallas kernels  9.64 us (25%)
  waiting for transfers between devices  7.61 us (20%)
  starting transfers between devices  4.95 us (13%)
  between operations  0.79 us (2%)
  other arithmetic  0.63 us (2%)
    all_to_all x1, blocking collectives, shards(): exchanged = lax.all_to_all(image_parts, 'freq', 0, 0)  7.89 us
    ppermute x2, waiting for transfers between devices, passed_along(): lax.ppermute(value, axis, [(source, source + steps) for source in range(i...  7.61 us
    all_gather x1, blocking collectives, shards(): planes = lax.all_gather(slowness, 'freq', axis=0)  7.18 us
    ppermute x2, starting transfers between devices, passed_along(): lax.ppermute(value, axis, [(source, source + steps) for source in range(i...  4.95 us
    pallas_call x1, Pallas kernels, shards(): kernel(own_kernel, (halo, rows(freqs, terms), rows(freqs, parts, stored),...  3.34 us
    pallas_call x1, Pallas kernels, shards(): pl.pallas_call(lower_kernel, out_shape=(shape(lax.axis_size('freq'), *slo...  2.87 us
    pallas_call x1, Pallas kernels, shards(): kernel(upper_kernel, (rows(count, stored), shape(count * stored * 8, wide...  1.61 us
    pallas_call x1, Pallas kernels, shards(): kernel(rows_kernel, (rows(count, stored), shape(count * stored * 8, wide)...  1.09 us
  transfers between devices with their start and end apart: 2, of which 2 were waited for; matrix products, arithmetic and copies ran while one was open for 0% of the time, Pallas kernels for 16%

profile of v10, /device:TPU:0, one launch (start us, length us, event | category | flops | bytes accessed | tf_op | source)
XLA Modules:
  0.0 38.7 jit_solution(3281661235071918048)
XLA Ops:
  0.6 0.0 copy-start.4
  0.6 0.0 copy-start.2
  0.7 0.0 copy-start.1
  0.7 7.2 %all-gather = f32[8,24,256]{2,1,0:T(8,128)S(1)} all-gather(f32[2,24,256]{2,1,0:T(8,128)} %param.10), channel_id=2, replica_groups=mesh['tile'=8,'freq'=4] {'freq'}, dimensions={0}, use_global_device_ids=true | all-gather | bytes 245760 | tf_op jit(solution)/shard_map/all_gather | solution.py:532
  7.8 0.1 slow.1.slow_in
  7.9 0.0 copy-done.4
  7.9 0.0 copy-done.2
  7.9 0.0 copy-done.1
  7.9 0.0 copy-start.3
  7.9 0.0 copy-start.5
  8.0 0.0 copy-start.6
  8.0 0.7 %ahead.1 = f32[68,8,128]{2,1,0:T(8,128)S(1)} custom-call(s32[8]{0:T(128)S(1)} %copy-done.4, f32[2,2,24,1024]{3,2,1,0:T(8,128)S(1)} %copy-done.1, f32[2,2,24,1024]{3,2,1,0:T(8,128)S(1)} %copy-done.2, f32[2,24,8,128]{3,2,1,0:T(8,128)S(1)} %slow.1.slow_in), custom_call_target="tpu_custom_call" | custom-call | flops 1000 | bytes 1000 | tf_op jit(solution)/shard_map/ahead/pallas_call | solution.py:543
  8.6 3.7 %collective-permute-start = (f32[68,8,128]{2,1,0:T(8,128)S(1)}, f32[68,8,128]{2,1,0:T(8,128)S(1)}, u32[]{:S(2)}, u32[]{:S(2)}) collective-permute-start(f32[68,8,128]{2,1,0:T(8,128)S(1)} %ahead.1), channel_id=1, source_target_pairs={{0,4},{4,8},{8,12},{12,16},{16,20},{20,24},{24,28},{1,5},{5,9},{9,... | collective-permute-start | bytes 835592 | tf_op jit(solution)/shard_map/ppermute | solution.py:497
  12.3 0.0 copy-done
  12.3 1.1 %rows.1 = (f32[8,24,8,128]{3,2,1,0:T(8,128)S(1)}, f32[1536,512]{1,0:T(8,128)S(1)}) custom-call(f32[2,2,24,1024]{3,2,1,0:T(8,128)S(1)} %copy-done.1, f32[2,2,24,1024]{3,2,1,0:T(8,128)S(1)} %copy-done.2, bf16[256,512]{1,0:T(8,128)(2,1)S(1)} %copy-done), custom_call_target="tpu_custom_call" | custom-call | flops 1000 | bytes 1000 | tf_op jit(solution)/shard_map/rows/pallas_call | solution.py:549
  13.4 0.0 copy-done.3
  13.4 3.3 %own.1 = (f32[68,8,128]{2,1,0:T(8,128)S(1)}, f32[2,30,8,128]{3,2,1,0:T(8,128)S(1)}, f32[2,10,24,8,128]{4,3,2,1,0:T(8,128)S(1)}, f32[2,10,24,8,128]{4,3,2,1,0:T(8...) custom-call(f32[2]{0:T(128)S(1)} %copy-done.6, ...), custom_call_target="tpu_custom_call" | custom-call | flops 1000 | bytes 1000 | tf_op jit(solution)/shard_map/own/pallas_call | solution.py:562
  16.8 1.3 %collective-permute-start.1 = (f32[68,8,128]{2,1,0:T(8,128)S(1)}, f32[68,8,128]{2,1,0:T(8,128)S(1)}, u32[]{:S(2)}, u32[]{:S(2)}) collective-permute-start(f32[68,8,128]{2,1,0:T(8,128)S(1)} %get-tuple-element.33), channel_id=1, source_target_pairs={{4,0},{8,4},{12,8},{16,12},{20,16},{24,20},{28,24},{5,1},{9,5},{13... | collective-permute-start | bytes 835592 | tf_op jit(solution)/shard_map/ppermute | solution.py:497
  18.1 0.6 %collective-permute-done.from_before = f32[68,8,128]{2,1,0:T(8,128)S(1)} collective-permute-done((f32[68,8,128]{2,1,0:T(8,128)S(1)}, f32[68,8,128]{2,1,0:T(8,128)S(1)}, u32[]{:S(2)}, u32[]{:S(2)}) %collective-permute-start) | collective-permute-done | bytes 278560 | tf_op jit(solution)/shard_map/ppermute | solution.py:497
  18.7 1.6 %upper.1 = (f32[8,24,8,128]{3,2,1,0:T(8,128)S(1)}, f32[1536,512]{1,0:T(8,128)S(1)}, f32[8,16,8,128]{3,2,1,0:T(8,128)S(1)}, f32[2,20,8,128]{3,2,1,0:T(8,128)S(1)}) custom-call(f32[8,24,8,128]{3,2,1,0:T(8,128)S(1)} %get-tuple-element.19.rows_in, f32[1536,512]{1,0:T(8,128)S(1)} %get-tuple-element.20.powers_in, f32[2,24,8,128]{3,2,1,0:T(8,128)S(1)} %slow.1.slow_in, ...), custom_call_target="tpu_custom_call" | custom-call | flops 1000 | bytes 1000 | tf_op jit(solution)/shard_map/upper/pallas_call | solution.py:592
  20.3 7.0 %collective-permute-done.1.from_after = f32[68,8,128]{2,1,0:T(8,128)S(1)} collective-permute-done((f32[68,8,128]{2,1,0:T(8,128)S(1)}, f32[68,8,128]{2,1,0:T(8,128)S(1)}, u32[]{:S(2)}, u32[]{:S(2)}) %collective-permute-start.1) | collective-permute-done | bytes 278560 | tf_op jit(solution)/shard_map/ppermute | solution.py:497
  27.3 2.9 %lower.1 = (f32[4,2,24,256]{3,2,1,0:T(8,128)S(1)}, f32[2,2,24,1024]{3,2,1,0:T(8,128)}) custom-call(s32[8]{0:T(128)S(1)} %copy-done.4, f32[8,24,8,128]{3,2,1,0:T(8,128)S(1)} %get-tuple-element.19.rows_in, f32[1536,512]{1,0:T(8,128)S(1)} %get-tuple-element.20.powers_in, f32[2,24,8,128]{3,2,1,0:T(8,128)S(1)} %slow.1.slow_in, ...), custom_call_target="tpu_custom_call" | custom-call | flops 1000 | bytes 1000 | tf_op jit(solution)/shard_map/lower/pallas_call | solution.py:604
  30.2 7.9 %all_to_all.5 = f32[4,2,24,256]{3,2,1,0:T(8,128)S(1)} all-to-all(f32[4,2,24,256]{3,2,1,0:T(8,128)S(1)} %get-tuple-element.34), channel_id=1, replica_groups=mesh['tile'=8,'freq'=4] {'freq'}, dimensions={0} | all-to-all | bytes 393216 | tf_op jit(solution)/shard_map/all_to_all | solution.py:626
  38.1 0.6 %reduce_sum.9 = f32[2,24,256]{2,1,0:T(8,128)} reduce(f32[4,2,24,256]{3,2,1,0:T(8,128)S(1)} %all_to_all.5, f32[]{:T(128)} %constant.1.clone.1), dimensions={0}, to_apply=%region_0.0 | reduce | flops 36864 | bytes 245764 | tf_op jit(solution)/shard_map/reduce_sum | solution.py:627
  (3 shorter events, 0.0 us)
Async XLA Ops:
  0.6 7.3 %copy-start.4 = (s32[8]{0:T(128)S(1)}, s32[8]{0:T(128)}, u32[]{:S(2)}) copy-start(s32[8]{0:T(128)} %aperture.3) | copy-start | bytes 100
  0.6 7.3 %copy-start.2 = (f32[2,2,24,1024]{3,2,1,0:T(8,128)S(1)}, f32[2,2,24,1024]{3,2,1,0:T(8,128)}, u32[]{:S(2)}) copy-start(f32[2,2,24,1024]{3,2,1,0:T(8,128)} %receiver.3) | copy-start | bytes 1179652
  0.7 7.3 %copy-start.1 = (f32[2,2,24,1024]{3,2,1,0:T(8,128)S(1)}, f32[2,2,24,1024]{3,2,1,0:T(8,128)}, u32[]{:S(2)}) copy-start(f32[2,2,24,1024]{3,2,1,0:T(8,128)} %source.3) | copy-start | bytes 1179652
  7.8 4.5 %copy-start = (bf16[256,512]{1,0:T(8,128)(2,1)S(1)}, bf16[256,512]{1,0:T(8,128)(2,1)}, u32[]{:S(2)}) copy-start(bf16[256,512]{1,0:T(8,128)(2,1)} %constant.4.clone.y_matrix) | copy-start | bytes 786436
  7.9 5.5 %copy-start.3 = (f32[2,5,3]{1,0,2:T(2,128)S(1)}, f32[2,5,3]{1,0,2:T(2,128)}, u32[]{:S(2)}) copy-start(f32[2,5,3]{1,0,2:T(2,128)} %param.13) | copy-start | bytes 364
  7.9 5.5 %copy-start.5 = (s32[2,2]{1,0:T(2,128)S(1)}, s32[2,2]{1,0:T(2,128)}, u32[]{:S(2)}) copy-start(s32[2,2]{1,0:T(2,128)} %order_table.1) | copy-start | bytes 52
  8.0 5.5 %copy-start.6 = (f32[2]{0:T(128)S(1)}, f32[2]{0:T(128)}, u32[]{:S(2)}) copy-start(f32[2]{0:T(128)} %frequency.1) | copy-start | bytes 28
  8.6 10.1 %collective-permute-start = (f32[68,8,128]{2,1,0:T(8,128)S(1)}, f32[68,8,128]{2,1,0:T(8,128)S(1)}, u32[]{:S(2)}, u32[]{:S(2)}) collective-permute-start(f32[68,8,128]{2,1,0:T(8,128)S(1)} %ahead.1), channel_id=1, source_target_pairs={{0,4},{4,8},{8,12},{12,16},{16,20},{20,24},{24,28},{1,5},{5,9},{9,... | collective-permute-start | bytes 835592 | tf_op jit(solution)/shard_map/ppermute | solution.py:497
  16.8 10.5 %collective-permute-start.1 = (f32[68,8,128]{2,1,0:T(8,128)S(1)}, f32[68,8,128]{2,1,0:T(8,128)S(1)}, u32[]{:S(2)}, u32[]{:S(2)}) collective-permute-start(f32[68,8,128]{2,1,0:T(8,128)S(1)} %get-tuple-element.33), channel_id=1, source_target_pairs={{4,0},{8,4},{12,8},{16,12},{20,16},{24,20},{28,24},{5,1},{9,5},{13... | collective-permute-start | bytes 835592 | tf_op jit(solution)/shard_map/ppermute | solution.py:497

commit v11 on v9

--- a/solution.py
+++ b/solution.py
@@ -182,8 +182,11 @@
 
 
 def rows_kernel(
-    source, receiver, slow, y_matrix, behind, rows_out, powers_out, flat, left
+    frequency, order_table, filter_coeffs, source, receiver, slow, y_matrix,
+    behind, rows_out, powers_out, weights_out, first_out, later_out,
+    flat, left, later_weights,
 ):
+    powers = filter_coeffs.shape[0]
     freqs, stored = source.shape[1:3]
     count = 4 * freqs
     row_tiles = stored // 8
@@ -198,16 +201,6 @@
         split_rows(rows_out[plane], left, plane * stored * 8)
     powers_out[...] = multiply(left, count * stored * 8, y_matrix)
 
-
-def own_kernel(
-    frequency, order_table, filter_coeffs, rows_in, powers_in, slow_in, y_matrix,
-    weights_out, first_out, later_out,
-    middle_out, middle_powers_out, last_out, first_image, last_image,
-    left, later_weights, partial,
-):
-    count, stored = rows_in.shape[:2]
-    freqs = count // 4
-    powers = filter_coeffs.shape[0]
     for depth, weights in enumerate((weights_out, later_weights)):
         for freq in range(freqs):
             omega = jnp.full((8, 128), frequency[freq], F32)
@@ -235,11 +228,19 @@
                 def store(part, value):
                     out[freq, part, r] = value
 
-                coefficients(weights, freq, slow_in[depth, r], store)
+                coefficients(weights, freq, slow[depth, r], store)
         return carry
 
     lax.fori_loop(0, stored, tables, 0, unroll=2)
 
+
+def own_kernel(
+    rows_in, powers_in, first_in, later_in, y_matrix,
+    middle_out, middle_powers_out, last_out, first_image, last_image,
+    left, partial,
+):
+    count, stored = rows_in.shape[:2]
+    freqs = count // 4
     inner = stored - 2 * ORDER
 
     def write_middle(p, o, value):
@@ -249,7 +250,7 @@
         freqs,
         lambda p, o: rows_in[p, o + ORDER],
         power_of(powers_in, stored),
-        lambda freq, part, o: first_out[freq, part, o + ORDER],
+        lambda freq, part, o: first_in[freq, part, o + ORDER],
         write_middle,
         partial,
         inner,
@@ -267,7 +268,7 @@
         freqs,
         lambda p, o: middle_out[p, o + ORDER],
         power_of(middle_powers_out, inner),
-        lambda freq, part, o: later_out[freq, part, o + HALO],
+        lambda freq, part, o: later_in[freq, part, o + HALO],
         write_last,
         partial,
         inner - 2 * ORDER,
@@ -546,40 +547,41 @@
     from_before = passed_along(ahead, "tile", 1)
 
     y_matrix = jnp.asarray(y_weights(), BF16)
-    behind, own_rows, own_powers = kernel(
+    coeffs = jnp.transpose(filter_coeffs, (2, 0, 1))
+    terms = parts * coeffs.shape[0]
+    behind, own_rows, own_powers, weights, first, later = kernel(
         rows_kernel,
-        (halo, rows(count, stored), shape(count * stored * 8, wide)),
-        [VMEM] * 4,
+        (
+            halo,
+            rows(count, stored),
+            shape(count * stored * 8, wide),
+            rows(freqs, terms),
+            rows(freqs, parts, stored),
+            rows(freqs, parts, stored),
+        ),
+        [SMEM] * 3 + [VMEM] * 4,
         [
             pltpu.VMEM((count, stored * 8, 128), F32),
             pltpu.VMEM((count * stored * 8, 512), BF16),
+            scratch(freqs, terms),
         ],
         "rows",
-    )(source_field, receiver_field, slow, y_matrix)
+    )(frequency, order_table, coeffs, source_field, receiver_field, slow, y_matrix)
     from_after = passed_along(behind, "tile", -1)
 
-    coeffs = jnp.transpose(filter_coeffs, (2, 0, 1))
-    terms = parts * coeffs.shape[0]
-    weights, first, later, *inside = kernel(
+    inside = kernel(
         own_kernel,
         (
-            rows(freqs, terms),
-            rows(freqs, parts, stored),
-            rows(freqs, parts, stored),
             rows(count, inner),
             shape(count * inner * 8, wide),
             rows(count, inner - HALO),
             rows(inner),
             rows(inner - HALO),
         ),
-        [SMEM] * 3 + [VMEM] * 4,
-        [
-            pltpu.VMEM((count * inner * 8, 512), BF16),
-            scratch(freqs, terms),
-            scratch(2, inner),
-        ],
+        [VMEM] * 5,
+        [pltpu.VMEM((count * inner * 8, 512), BF16), scratch(2, inner)],
         "own",
-    )(frequency, order_table, coeffs, own_rows, own_powers, slow, y_matrix)
+    )(own_rows, own_powers, first, later, y_matrix)
     edge = [
         scratch(count, HALO),
         pltpu.VMEM((count * HALO * 8, 512), BF16),

time: 38.1 us -> 37.1 us (0.974)
  waiting for transfers between devices: 6.58 us -> 5.6 us
    pallas_call x1, Pallas kernels: 1.1 us -> 2.57 us  [shards(): kernel(rows_kernel, (halo, rows(count, stored), shape(count * stored * 8,...]
    pallas_call x1, Pallas kernels: 3.33 us -> 1.92 us  [shards(): kernel(own_kernel, (rows(count, inner), shape(count * inner * 8, wide), r...]
    ppermute x2, waiting for transfers between devices: 6.58 us -> 5.6 us  [passed_along(): lax.ppermute(value, axis, [(source, source + steps) for source in range(i...]
  transfers between devices with their start and end apart: 2 -> 2, of which waited for: 1 -> 2; matrix products, arithmetic and copies ran while one was open for 0% -> 0% of each run, Pallas kernels for 16% -> 17%
where the time goes in v11:
time: 37.1 us; the launch traced here: 36.9 us
  blocking collectives  15.1 us (41%)
  Pallas kernels  9.84 us (27%)
  waiting for transfers between devices  5.6 us (15%)
  starting transfers between devices  4.95 us (13%)
  between operations  0.77 us (2%)
  other arithmetic  0.63 us (2%)
    all_to_all x1, blocking collectives, shards(): exchanged = lax.all_to_all(image_parts, 'freq', 0, 0)  7.9 us
    all_gather x1, blocking collectives, shards(): planes = lax.all_gather(slowness, 'freq', axis=0)  7.18 us
    ppermute x2, waiting for transfers between devices, passed_along(): lax.ppermute(value, axis, [(source, source + steps) for source in range(i...  5.6 us
    ppermute x2, starting transfers between devices, passed_along(): lax.ppermute(value, axis, [(source, source + steps) for source in range(i...  4.95 us
    pallas_call x1, Pallas kernels, shards(): pl.pallas_call(lower_kernel, out_shape=(shape(lax.axis_size('freq'), *slo...  2.94 us
    pallas_call x1, Pallas kernels, shards(): kernel(rows_kernel, (halo, rows(count, stored), shape(count * stored * 8,...  2.57 us
    pallas_call x1, Pallas kernels, shards(): kernel(own_kernel, (rows(count, inner), shape(count * inner * 8, wide), r...  1.92 us
    pallas_call x1, Pallas kernels, shards(): kernel(upper_kernel, (rows(count, stored), shape(count * stored * 8, wide...  1.69 us
  transfers between devices with their start and end apart: 2, of which 2 were waited for; matrix products, arithmetic and copies ran while one was open for 0% of the time, Pallas kernels for 17%

profile of v11, /device:TPU:0, one launch (start us, length us, event | category | flops | bytes accessed | tf_op | source)
XLA Modules:
  0.0 36.9 jit_solution(13045014683273939517)
XLA Ops:
  0.6 0.0 copy-start.4
  0.6 0.0 copy-start.2
  0.7 0.0 copy-start.1
  0.7 7.2 %all-gather = f32[8,24,256]{2,1,0:T(8,128)S(1)} all-gather(f32[2,24,256]{2,1,0:T(8,128)} %param.10), channel_id=2, replica_groups=mesh['tile'=8,'freq'=4] {'freq'}, dimensions={0}, use_global_device_ids=true | all-gather | bytes 245760 | tf_op jit(solution)/shard_map/all_gather | solution.py:533
  7.8 0.0 copy-start
  7.9 0.1 slow.1.slow_in
  7.9 0.0 copy-done.4
  7.9 0.0 copy-done.2
  7.9 0.0 copy-done.1
  7.9 0.7 %ahead.1 = f32[68,8,128]{2,1,0:T(8,128)S(1)} custom-call(s32[8]{0:T(128)S(1)} %copy-done.4, f32[2,2,24,1024]{3,2,1,0:T(8,128)S(1)} %copy-done.1, f32[2,2,24,1024]{3,2,1,0:T(8,128)S(1)} %copy-done.2, f32[2,24,8,128]{3,2,1,0:T(8,128)S(1)} %slow.1.slow_in), custom_call_target="tpu_custom_call" | custom-call | flops 1000 | bytes 1000 | tf_op jit(solution)/shard_map/ahead/pallas_call | solution.py:544
  8.6 3.7 %collective-permute-start = (f32[68,8,128]{2,1,0:T(8,128)S(1)}, f32[68,8,128]{2,1,0:T(8,128)S(1)}, u32[]{:S(2)}, u32[]{:S(2)}) collective-permute-start(f32[68,8,128]{2,1,0:T(8,128)S(1)} %ahead.1), channel_id=1, source_target_pairs={{0,4},{4,8},{8,12},{12,16},{16,20},{20,24},{24,28},{1,5},{5,9},{9,... | collective-permute-start | bytes 835592 | tf_op jit(solution)/shard_map/ppermute | solution.py:498
  12.3 0.0 copy-done
  12.3 0.0 copy-done.3
  12.3 0.0 copy-done.5
  12.3 0.0 copy-done.6
  12.3 2.6 %rows.1 = (f32[68,8,128]{2,1,0:T(8,128)S(1)}, f32[8,24,8,128]{3,2,1,0:T(8,128)S(1)}, f32[1536,512]{1,0:T(8,128)S(1)}, f32[2,30,8,128]{3,2,1,0:T(8,128)S(1)}, f32...) custom-call(f32[2]{0:T(128)S(1)} %copy-done.6, s32[2,2]{1,0:T(2,128)S(1)} %copy-done.5, ...), custom_call_target="tpu_custom_call" | custom-call | flops 1000 | bytes 1000 | tf_op jit(solution)/shard_map/rows/pallas_call | solution.py:552
  14.9 1.3 %collective-permute-start.1 = (f32[68,8,128]{2,1,0:T(8,128)S(1)}, f32[68,8,128]{2,1,0:T(8,128)S(1)}, u32[]{:S(2)}, u32[]{:S(2)}) collective-permute-start(f32[68,8,128]{2,1,0:T(8,128)S(1)} %get-tuple-element.33), channel_id=1, source_target_pairs={{4,0},{8,4},{12,8},{16,12},{20,16},{24,20},{28,24},{5,1},{9,5},{13... | collective-permute-start | bytes 835592 | tf_op jit(solution)/shard_map/ppermute | solution.py:498
  16.2 1.9 %own.1 = (f32[8,16,8,128]{3,2,1,0:T(8,128)S(1)}, f32[1024,512]{1,0:T(8,128)S(1)}, f32[8,8,8,128]{3,2,1,0:T(8,128)S(1)}, f32[16,8,128]{2,1,0:T(8,128)S(1)}, f32[8,8,128]{2,1,0:T(8,128)S(1)}) custom-call(f32[8,24,8,128]{3,2,1,0:T(8,128)S(1)} %get-tuple-element.19.rows_in, f32[1536,512]{1,0:T(8,128)S(1)} %get-tuple-element.20.powers_in, ...), custom_call_target="tpu_custom_call" | custom-call | flops 1000 | bytes 1000 | tf_op jit(solution)/shard_map/own/pallas_call | solution.py:572
  18.1 0.5 %collective-permute-done.from_before = f32[68,8,128]{2,1,0:T(8,128)S(1)} collective-permute-done((f32[68,8,128]{2,1,0:T(8,128)S(1)}, f32[68,8,128]{2,1,0:T(8,128)S(1)}, u32[]{:S(2)}, u32[]{:S(2)}) %collective-permute-start) | collective-permute-done | bytes 278560 | tf_op jit(solution)/shard_map/ppermute | solution.py:498
  18.7 1.7 %upper.1 = (f32[8,24,8,128]{3,2,1,0:T(8,128)S(1)}, f32[1536,512]{1,0:T(8,128)S(1)}, f32[8,16,8,128]{3,2,1,0:T(8,128)S(1)}, f32[2,20,8,128]{3,2,1,0:T(8,128)S(1)}) custom-call(f32[8,24,8,128]{3,2,1,0:T(8,128)S(1)} %get-tuple-element.19.rows_in, f32[1536,512]{1,0:T(8,128)S(1)} %get-tuple-element.20.powers_in, f32[2,24,8,128]{3,2,1,0:T(8,128)S(1)} %slow.1.slow_in, ...), custom_call_target="tpu_custom_call" | custom-call | flops 1000 | bytes 1000 | tf_op jit(solution)/shard_map/upper/pallas_call | solution.py:593
  20.4 5.0 %collective-permute-done.1.from_after = f32[68,8,128]{2,1,0:T(8,128)S(1)} collective-permute-done((f32[68,8,128]{2,1,0:T(8,128)S(1)}, f32[68,8,128]{2,1,0:T(8,128)S(1)}, u32[]{:S(2)}, u32[]{:S(2)}) %collective-permute-start.1) | collective-permute-done | bytes 278560 | tf_op jit(solution)/shard_map/ppermute | solution.py:498
  25.4 2.9 %lower.1 = (f32[4,2,24,256]{3,2,1,0:T(8,128)S(1)}, f32[2,2,24,1024]{3,2,1,0:T(8,128)}) custom-call(s32[8]{0:T(128)S(1)} %copy-done.4, f32[8,24,8,128]{3,2,1,0:T(8,128)S(1)} %get-tuple-element.19.rows_in, f32[1536,512]{1,0:T(8,128)S(1)} %get-tuple-element.20.powers_in, f32[2,24,8,128]{3,2,1,0:T(8,128)S(1)} %slow.1.slow_in, ...), custom_call_target="tpu_custom_call" | custom-call | flops 1000 | bytes 1000 | tf_op jit(solution)/shard_map/lower/pallas_call | solution.py:605
  28.4 7.9 %all_to_all.5 = f32[4,2,24,256]{3,2,1,0:T(8,128)S(1)} all-to-all(f32[4,2,24,256]{3,2,1,0:T(8,128)S(1)} %get-tuple-element.34), channel_id=1, replica_groups=mesh['tile'=8,'freq'=4] {'freq'}, dimensions={0} | all-to-all | bytes 393216 | tf_op jit(solution)/shard_map/all_to_all | solution.py:627
  36.3 0.6 %reduce_sum.9 = f32[2,24,256]{2,1,0:T(8,128)} reduce(f32[4,2,24,256]{3,2,1,0:T(8,128)S(1)} %all_to_all.5, f32[]{:T(128)} %constant.1.clone.1), dimensions={0}, to_apply=%region_0.0 | reduce | flops 36864 | bytes 245764 | tf_op jit(solution)/shard_map/reduce_sum | solution.py:628
  (3 shorter events, 0.0 us)
Async XLA Ops:
  0.6 7.3 %copy-start.4 = (s32[8]{0:T(128)S(1)}, s32[8]{0:T(128)}, u32[]{:S(2)}) copy-start(s32[8]{0:T(128)} %aperture.3) | copy-start | bytes 100
  0.6 7.3 %copy-start.2 = (f32[2,2,24,1024]{3,2,1,0:T(8,128)S(1)}, f32[2,2,24,1024]{3,2,1,0:T(8,128)}, u32[]{:S(2)}) copy-start(f32[2,2,24,1024]{3,2,1,0:T(8,128)} %receiver.3) | copy-start | bytes 1179652
  0.7 7.3 %copy-start.1 = (f32[2,2,24,1024]{3,2,1,0:T(8,128)S(1)}, f32[2,2,24,1024]{3,2,1,0:T(8,128)}, u32[]{:S(2)}) copy-start(f32[2,2,24,1024]{3,2,1,0:T(8,128)} %source.3) | copy-start | bytes 1179652
  7.8 4.4 %copy-start = (bf16[256,512]{1,0:T(8,128)(2,1)S(1)}, bf16[256,512]{1,0:T(8,128)(2,1)}, u32[]{:S(2)}) copy-start(bf16[256,512]{1,0:T(8,128)(2,1)} %constant.4.clone.y_matrix) | copy-start | bytes 786436
  7.8 4.5 %copy-start.3 = (f32[2,5,3]{1,0,2:T(2,128)S(1)}, f32[2,5,3]{1,0,2:T(2,128)}, u32[]{:S(2)}) copy-start(f32[2,5,3]{1,0,2:T(2,128)} %param.13) | copy-start | bytes 364
  7.8 4.5 %copy-start.5 = (s32[2,2]{1,0:T(2,128)S(1)}, s32[2,2]{1,0:T(2,128)}, u32[]{:S(2)}) copy-start(s32[2,2]{1,0:T(2,128)} %order_table.1) | copy-start | bytes 52
  7.8 4.5 %copy-start.6 = (f32[2]{0:T(128)S(1)}, f32[2]{0:T(128)}, u32[]{:S(2)}) copy-start(f32[2]{0:T(128)} %frequency.1) | copy-start | bytes 28
  8.6 10.1 %collective-permute-start = (f32[68,8,128]{2,1,0:T(8,128)S(1)}, f32[68,8,128]{2,1,0:T(8,128)S(1)}, u32[]{:S(2)}, u32[]{:S(2)}) collective-permute-start(f32[68,8,128]{2,1,0:T(8,128)S(1)} %ahead.1), channel_id=1, source_target_pairs={{0,4},{4,8},{8,12},{12,16},{16,20},{20,24},{24,28},{1,5},{5,9},{9,... | collective-permute-start | bytes 835592 | tf_op jit(solution)/shard_map/ppermute | solution.py:498
  14.9 10.5 %collective-permute-start.1 = (f32[68,8,128]{2,1,0:T(8,128)S(1)}, f32[68,8,128]{2,1,0:T(8,128)S(1)}, u32[]{:S(2)}, u32[]{:S(2)}) collective-permute-start(f32[68,8,128]{2,1,0:T(8,128)S(1)} %get-tuple-element.33), channel_id=1, source_target_pairs={{4,0},{8,4},{12,8},{16,12},{20,16},{24,20},{28,24},{5,1},{9,5},{13... | collective-permute-start | bytes 835592 | tf_op jit(solution)/shard_map/ppermute | solution.py:498

commit v12 on v11

--- a/solution.py
+++ b/solution.py
@@ -1,3 +1,4 @@
+import functools
 from math import comb
 
 import jax
@@ -182,11 +183,11 @@
 
 
 def rows_kernel(
-    frequency, order_table, filter_coeffs, source, receiver, slow, y_matrix,
-    behind, rows_out, powers_out, weights_out, first_out, later_out,
-    flat, left, later_weights,
+    frequency, order_table, filter_coeffs, source, receiver, slow, y_matrix, *others
 ):
     powers = filter_coeffs.shape[0]
+    behind, others = others[: source.shape[1]], others[source.shape[1] :]
+    rows_out, powers_out, weights_out, first_out, later_out, flat, left, later_weights = others
     freqs, stored = source.shape[1:3]
     count = 4 * freqs
     row_tiles = stored // 8
@@ -195,8 +196,8 @@
         for r in range(stored):
             rows_out[plane, r] = row_of(flat.at[plane], r)
     for plane in range(count):
-        behind[pl.ds(plane * HALO, HALO)] = rows_out[plane, pl.ds(0, HALO)]
-    behind[pl.ds(count * HALO, ORDER)] = slow[0, pl.ds(0, ORDER)]
+        behind[plane % freqs][pl.ds(plane // freqs * HALO, HALO)] = rows_out[plane, pl.ds(0, HALO)]
+    behind[0][pl.ds(4 * HALO, ORDER)] = slow[0, pl.ds(0, ORDER)]
     for plane in range(count):
         split_rows(rows_out[plane], left, plane * stored * 8)
     powers_out[...] = multiply(left, count * stored * 8, y_matrix)
@@ -364,90 +365,122 @@
         images[1, k] = image_row(freqs, lambda p: last[p, k])
 
 
-def lower_kernel(
-    aperture, rows_in, powers_in, slow_in, weights, first_in, later,
-    middle_in, middle_powers_in, last_in, images_in, y_matrix, from_after,
-    image_out, receiver_hbm,
-    receiver_out, sems,
-    flat, edges, left, edge_powers, slow, first, middle, last, images, partial,
+def lower_rows(
+    freq, width, last_tile, own, after, slow, edges, left, edge_powers, first, middle, last, partial
 ):
-    tile = lax.axis_index("tile")
-    width = aperture[tile]
+    rows_in, powers_in, weights, first_in, later, middle_in, middle_powers_in, y_matrix = own
     count, stored = rows_in.shape[:2]
     freqs = count // 4
-    row_tiles = stored // 8
-    inner = stored - 2 * ORDER
-
-    @pl.when(tile == lax.axis_size("tile") - 1)
+
+    @pl.when(last_tile)
     def _():
-        for p in range(count):
-            edges[p, 0] = jnp.zeros((8, 128), F32)
-            for k in range(1, HALO):
-                edges[p, k] = -rows_in[p, width - k]
-        slow[0] = slow_in[0, width - 1]
-        for k in range(1, ORDER):
-            slow[k] = slow_in[0, width - k]
-
-    @pl.when(tile < lax.axis_size("tile") - 1)
+        for k in range(4):
+            edges[k, 0] = jnp.zeros((8, 128), F32)
+            for r in range(1, HALO):
+                edges[k, r] = -rows_in[k * freqs + freq, width - r]
+
+    @pl.when(jnp.logical_not(last_tile))
     def _():
-        for p in range(count):
-            edges[p] = from_after[pl.ds(p * HALO, HALO)]
-        slow[...] = from_after[pl.ds(count * HALO, ORDER)]
-
-    for p in range(count):
-        split_rows(edges[p], left, p * HALO * 8)
-    edge_powers[...] = multiply(left, count * HALO * 8, y_matrix)
+        for k in range(4):
+            edges[k] = after[pl.ds(k * HALO, HALO)]
+
+    for k in range(4):
+        split_rows(edges[k], left, k * HALO * 8)
+    edge_powers[...] = multiply(left, 4 * HALO * 8, y_matrix)
     for r in range(ORDER):
-        for freq in range(freqs):
-            def store(part, value):
-                first[freq, part, r] = value
-
-            coefficients(weights, freq, slow[r], store)
+        def store(part, value):
+            first[part, r] = value
+
+        coefficients(weights, freq, slow[r], store)
 
     outer = power_of(edge_powers, HALO)
-    own = power_of(powers_in, stored)
+    inside = power_of(powers_in, stored)
     done = power_of(middle_powers_in, stored)
 
-    def write_middle(p, o, value):
-        middle[p, o] = value
+    def write_middle(k, o, value):
+        middle[k, o] = value
+
+    def write_last(k, o, value):
+        last[k, o] = value
 
     sweep(
-        freqs,
-        lambda p, o: rows_in[p, o + width - ORDER] if o < ORDER else edges[p, o - ORDER],
-        lambda p, m, row: (
-            own(p, m, row + width - HALO) if row < HALO else outer(p, m, row - HALO)
-        ),
-        lambda freq, part, o: (
-            first_in[freq, part, o + width - ORDER] if o < ORDER else first[freq, part, o - ORDER]
+        1,
+        lambda k, o: (
+            rows_in[k * freqs + freq, o + width - ORDER] if o < ORDER else edges[k, o - ORDER]
+        ),
+        lambda k, m, row: (
+            inside(k * freqs + freq, m, row + width - HALO)
+            if row < HALO
+            else outer(k, m, row - HALO)
+        ),
+        lambda _, part, o: (
+            first_in[freq, part, o + width - ORDER] if o < ORDER else first[part, o - ORDER]
         ),
         write_middle,
         partial,
         2 * ORDER,
     )
-    for p in range(count):
-        split_rows(middle[p], left, p * HALO * 8)
-    edge_powers[...] = multiply(left, count * HALO * 8, y_matrix)
-
-    def write_last(p, o, value):
-        last[p, o + width - HALO] = value
-
-    for p in range(2 * freqs, count):
-        last[p, pl.ds(0, inner)] = last_in[p]
-    images[:, pl.ds(0, stored - ORDER)] = images_in[...]
-
-    def finish(which):
-        sweep(
-            freqs,
-            lambda p, o: middle_in[p, o + width - ORDER] if o < ORDER else middle[p, o - ORDER],
-            lambda p, m, row: (
-                done(p, m, row + width - HALO) if row < HALO else outer(p, m, row - HALO)
-            ),
-            lambda freq, part, o: later[freq, part, o + width - HALO],
-            write_last,
-            partial,
-            HALO,
-            which,
-        )
+    for k in range(4):
+        split_rows(middle[k], left, k * HALO * 8)
+    edge_powers[...] = multiply(left, 4 * HALO * 8, y_matrix)
+    sweep(
+        1,
+        lambda k, o: (
+            middle_in[k * freqs + freq, o + width - ORDER] if o < ORDER else middle[k, o - ORDER]
+        ),
+        lambda k, m, row: (
+            done(k * freqs + freq, m, row + width - HALO)
+            if row < HALO
+            else outer(k, m, row - HALO)
+        ),
+        lambda _, part, o: later[freq, part, o + width - HALO],
+        write_last,
+        partial,
+        HALO,
+    )
+
+
+def lower_kernel(freq, aperture, slow_in, *refs):
+    own, refs = refs[:8], refs[8:]
+    tile = lax.axis_index("tile")
+    width = aperture[tile]
+    last_tile = tile == lax.axis_size("tile") - 1
+    if freq == 0:
+        after, receiver_rows, images, slow, *scratch = refs
+
+        @pl.when(last_tile)
+        def _():
+            slow[0] = slow_in[0, width - 1]
+            for k in range(1, ORDER):
+                slow[k] = slow_in[0, width - k]
+
+        @pl.when(jnp.logical_not(last_tile))
+        def _():
+            slow[...] = after[pl.ds(4 * HALO, ORDER)]
+    else:
+        after, slow, receiver_rows, images, *scratch = refs
+    lower_rows(freq, width, last_tile, own, after, slow, *scratch)
+    middle, last = scratch[4:6]
+    receiver_rows[...] = last[pl.ds(2, 2)]
+    for k in range(ORDER):
+        images[k] = image_row(1, lambda p: middle[p, k])
+    for k in range(HALO):
+        images[ORDER + k] = image_row(1, lambda p: last[p, k])
+
+
+def final_kernel(freq, aperture, slow, *refs):
+    own, refs = refs[:8], refs[8:]
+    after, last_in, images_in, *refs = refs
+    others, refs = refs[: 2 * freq], refs[2 * freq :]
+    image_out, receiver_hbm, receiver_out, sems, flat, rows, images, *scratch = refs
+    tile = lax.axis_index("tile")
+    width = aperture[tile]
+    lower_rows(freq, width, tile == lax.axis_size("tile") - 1, own, after, slow, *scratch)
+    middle, last = scratch[4:6]
+    count, inner = last_in.shape[:2]
+    freqs = count // 4
+    stored = own[0].shape[1]
+    row_tiles = stored // 8
 
     def put(slot, load_row, store_tile):
         for r in range(stored):
@@ -457,29 +490,35 @@
             for j in range(8):
                 store_tile(i, j, flat[slot, pl.ds((i * 8 + j) * 8, 8), :])
 
-    finish((1,))
     sent = []
     for part in range(2):
-        for freq in range(freqs):
+        for at in range(freqs):
             def store_receiver(i, j, value):
-                receiver_out[part, freq, pl.ds(8 * i, 8), pl.ds(128 * j, 128)] = value
-
-            p = (2 + part) * freqs + freq
-            put(NDEPTH + part * freqs + freq, lambda r: last[p, r], store_receiver)
+                receiver_out[part, at, pl.ds(8 * i, 8), pl.ds(128 * j, 128)] = value
+
+            p = part * freqs + at
+            rows[p, pl.ds(0, inner)] = last_in[2 * freqs + p]
+            rows[p, pl.ds(width - HALO, HALO)] = last[2 + part] if at == freq else others[2 * at][part]
+            put(NDEPTH + p, lambda r: rows[p, r], store_receiver)
             sent.append(
                 pltpu.make_async_copy(
-                    receiver_out.at[part, freq],
-                    receiver_hbm.at[part, freq],
-                    sems.at[part * freqs + freq],
+                    receiver_out.at[part, at], receiver_hbm.at[part, at], sems.at[p]
                 )
             )
             sent[-1].start()
-    finish((0,))
-
-    for k in range(ORDER):
-        images[0, width - ORDER + k] = image_row(freqs, lambda p: middle[p, k])
-    for k in range(HALO):
-        images[1, width - HALO + k] = image_row(freqs, lambda p: last[p, width - HALO + k])
+
+    images[:, pl.ds(0, stored - ORDER)] = images_in[...]
+    for k in range(ORDER + HALO):
+        if k < ORDER:
+            total = image_row(1, lambda p: middle[p, k])
+        else:
+            total = image_row(1, lambda p: last[p, k - ORDER])
+        for at in range(freq):
+            total = total + others[2 * at + 1][k]
+        if k < ORDER:
+            images[0, width - ORDER + k] = total
+        else:
+            images[1, width - HALO + k - ORDER] = total
     columns = image_out.shape[3]
     for depth in range(NDEPTH):
         def store_image(i, j, value):
@@ -549,10 +588,11 @@
     y_matrix = jnp.asarray(y_weights(), BF16)
     coeffs = jnp.transpose(filter_coeffs, (2, 0, 1))
     terms = parts * coeffs.shape[0]
-    behind, own_rows, own_powers, weights, first, later = kernel(
+    *behind, own_rows, own_powers, weights, first, later = kernel(
         rows_kernel,
         (
-            halo,
+            rows(4 * HALO + ORDER),
+            *[rows(4 * HALO)] * (freqs - 1),
             rows(count, stored),
             shape(count * stored * 8, wide),
             rows(freqs, terms),
@@ -567,7 +607,7 @@
         ],
         "rows",
     )(frequency, order_table, coeffs, source_field, receiver_field, slow, y_matrix)
-    from_after = passed_along(behind, "tile", -1)
+    from_after = [passed_along(value, "tile", -1) for value in behind]
 
     inside = kernel(
         own_kernel,
@@ -602,28 +642,55 @@
         edge + [scratch(2, HALO)],
         "upper",
     )(*tables, *inside, y_matrix, from_before)
+    own = (own_rows, own_powers, weights, first, later, *upper[:2], y_matrix)
+    edge = [
+        scratch(4, HALO),
+        pltpu.VMEM((4 * HALO * 8, 512), BF16),
+        pltpu.VMEM((4 * HALO * 8, wide), F32),
+        scratch(parts, ORDER),
+        scratch(4, HALO),
+        scratch(4, HALO),
+        scratch(2, HALO),
+    ]
+    others = []
+    for freq in range(freqs - 1):
+        operands = (aperture, slow, *own, from_after[freq])
+        results = (rows(2, HALO), rows(ORDER + HALO))
+        if freq == 0:
+            results = (*results, rows(ORDER))
+        else:
+            operands = (*operands, slow_after)
+        out = kernel(
+            functools.partial(lower_kernel, freq),
+            results,
+            [SMEM] + [VMEM] * (len(operands) - 1),
+            edge,
+            "lower",
+        )(*operands)
+        others += out[:2]
+        if freq == 0:
+            slow_after = out[2]
+    operands = (aperture, slow_after, *own, from_after[-1], *upper[2:], *others)
     image_parts, receiver_out = pl.pallas_call(
-        lower_kernel,
+        functools.partial(final_kernel, freqs - 1),
         out_shape=(
             shape(lax.axis_size("freq"), *slowness.shape),
             shape(*receiver_field.shape),
         ),
-        in_specs=[SMEM] + [VMEM] * (len(tables) + len(upper) + 2),
+        in_specs=[SMEM] + [VMEM] * (len(operands) - 1),
         out_specs=(VMEM, pl.BlockSpec(memory_space=pl.ANY)),
         scratch_shapes=[
             same(receiver_field),
             pltpu.SemaphoreType.DMA((2 * freqs,)),
             pltpu.VMEM((NDEPTH + 2 * freqs, stored * 8, 128), F32),
+            scratch(2 * freqs, stored),
+            scratch(NDEPTH, stored),
             *edge,
-            scratch(count, HALO),
-            scratch(count, stored),
-            scratch(NDEPTH, stored),
-            scratch(2, HALO),
         ],
         compiler_params=pltpu.CompilerParams(vmem_limit_bytes=24 << 20),
         cost_estimate=pl.CostEstimate(flops=1000, bytes_accessed=1000, transcendentals=0),
-        name="lower",
-    )(aperture, *tables, *upper, y_matrix, from_after)
+        name="final",
+    )(*operands)
     exchanged = lax.all_to_all(image_parts, "freq", 0, 0)
     return jnp.sum(exchanged, axis=0), receiver_out
 

time: 37.1 us -> 36.5 us (0.984)
  waiting for transfers between devices: 5.6 us -> 2.9 us
  starting transfers between devices: 4.95 us -> 6.24 us
  Pallas kernels: 9.84 us -> 10.6 us
    ppermute x2 -> x3, waiting for transfers between devices: 5.6 us -> 2.9 us  [passed_along(): lax.ppermute(value, axis, [(source, source + steps) for source in range(i...]
    ppermute x2 -> x3, starting transfers between devices: 4.95 us -> 6.24 us  [passed_along(): lax.ppermute(value, axis, [(source, source + steps) for source in range(i...]
    pallas_call x2 -> x3, Pallas kernels: 5.51 us -> 6.32 us  [the longest x1 2.58 us: shards(): kernel(rows_kernel, (rows(4 * HALO + ORDER), *[rows(4 * HALO)] * (freqs -...]
  transfers between devices with their start and end apart: 2 -> 3, of which waited for: 2 -> 2; matrix products, arithmetic and copies ran while one was open for 0% -> 0% of each run, Pallas kernels for 17% -> 21%
where the time goes in v12:
time: 36.5 us; the launch traced here: 36.3 us
  blocking collectives  15.1 us (41%)
  Pallas kernels  10.6 us (29%)
  starting transfers between devices  6.24 us (17%)
  waiting for transfers between devices  2.9 us (8%)
  between operations  0.8 us (2%)
  other arithmetic  0.63 us (2%)
    all_to_all x1, blocking collectives, shards(): exchanged = lax.all_to_all(image_parts, 'freq', 0, 0)  7.89 us
    all_gather x1, blocking collectives, shards(): planes = lax.all_gather(slowness, 'freq', axis=0)  7.18 us
    ppermute x3, starting transfers between devices, passed_along(): lax.ppermute(value, axis, [(source, source + steps) for source in range(i...  6.24 us
    ppermute x3, waiting for transfers between devices, passed_along(): lax.ppermute(value, axis, [(source, source + steps) for source in range(i...  2.9 us
    pallas_call x1, Pallas kernels, shards(): kernel(rows_kernel, (rows(4 * HALO + ORDER), *[rows(4 * HALO)] * (freqs -...  2.58 us
    pallas_call x1, Pallas kernels, shards(): pl.pallas_call(functools.partial(final_kernel, freqs - 1), out_shape=(sha...  2.28 us
    pallas_call x1, Pallas kernels, shards(): kernel(own_kernel, (rows(count, inner), shape(count * inner * 8, wide), r...  1.81 us
    pallas_call x1, Pallas kernels, shards(): kernel(upper_kernel, (rows(count, stored), shape(count * stored * 8, wide...  1.73 us
  transfers between devices with their start and end apart: 3, of which 2 were waited for; matrix products, arithmetic and copies ran while one was open for 0% of the time, Pallas kernels for 21%

profile of v12, /device:TPU:0, one launch (start us, length us, event | category | flops | bytes accessed | tf_op | source)
XLA Modules:
  0.0 36.3 jit_solution(10533199965426169994)
XLA Ops:
  0.6 0.0 copy-start.3
  0.6 0.0 copy-start.2
  0.7 0.0 copy-start.1
  0.7 7.2 %all-gather = f32[8,24,256]{2,1,0:T(8,128)S(1)} all-gather(f32[2,24,256]{2,1,0:T(8,128)} %param.10), channel_id=2, replica_groups=mesh['tile'=8,'freq'=4] {'freq'}, dimensions={0}, use_global_device_ids=true | all-gather | bytes 245760 | tf_op jit(solution)/shard_map/all_gather | solution.py:572
  7.9 0.1 slow.1.slow_in
  7.9 0.0 copy-done.3
  7.9 0.0 copy-done.2
  7.9 0.0 copy-done.1
  7.9 0.7 %ahead.1 = f32[68,8,128]{2,1,0:T(8,128)S(1)} custom-call(s32[8]{0:T(128)S(1)} %copy-done.3, f32[2,2,24,1024]{3,2,1,0:T(8,128)S(1)} %copy-done.1, f32[2,2,24,1024]{3,2,1,0:T(8,128)S(1)} %copy-done.2, f32[2,24,8,128]{3,2,1,0:T(8,128)S(1)} %slow.1.slow_in), custom_call_target="tpu_custom_call" | custom-call | flops 1000 | bytes 1000 | tf_op jit(solution)/shard_map/ahead/pallas_call | solution.py:583
  8.6 3.7 %collective-permute-start = (f32[68,8,128]{2,1,0:T(8,128)S(1)}, f32[68,8,128]{2,1,0:T(8,128)S(1)}, u32[]{:S(2)}, u32[]{:S(2)}) collective-permute-start(f32[68,8,128]{2,1,0:T(8,128)S(1)} %ahead.1), channel_id=1, source_target_pairs={{0,4},{4,8},{8,12},{12,16},{16,20},{20,24},{24,28},{1,5},{5,9},{9,... | collective-permute-start | bytes 835592 | tf_op jit(solution)/shard_map/ppermute | solution.py:537
  12.3 0.0 copy-done
  12.3 0.0 copy-done.4
  12.3 2.6 %rows.1 = (f32[36,8,128]{2,1,0:T(8,128)S(1)}, f32[32,8,128]{2,1,0:T(8,128)S(1)}, f32[8,24,8,128]{3,2,1,0:T(8,128)S(1)}, f32[1536,512]{1,0:T(8,128)S(1)}, f32[2,3...) custom-call(f32[2]{0:T(128)S(1)} %copy-done.6, ...), custom_call_target="tpu_custom_call" | custom-call | flops 1000 | bytes 1000 | tf_op jit(solution)/shard_map/rows/pallas_call | solution.py:591
  14.9 1.3 %collective-permute-start.1 = (f32[36,8,128]{2,1,0:T(8,128)S(1)}, f32[36,8,128]{2,1,0:T(8,128)S(1)}, u32[]{:S(2)}, u32[]{:S(2)}) collective-permute-start(f32[36,8,128]{2,1,0:T(8,128)S(1)} %get-tuple-element.35), channel_id=1, source_target_pairs={{4,0},{8,4},{12,8},{16,12},{20,16},{24,20},{28,24},{5,1},{9,5},{13... | collective-permute-start | bytes 442376 | tf_op jit(solution)/shard_map/ppermute | solution.py:537
  16.2 1.3 %collective-permute-start.2 = (f32[32,8,128]{2,1,0:T(8,128)S(1)}, f32[32,8,128]{2,1,0:T(8,128)S(1)}, u32[]{:S(2)}, u32[]{:S(2)}) collective-permute-start(f32[32,8,128]{2,1,0:T(8,128)S(1)} %get-tuple-element.37), channel_id=1, source_target_pairs={{4,0},{8,4},{12,8},{16,12},{20,16},{24,20},{28,24},{5,1},{9,5},{13... | collective-permute-start | bytes 393224 | tf_op jit(solution)/shard_map/ppermute | solution.py:537
  17.5 1.8 %own.1 = (f32[8,16,8,128]{3,2,1,0:T(8,128)S(1)}, f32[1024,512]{1,0:T(8,128)S(1)}, f32[8,8,8,128]{3,2,1,0:T(8,128)S(1)}, f32[16,8,128]{2,1,0:T(8,128)S(1)}, f32[8,8,128]{2,1,0:T(8,128)S(1)}) custom-call(f32[8,24,8,128]{3,2,1,0:T(8,128)S(1)} %get-tuple-element.23.rows_in.refs_0_, f32[1536,512]{1,0:T(8,128)S(1)} %get-tuple-element.24.powers_in.refs_1_, ...), custom_call_target="tpu_custom_call" | custom-call | flops 1000 | bytes 1000 | tf_op jit(solution)/shard_map/own/pallas_call | solution.py:612
  19.3 0.0 collective-permute-done.from_before
  19.3 1.7 %upper.1 = (f32[8,24,8,128]{3,2,1,0:T(8,128)S(1)}, f32[1536,512]{1,0:T(8,128)S(1)}, f32[8,16,8,128]{3,2,1,0:T(8,128)S(1)}, f32[2,20,8,128]{3,2,1,0:T(8,128)S(1)}) custom-call(f32[8,24,8,128]{3,2,1,0:T(8,128)S(1)} %get-tuple-element.23.rows_in.refs_0_, f32[1536,512]{1,0:T(8,128)S(1)} %get-tuple-element.24.powers_in.refs_1_, ...), custom_call_target="tpu_custom_call" | custom-call | flops 1000 | bytes 1000 | tf_op jit(solution)/shard_map/upper/pallas_call | solution.py:633
  21.1 2.4 %collective-permute-done.1.refs_8_ = f32[36,8,128]{2,1,0:T(8,128)S(1)} collective-permute-done((f32[36,8,128]{2,1,0:T(8,128)S(1)}, f32[36,8,128]{2,1,0:T(8,128)S(1)}, u32[]{:S(2)}, u32[]{:S(2)}) %collective-permute-start.1) | collective-permute-done | bytes 147488 | tf_op jit(solution)/shard_map/ppermute | solution.py:537
  23.5 1.5 %lower.1 = (f32[2,8,8,128]{3,2,1,0:T(8,128)S(1)}, f32[12,8,128]{2,1,0:T(8,128)S(1)}, f32[4,8,128]{2,1,0:T(8,128)S(1)}) custom-call(s32[8]{0:T(128)S(1)} %copy-done.3, f32[2,24,8,128]{3,2,1,0:T(8,128)S(1)} %slow.1.slow_in, f32[8,24,8,128]{3,2,1,0:T(8,128)S(1)} %get-tuple-element.23.rows_in.refs_0_, f32[1536,512]{1,0:T(8,128)S(1)} %get-tuple-element.24.powers_in.refs_1_, ...), custom_call_target="tpu_custom_call" | custom-call | flops 1000 | bytes 1000 | tf_op jit(solution)/shard_map/lower/pallas_call | solution.py:663
  25.0 0.5 %collective-permute-done.2.refs_8_ = f32[32,8,128]{2,1,0:T(8,128)S(1)} collective-permute-done((f32[32,8,128]{2,1,0:T(8,128)S(1)}, f32[32,8,128]{2,1,0:T(8,128)S(1)}, u32[]{:S(2)}, u32[]{:S(2)}) %collective-permute-start.2) | collective-permute-done | bytes 131104 | tf_op jit(solution)/shard_map/ppermute | solution.py:537
  25.4 2.3 %final.1 = (f32[4,2,24,256]{3,2,1,0:T(8,128)S(1)}, f32[2,2,24,1024]{3,2,1,0:T(8,128)}) custom-call(s32[8]{0:T(128)S(1)} %copy-done.3, f32[4,8,128]{2,1,0:T(8,128)S(1)} %get-tuple-element.36.slow, f32[8,24,8,128]{3,2,1,0:T(8,128)S(1)} %get-tuple-element.23.rows_in.refs_0_, f32[1536,512]{1,0:T(8,128)S(1)} %get-tuple-element.24.powers_in.refs_1_, ...), custom_call_target="tpu_custom_call" | custom-call | flops 1000 | bytes 1000 | tf_op jit(solution)/shard_map/final/pallas_call | solution.py:674
  27.7 7.9 %all_to_all.5 = f32[4,2,24,256]{3,2,1,0:T(8,128)S(1)} all-to-all(f32[4,2,24,256]{3,2,1,0:T(8,128)S(1)} %get-tuple-element.42), channel_id=1, replica_groups=mesh['tile'=8,'freq'=4] {'freq'}, dimensions={0} | all-to-all | bytes 393216 | tf_op jit(solution)/shard_map/all_to_all | solution.py:694
  35.6 0.6 %reduce_sum.9 = f32[2,24,256]{2,1,0:T(8,128)} reduce(f32[4,2,24,256]{3,2,1,0:T(8,128)S(1)} %all_to_all.5, f32[]{:T(128)} %constant.1.clone.1), dimensions={0}, to_apply=%region_0.0 | reduce | flops 36864 | bytes 245764 | tf_op jit(solution)/shard_map/reduce_sum | solution.py:695
  (6 shorter events, 0.0 us)
Async XLA Ops:
  0.6 7.3 %copy-start.3 = (s32[8]{0:T(128)S(1)}, s32[8]{0:T(128)}, u32[]{:S(2)}) copy-start(s32[8]{0:T(128)} %aperture.5) | copy-start | bytes 100
  0.6 7.3 %copy-start.2 = (f32[2,2,24,1024]{3,2,1,0:T(8,128)S(1)}, f32[2,2,24,1024]{3,2,1,0:T(8,128)}, u32[]{:S(2)}) copy-start(f32[2,2,24,1024]{3,2,1,0:T(8,128)} %receiver.3) | copy-start | bytes 1179652
  0.7 7.3 %copy-start.1 = (f32[2,2,24,1024]{3,2,1,0:T(8,128)S(1)}, f32[2,2,24,1024]{3,2,1,0:T(8,128)}, u32[]{:S(2)}) copy-start(f32[2,2,24,1024]{3,2,1,0:T(8,128)} %source.3) | copy-start | bytes 1179652
  7.8 4.4 %copy-start = (bf16[256,512]{1,0:T(8,128)(2,1)S(1)}, bf16[256,512]{1,0:T(8,128)(2,1)}, u32[]{:S(2)}) copy-start(bf16[256,512]{1,0:T(8,128)(2,1)} %constant.4.clone.y_matrix.refs_7_) | copy-start | bytes 786436
  7.8 4.5 %copy-start.4 = (f32[2,5,3]{1,0,2:T(2,128)S(1)}, f32[2,5,3]{1,0,2:T(2,128)}, u32[]{:S(2)}) copy-start(f32[2,5,3]{1,0,2:T(2,128)} %param.13) | copy-start | bytes 364
  7.8 4.5 %copy-start.5 = (s32[2,2]{1,0:T(2,128)S(1)}, s32[2,2]{1,0:T(2,128)}, u32[]{:S(2)}) copy-start(s32[2,2]{1,0:T(2,128)} %order_table.1) | copy-start | bytes 52
  7.8 4.5 %copy-start.6 = (f32[2]{0:T(128)S(1)}, f32[2]{0:T(128)}, u32[]{:S(2)}) copy-start(f32[2]{0:T(128)} %frequency.1) | copy-start | bytes 28
  8.6 10.7 %collective-permute-start = (f32[68,8,128]{2,1,0:T(8,128)S(1)}, f32[68,8,128]{2,1,0:T(8,128)S(1)}, u32[]{:S(2)}, u32[]{:S(2)}) collective-permute-start(f32[68,8,128]{2,1,0:T(8,128)S(1)} %ahead.1), channel_id=1, source_target_pairs={{0,4},{4,8},{8,12},{12,16},{16,20},{20,24},{24,28},{1,5},{5,9},{9,... | collective-permute-start | bytes 835592 | tf_op jit(solution)/shard_map/ppermute | solution.py:537
  14.9 8.6 %collective-permute-start.1 = (f32[36,8,128]{2,1,0:T(8,128)S(1)}, f32[36,8,128]{2,1,0:T(8,128)S(1)}, u32[]{:S(2)}, u32[]{:S(2)}) collective-permute-start(f32[36,8,128]{2,1,0:T(8,128)S(1)} %get-tuple-element.35), channel_id=1, source_target_pairs={{4,0},{8,4},{12,8},{16,12},{20,16},{24,20},{28,24},{5,1},{9,5},{13... | collective-permute-start | bytes 442376 | tf_op jit(solution)/shard_map/ppermute | solution.py:537
  16.2 9.2 %collective-permute-start.2 = (f32[32,8,128]{2,1,0:T(8,128)S(1)}, f32[32,8,128]{2,1,0:T(8,128)S(1)}, u32[]{:S(2)}, u32[]{:S(2)}) collective-permute-start(f32[32,8,128]{2,1,0:T(8,128)S(1)} %get-tuple-element.37), channel_id=1, source_target_pairs={{4,0},{8,4},{12,8},{16,12},{20,16},{24,20},{28,24},{5,1},{9,5},{13... | collective-permute-start | bytes 393224 | tf_op jit(solution)/shard_map/ppermute | solution.py:537

commit v13 on v12

--- a/solution.py
+++ b/solution.py
@@ -475,7 +475,6 @@
     image_out, receiver_hbm, receiver_out, sems, flat, rows, images, *scratch = refs
     tile = lax.axis_index("tile")
     width = aperture[tile]
-    lower_rows(freq, width, tile == lax.axis_size("tile") - 1, own, after, slow, *scratch)
     middle, last = scratch[4:6]
     count, inner = last_in.shape[:2]
     freqs = count // 4
@@ -491,14 +490,15 @@
                 store_tile(i, j, flat[slot, pl.ds((i * 8 + j) * 8, 8), :])
 
     sent = []
-    for part in range(2):
-        for at in range(freqs):
+
+    def send(at, load_last):
+        for part in range(2):
             def store_receiver(i, j, value):
                 receiver_out[part, at, pl.ds(8 * i, 8), pl.ds(128 * j, 128)] = value
 
             p = part * freqs + at
             rows[p, pl.ds(0, inner)] = last_in[2 * freqs + p]
-            rows[p, pl.ds(width - HALO, HALO)] = last[2 + part] if at == freq else others[2 * at][part]
+            rows[p, pl.ds(width - HALO, HALO)] = load_last(part)
             put(NDEPTH + p, lambda r: rows[p, r], store_receiver)
             sent.append(
                 pltpu.make_async_copy(
@@ -506,6 +506,11 @@
                 )
             )
             sent[-1].start()
+
+    for at in range(freq):
+        send(at, lambda part: others[2 * at][part])
+    lower_rows(freq, width, tile == lax.axis_size("tile") - 1, own, after, slow, *scratch)
+    send(freq, lambda part: last[2 + part])
 
     images[:, pl.ds(0, stored - ORDER)] = images_in[...]
     for k in range(ORDER + HALO):

time: 36.5 us -> 36.5 us (level)
  no operation moved by 1% of the time
where the time goes in v13:
time: 36.5 us; the launch traced here: 36.3 us
  blocking collectives  15.1 us (41%)
  Pallas kernels  10.6 us (29%)
  starting transfers between devices  6.24 us (17%)
  waiting for transfers between devices  2.9 us (8%)
  between operations  0.8 us (2%)
  other arithmetic  0.63 us (2%)
    all_to_all x1, blocking collectives, shards(): exchanged = lax.all_to_all(image_parts, 'freq', 0, 0)  7.89 us
    all_gather x1, blocking collectives, shards(): planes = lax.all_gather(slowness, 'freq', axis=0)  7.18 us
    ppermute x3, starting transfers between devices, passed_along(): lax.ppermute(value, axis, [(source, source + steps) for source in range(i...  6.24 us
    ppermute x3, waiting for transfers between devices, passed_along(): lax.ppermute(value, axis, [(source, source + steps) for source in range(i...  2.9 us
    pallas_call x1, Pallas kernels, shards(): kernel(rows_kernel, (rows(4 * HALO + ORDER), *[rows(4 * HALO)] * (freqs -...  2.58 us
    pallas_call x1, Pallas kernels, shards(): pl.pallas_call(functools.partial(final_kernel, freqs - 1), out_shape=(sha...  2.32 us
    pallas_call x1, Pallas kernels, shards(): kernel(own_kernel, (rows(count, inner), shape(count * inner * 8, wide), r...  1.81 us
    pallas_call x1, Pallas kernels, shards(): kernel(upper_kernel, (rows(count, stored), shape(count * stored * 8, wide...  1.73 us
  transfers between devices with their start and end apart: 3, of which 2 were waited for; matrix products, arithmetic and copies ran while one was open for 0% of the time, Pallas kernels for 21%

profile of v13, /device:TPU:0, one launch (start us, length us, event | category | flops | bytes accessed | tf_op | source)
XLA Modules:
  0.0 36.3 jit_solution(4585098623470458391)
XLA Ops:
  0.6 0.0 copy-start.3
  0.6 0.0 copy-start.2
  0.7 0.0 copy-start.1
  0.7 7.2 %all-gather = f32[8,24,256]{2,1,0:T(8,128)S(1)} all-gather(f32[2,24,256]{2,1,0:T(8,128)} %param.10), channel_id=2, replica_groups=mesh['tile'=8,'freq'=4] {'freq'}, dimensions={0}, use_global_device_ids=true | all-gather | bytes 245760 | tf_op jit(solution)/shard_map/all_gather | solution.py:577
  7.9 0.1 slow.1.slow_in
  7.9 0.0 copy-done.3
  7.9 0.7 %ahead.1 = f32[68,8,128]{2,1,0:T(8,128)S(1)} custom-call(s32[8]{0:T(128)S(1)} %copy-done.3, f32[2,2,24,1024]{3,2,1,0:T(8,128)S(1)} %copy-done.1, f32[2,2,24,1024]{3,2,1,0:T(8,128)S(1)} %copy-done.2, f32[2,24,8,128]{3,2,1,0:T(8,128)S(1)} %slow.1.slow_in), custom_call_target="tpu_custom_call" | custom-call | flops 1000 | bytes 1000 | tf_op jit(solution)/shard_map/ahead/pallas_call | solution.py:588
  8.6 3.7 %collective-permute-start = (f32[68,8,128]{2,1,0:T(8,128)S(1)}, f32[68,8,128]{2,1,0:T(8,128)S(1)}, u32[]{:S(2)}, u32[]{:S(2)}) collective-permute-start(f32[68,8,128]{2,1,0:T(8,128)S(1)} %ahead.1), channel_id=1, source_target_pairs={{0,4},{4,8},{8,12},{12,16},{16,20},{20,24},{24,28},{1,5},{5,9},{9,... | collective-permute-start | bytes 835592 | tf_op jit(solution)/shard_map/ppermute | solution.py:542
  12.3 0.0 copy-done
  12.3 0.0 copy-done.4
  12.3 0.0 copy-done.5
  12.3 0.0 copy-done.6
  12.3 2.6 %rows.1 = (f32[36,8,128]{2,1,0:T(8,128)S(1)}, f32[32,8,128]{2,1,0:T(8,128)S(1)}, f32[8,24,8,128]{3,2,1,0:T(8,128)S(1)}, f32[1536,512]{1,0:T(8,128)S(1)}, f32[2,3...) custom-call(f32[2]{0:T(128)S(1)} %copy-done.6, ...), custom_call_target="tpu_custom_call" | custom-call | flops 1000 | bytes 1000 | tf_op jit(solution)/shard_map/rows/pallas_call | solution.py:596
  14.9 1.3 %collective-permute-start.1 = (f32[36,8,128]{2,1,0:T(8,128)S(1)}, f32[36,8,128]{2,1,0:T(8,128)S(1)}, u32[]{:S(2)}, u32[]{:S(2)}) collective-permute-start(f32[36,8,128]{2,1,0:T(8,128)S(1)} %get-tuple-element.35), channel_id=1, source_target_pairs={{4,0},{8,4},{12,8},{16,12},{20,16},{24,20},{28,24},{5,1},{9,5},{13... | collective-permute-start | bytes 442376 | tf_op jit(solution)/shard_map/ppermute | solution.py:542
  16.2 1.3 %collective-permute-start.2 = (f32[32,8,128]{2,1,0:T(8,128)S(1)}, f32[32,8,128]{2,1,0:T(8,128)S(1)}, u32[]{:S(2)}, u32[]{:S(2)}) collective-permute-start(f32[32,8,128]{2,1,0:T(8,128)S(1)} %get-tuple-element.37), channel_id=1, source_target_pairs={{4,0},{8,4},{12,8},{16,12},{20,16},{24,20},{28,24},{5,1},{9,5},{13... | collective-permute-start | bytes 393224 | tf_op jit(solution)/shard_map/ppermute | solution.py:542
  17.5 1.8 %own.1 = (f32[8,16,8,128]{3,2,1,0:T(8,128)S(1)}, f32[1024,512]{1,0:T(8,128)S(1)}, f32[8,8,8,128]{3,2,1,0:T(8,128)S(1)}, f32[16,8,128]{2,1,0:T(8,128)S(1)}, f32[8,8,128]{2,1,0:T(8,128)S(1)}) custom-call(f32[8,24,8,128]{3,2,1,0:T(8,128)S(1)} %get-tuple-element.23.rows_in.refs_0_, f32[1536,512]{1,0:T(8,128)S(1)} %get-tuple-element.24.powers_in.refs_1_, ...), custom_call_target="tpu_custom_call" | custom-call | flops 1000 | bytes 1000 | tf_op jit(solution)/shard_map/own/pallas_call | solution.py:617
  19.3 0.0 collective-permute-done.from_before
  19.3 1.7 %upper.1 = (f32[8,24,8,128]{3,2,1,0:T(8,128)S(1)}, f32[1536,512]{1,0:T(8,128)S(1)}, f32[8,16,8,128]{3,2,1,0:T(8,128)S(1)}, f32[2,20,8,128]{3,2,1,0:T(8,128)S(1)}) custom-call(f32[8,24,8,128]{3,2,1,0:T(8,128)S(1)} %get-tuple-element.23.rows_in.refs_0_, f32[1536,512]{1,0:T(8,128)S(1)} %get-tuple-element.24.powers_in.refs_1_, ...), custom_call_target="tpu_custom_call" | custom-call | flops 1000 | bytes 1000 | tf_op jit(solution)/shard_map/upper/pallas_call | solution.py:638
  21.1 2.4 %collective-permute-done.1.refs_8_ = f32[36,8,128]{2,1,0:T(8,128)S(1)} collective-permute-done((f32[36,8,128]{2,1,0:T(8,128)S(1)}, f32[36,8,128]{2,1,0:T(8,128)S(1)}, u32[]{:S(2)}, u32[]{:S(2)}) %collective-permute-start.1) | collective-permute-done | bytes 147488 | tf_op jit(solution)/shard_map/ppermute | solution.py:542
  23.5 1.5 %lower.1 = (f32[2,8,8,128]{3,2,1,0:T(8,128)S(1)}, f32[12,8,128]{2,1,0:T(8,128)S(1)}, f32[4,8,128]{2,1,0:T(8,128)S(1)}) custom-call(s32[8]{0:T(128)S(1)} %copy-done.3, f32[2,24,8,128]{3,2,1,0:T(8,128)S(1)} %slow.1.slow_in, f32[8,24,8,128]{3,2,1,0:T(8,128)S(1)} %get-tuple-element.23.rows_in.refs_0_, f32[1536,512]{1,0:T(8,128)S(1)} %get-tuple-element.24.powers_in.refs_1_, ...), custom_call_target="tpu_custom_call" | custom-call | flops 1000 | bytes 1000 | tf_op jit(solution)/shard_map/lower/pallas_call | solution.py:668
  25.0 0.5 %collective-permute-done.2.refs_8_ = f32[32,8,128]{2,1,0:T(8,128)S(1)} collective-permute-done((f32[32,8,128]{2,1,0:T(8,128)S(1)}, f32[32,8,128]{2,1,0:T(8,128)S(1)}, u32[]{:S(2)}, u32[]{:S(2)}) %collective-permute-start.2) | collective-permute-done | bytes 131104 | tf_op jit(solution)/shard_map/ppermute | solution.py:542
  25.4 2.3 %final.1 = (f32[4,2,24,256]{3,2,1,0:T(8,128)S(1)}, f32[2,2,24,1024]{3,2,1,0:T(8,128)}) custom-call(s32[8]{0:T(128)S(1)} %copy-done.3, f32[4,8,128]{2,1,0:T(8,128)S(1)} %get-tuple-element.36.slow, f32[8,24,8,128]{3,2,1,0:T(8,128)S(1)} %get-tuple-element.23.rows_in.refs_0_, f32[1536,512]{1,0:T(8,128)S(1)} %get-tuple-element.24.powers_in.refs_1_, ...), custom_call_target="tpu_custom_call" | custom-call | flops 1000 | bytes 1000 | tf_op jit(solution)/shard_map/final/pallas_call | solution.py:679
  27.8 7.9 %all_to_all.5 = f32[4,2,24,256]{3,2,1,0:T(8,128)S(1)} all-to-all(f32[4,2,24,256]{3,2,1,0:T(8,128)S(1)} %get-tuple-element.42), channel_id=1, replica_groups=mesh['tile'=8,'freq'=4] {'freq'}, dimensions={0} | all-to-all | bytes 393216 | tf_op jit(solution)/shard_map/all_to_all | solution.py:699
  35.7 0.6 %reduce_sum.9 = f32[2,24,256]{2,1,0:T(8,128)} reduce(f32[4,2,24,256]{3,2,1,0:T(8,128)S(1)} %all_to_all.5, f32[]{:T(128)} %constant.1.clone.1), dimensions={0}, to_apply=%region_0.0 | reduce | flops 36864 | bytes 245764 | tf_op jit(solution)/shard_map/reduce_sum | solution.py:700
  (6 shorter events, 0.0 us)
Async XLA Ops:
  0.6 7.3 %copy-start.3 = (s32[8]{0:T(128)S(1)}, s32[8]{0:T(128)}, u32[]{:S(2)}) copy-start(s32[8]{0:T(128)} %aperture.5) | copy-start | bytes 100
  0.6 7.3 %copy-start.2 = (f32[2,2,24,1024]{3,2,1,0:T(8,128)S(1)}, f32[2,2,24,1024]{3,2,1,0:T(8,128)}, u32[]{:S(2)}) copy-start(f32[2,2,24,1024]{3,2,1,0:T(8,128)} %receiver.3) | copy-start | bytes 1179652
  0.7 7.3 %copy-start.1 = (f32[2,2,24,1024]{3,2,1,0:T(8,128)S(1)}, f32[2,2,24,1024]{3,2,1,0:T(8,128)}, u32[]{:S(2)}) copy-start(f32[2,2,24,1024]{3,2,1,0:T(8,128)} %source.3) | copy-start | bytes 1179652
  7.8 4.4 %copy-start = (bf16[256,512]{1,0:T(8,128)(2,1)S(1)}, bf16[256,512]{1,0:T(8,128)(2,1)}, u32[]{:S(2)}) copy-start(bf16[256,512]{1,0:T(8,128)(2,1)} %constant.4.clone.y_matrix.refs_7_) | copy-start | bytes 786436
  7.8 4.5 %copy-start.4 = (f32[2,5,3]{1,0,2:T(2,128)S(1)}, f32[2,5,3]{1,0,2:T(2,128)}, u32[]{:S(2)}) copy-start(f32[2,5,3]{1,0,2:T(2,128)} %param.13) | copy-start | bytes 364
  7.8 4.5 %copy-start.5 = (s32[2,2]{1,0:T(2,128)S(1)}, s32[2,2]{1,0:T(2,128)}, u32[]{:S(2)}) copy-start(s32[2,2]{1,0:T(2,128)} %order_table.1) | copy-start | bytes 52
  7.8 4.5 %copy-start.6 = (f32[2]{0:T(128)S(1)}, f32[2]{0:T(128)}, u32[]{:S(2)}) copy-start(f32[2]{0:T(128)} %frequency.1) | copy-start | bytes 28
  8.6 10.7 %collective-permute-start = (f32[68,8,128]{2,1,0:T(8,128)S(1)}, f32[68,8,128]{2,1,0:T(8,128)S(1)}, u32[]{:S(2)}, u32[]{:S(2)}) collective-permute-start(f32[68,8,128]{2,1,0:T(8,128)S(1)} %ahead.1), channel_id=1, source_target_pairs={{0,4},{4,8},{8,12},{12,16},{16,20},{20,24},{24,28},{1,5},{5,9},{9,... | collective-permute-start | bytes 835592 | tf_op jit(solution)/shard_map/ppermute | solution.py:542
  14.9 8.6 %collective-permute-start.1 = (f32[36,8,128]{2,1,0:T(8,128)S(1)}, f32[36,8,128]{2,1,0:T(8,128)S(1)}, u32[]{:S(2)}, u32[]{:S(2)}) collective-permute-start(f32[36,8,128]{2,1,0:T(8,128)S(1)} %get-tuple-element.35), channel_id=1, source_target_pairs={{4,0},{8,4},{12,8},{16,12},{20,16},{24,20},{28,24},{5,1},{9,5},{13... | collective-permute-start | bytes 442376 | tf_op jit(solution)/shard_map/ppermute | solution.py:542
  16.2 9.2 %collective-permute-start.2 = (f32[32,8,128]{2,1,0:T(8,128)S(1)}, f32[32,8,128]{2,1,0:T(8,128)S(1)}, u32[]{:S(2)}, u32[]{:S(2)}) collective-permute-start(f32[32,8,128]{2,1,0:T(8,128)S(1)} %get-tuple-element.37), channel_id=1, source_target_pairs={{4,0},{8,4},{12,8},{16,12},{20,16},{24,20},{28,24},{5,1},{9,5},{13... | collective-permute-start | bytes 393224 | tf_op jit(solution)/shard_map/ppermute | solution.py:542
